TPU v7x, 32 devices: a whole 2x2x4 slice. The times are simulated.
32 devices in a mesh: row: 16 (over z, x, core), seq: 2 (over y).
Axes of the slice: x: 2, y: 2, z: 4, core: 2. Of those that a mesh axis runs over, the one named last changes fastest.
Arguments:
- tokens: bfloat16 [32, 2048, 768], P('row', 'seq'), may hold values from -6 to 6
- segments: int32 [32, 2048], P('row'), may hold values from 0 to 3, as said below
- w_qkv: float32 [768, 2304], P(('row', 'seq')), may hold values from -0.21875 to 0.21875
- w_out: float32 [768, 768], P(('row', 'seq')), may hold values from -3.5 to 3.5
- w_up: float32 [768, 3072], P(('row', 'seq')), may hold values from -0.21875 to 0.21875
- w_down: float32 [3072, 768], P(('row', 'seq')), may hold values from -0.109375 to 0.109375
- gain_attn: float32 [768], P(('row', 'seq')), may hold values from 0.25 to 1.75
- gain_mlp: float32 [768], P(('row', 'seq')), may hold values from 0.25 to 1.75
- cotangent: bfloat16 [32, 2048, 768], P('row', 'seq'), may hold values from -6 to 6
Outputs:
- output: bfloat16 [32, 2048, 768], P('row', 'seq')
- d_tokens: float32 [32, 2048, 768], P('row', 'seq')
- grad_qkv: float32 [768, 2304], P(('row', 'seq'))
- grad_out: float32 [768, 768], P(('row', 'seq'))
- grad_up: float32 [768, 3072], P(('row', 'seq'))
- grad_down: float32 [3072, 768], P(('row', 'seq'))
- grad_gain_attn: float32 [768], P(('row', 'seq'))
- grad_gain_mlp: float32 [768], P(('row', 'seq'))
Inputs may be any that keep to these rules, and one draw needn't show every extreme that they name: `segments`: segment ids never fall along a row. Among the 2 rows at each index of row, at least one is a single segment.
All inputs are finite; a program needn't handle non-finite values.
Results may differ from a plain program's by a relative error of at most 0.017.
Values may be sent and summed in bfloat16 or wider, within the bound.
No kernel may reach another device: no remote copies, remote signals or barrier semaphores. Data moves between devices by JAX's collectives and lax.ppermute only.
A program may use at most 1 GiB of HBM per device.

v0:
```python
from functools import partial
import math

import jax
import jax.numpy as jnp
from jax import lax
from jax.sharding import PartitionSpec as P

H = 12
HD = 64
ROW_LEN = 2048


EPSILON = 1e-05
MASKED = -1e30


def from_behind(value, axis, steps):
    count = lax.axis_size(axis)
    first, last = (max(0, -steps), min(count, count - steps))
    return lax.ppermute(value, axis, [(source, source + steps) for source in range(first, last)])


def layer_norm(values, scaling):
    mean_value = jnp.mean(values, axis=-1, keepdims=True)
    shifted = values - mean_value
    spread = jnp.mean(shifted * shifted, axis=-1, keepdims=True)
    return shifted * lax.rsqrt(spread + EPSILON) * scaling


def block_masks(segments, position, source, block_len):
    offsets = jnp.arange(block_len, dtype=jnp.int32)
    query_pos = position * block_len + offsets
    key_pos = source * block_len + offsets
    query_start = position * block_len
    key_start = jnp.maximum(source, 0) * block_len
    query_seg = lax.dynamic_slice_in_dim(segments, query_start, block_len, 1)
    key_seg = lax.dynamic_slice_in_dim(segments, key_start, block_len, 1)
    same_doc = (query_seg[:, :, None] == key_seg[:, None, :]) & (source >= 0)
    earlier = key_pos[None, :] < query_pos[:, None]
    reached = key_pos[None, :] <= query_pos[:, None]
    return (same_doc & reached[None], same_doc & earlier[None])


def block_logits(queries, key_heads, carried, segments, position, source, offset):
    block_len = queries.shape[1]
    scores = jnp.einsum(
        "rqhd,rkhd->rhqk", queries, key_heads, preferred_element_type=jnp.float32
    ) * (1.0 / math.sqrt(HD))
    attend_mask, select_mask = block_masks(segments, position, source, block_len)
    chosen = jnp.where(select_mask, jax.nn.softplus(scores[:, 0] - offset), 0.0)
    running = jnp.cumsum(chosen, axis=1)
    penalty = carried[:, None, :] + running - chosen
    logits = jnp.where(attend_mask[:, None], scores - penalty[:, None], MASKED)
    return (scores, logits, attend_mask, select_mask, carried + running[:, -1])


def body(tokens, segments, w_qkv, w_out, w_up, w_down, gain_attn, gain_mlp, cotangent):
    low_pieces = (
        w_qkv.astype(jnp.bfloat16),
        w_out.astype(jnp.bfloat16),
        w_up.astype(jnp.bfloat16),
        w_down.astype(jnp.bfloat16),
        gain_attn.astype(jnp.bfloat16),
        gain_mlp.astype(jnp.bfloat16),
    )
    gathered = (
        lax.all_gather(low_pieces[0], ("row", "seq"), axis=0, tiled=True),
        lax.all_gather(low_pieces[1], ("row", "seq"), axis=0, tiled=True),
        lax.all_gather(low_pieces[2], ("row", "seq"), axis=0, tiled=True),
        lax.all_gather(low_pieces[3], ("row", "seq"), axis=0, tiled=True),
        lax.all_gather(low_pieces[4], ("row", "seq"), axis=0, tiled=True),
        lax.all_gather(low_pieces[5], ("row", "seq"), axis=0, tiled=True),
    )
    qkv_full, out_full, up_full, down_full, attn_scale, mlp_scale = gathered
    row_count, block_len, features = tokens.shape
    token_count = row_count * block_len
    position = lax.axis_index("seq")
    sections = lax.axis_size("seq")
    offset = math.log(ROW_LEN / 2.0) + 0.5
    inputs = tokens.astype(jnp.float32).reshape(token_count, features)
    normed, attn_norm_back = jax.vjp(layer_norm, inputs, attn_scale.astype(jnp.float32))
    normed_low = normed.astype(jnp.bfloat16)
    packed = jnp.dot(normed_low, qkv_full, preferred_element_type=jnp.float32).astype(jnp.bfloat16)
    packed = packed.reshape(row_count, block_len, 3 * features)
    queries = packed[:, :, :features].reshape(row_count, block_len, H, HD)
    key_value = packed[:, :, features:]
    carried = jnp.zeros((row_count, block_len), jnp.float32)
    running_max = jnp.full((row_count, H, block_len), MASKED, jnp.float32)
    running_sum = jnp.zeros((row_count, H, block_len), jnp.float32)
    accumulated = jnp.zeros((row_count, block_len, H, HD), jnp.float32)
    kept_pairs = []
    kept_sums = []
    for section in range(sections):
        source = position - section
        key_heads = key_value[:, :, :features].reshape(row_count, block_len, H, HD)
        value_heads = key_value[:, :, features:].reshape(row_count, block_len, H, HD)
        scores, logits, attend_mask, select_mask, passed = block_logits(
            queries, key_heads, carried, segments, position, source, offset
        )
        kept_pairs.append(key_value)
        kept_sums.append(carried)
        new_max = jnp.maximum(running_max, jnp.max(logits, axis=-1))
        rescale = jnp.exp(running_max - new_max)
        exp_scores = jnp.where(attend_mask[:, None], jnp.exp(logits - new_max[..., None]), 0.0)
        running_sum = running_sum * rescale + jnp.sum(exp_scores, axis=-1)
        accumulated = accumulated * jnp.transpose(rescale, (0, 2, 1))[..., None] + jnp.einsum(
            "rhqk,rkhd->rqhd",
            exp_scores.astype(jnp.bfloat16),
            value_heads,
            preferred_element_type=jnp.float32,
        )
        running_max = new_max
        if section + 1 < sections:
            key_value = from_behind(key_value, "seq", 1)
            carried = from_behind(passed, "seq", 1)
    log_norm = running_max + jnp.log(running_sum)
    attn_heads = accumulated / jnp.transpose(running_sum, (0, 2, 1))[..., None]
    mixed_low = attn_heads.reshape(token_count, features).astype(jnp.bfloat16)
    branch = jnp.dot(mixed_low, out_full, preferred_element_type=jnp.float32)
    middle = inputs + branch
    normed_mlp, mlp_norm_back = jax.vjp(layer_norm, middle, mlp_scale.astype(jnp.float32))
    normed_mlp_low = normed_mlp.astype(jnp.bfloat16)
    hidden = jnp.dot(normed_mlp_low, up_full, preferred_element_type=jnp.float32)
    active, gelu_back = jax.vjp(partial(jax.nn.gelu, approximate=False), hidden)
    active_low = active.astype(jnp.bfloat16)
    output = (middle + jnp.dot(active_low, down_full, preferred_element_type=jnp.float32)).astype(
        jnp.bfloat16
    )
    output = output.reshape(row_count, block_len, features)
    upstream = cotangent.reshape(token_count, features)
    grad_down = jnp.dot(active_low.T, upstream, preferred_element_type=jnp.float32)
    d_active = jnp.dot(upstream, down_full.T, preferred_element_type=jnp.float32)
    d_hidden = gelu_back(d_active)[0].astype(jnp.bfloat16)
    grad_up = jnp.dot(normed_mlp_low.T, d_hidden, preferred_element_type=jnp.float32)
    d_normed_mlp = jnp.dot(d_hidden, up_full.T, preferred_element_type=jnp.float32)
    d_middle_part, grad_mlp_gain = mlp_norm_back(d_normed_mlp)
    d_middle = upstream.astype(jnp.float32) + d_middle_part
    d_branch = d_middle.astype(jnp.bfloat16)
    grad_out = jnp.dot(mixed_low.T, d_branch, preferred_element_type=jnp.float32)
    d_mixed = jnp.dot(d_branch, out_full.T, preferred_element_type=jnp.float32).astype(jnp.bfloat16)
    d_mixed = d_mixed.reshape(row_count, block_len, H, HD)
    correction = jnp.transpose(
        jnp.sum(d_mixed.astype(jnp.float32) * attn_heads, axis=-1), (0, 2, 1)
    )
    score_scale = 1.0 / math.sqrt(HD)
    grads_pair = jnp.zeros((row_count, block_len, 2 * features), jnp.float32)
    grads_column = jnp.zeros((row_count, block_len), jnp.float32)
    grad_query = jnp.zeros((row_count, block_len, H, HD), jnp.float32)
    for section in reversed(range(sections)):
        source = position - section
        key_value = kept_pairs[section]
        key_heads = key_value[:, :, :features].reshape(row_count, block_len, H, HD)
        value_heads = key_value[:, :, features:].reshape(row_count, block_len, H, HD)
        scores, logits, attend_mask, select_mask, unused = block_logits(
            queries, key_heads, kept_sums[section], segments, position, source, offset
        )
        attention = jnp.where(attend_mask[:, None], jnp.exp(logits - log_norm[..., None]), 0.0)
        attention_low = attention.astype(jnp.bfloat16)
        grad_values = jnp.einsum(
            "rhqk,rqhd->rkhd", attention_low, d_mixed, preferred_element_type=jnp.float32
        )
        grad_attention = jnp.einsum(
            "rqhd,rkhd->rhqk", d_mixed, value_heads, preferred_element_type=jnp.float32
        )
        grad_logits = attention * (grad_attention - correction[..., None])
        summed = jnp.sum(grad_logits, axis=1)
        column = jnp.sum(summed, axis=1)
        running = jnp.cumsum(summed, axis=1)
        grad_chosen = jnp.where(
            select_mask, running - column[:, None, :] - grads_column[:, None, :], 0.0
        )
        grad_scores = grad_logits.at[:, 0].add(grad_chosen * jax.nn.sigmoid(scores[:, 0] - offset))
        grad_scores = grad_scores.astype(jnp.bfloat16)
        grad_query = (
            grad_query
            + jnp.einsum(
                "rhqk,rkhd->rqhd", grad_scores, key_heads, preferred_element_type=jnp.float32
            )
            * score_scale
        )
        grad_keys = (
            jnp.einsum("rhqk,rqhd->rkhd", grad_scores, queries, preferred_element_type=jnp.float32)
            * score_scale
        )
        grads_pair = grads_pair + jnp.concatenate(
            [
                grad_keys.reshape(row_count, block_len, features),
                grad_values.reshape(row_count, block_len, features),
            ],
            axis=-1,
        )
        grads_column = grads_column + column
        if section > 0:
            grads_pair, grads_column = (
                from_behind(grads_pair.astype(jnp.bfloat16), "seq", -1).astype(grads_pair.dtype),
                from_behind(grads_column.astype(jnp.bfloat16), "seq", -1).astype(
                    grads_column.dtype
                ),
            )
    d_packed = jnp.concatenate(
        [grad_query.reshape(token_count, features), grads_pair.reshape(token_count, 2 * features)],
        axis=-1,
    )
    d_packed = d_packed.astype(jnp.bfloat16)
    grad_qkv = jnp.dot(normed_low.T, d_packed, preferred_element_type=jnp.float32)
    d_normed = jnp.dot(d_packed, qkv_full.T, preferred_element_type=jnp.float32)
    d_inputs_part, grad_attn_gain = attn_norm_back(d_normed)
    d_tokens = (d_middle + d_inputs_part).reshape(row_count, block_len, features)
    gradients = (grad_qkv, grad_out, grad_up, grad_down, grad_attn_gain, grad_mlp_gain)
    reduced = (
        lax.psum_scatter(gradients[0], ("row", "seq"), scatter_dimension=0, tiled=True),
        lax.psum_scatter(gradients[1], ("row", "seq"), scatter_dimension=0, tiled=True),
        lax.psum_scatter(gradients[2], ("row", "seq"), scatter_dimension=0, tiled=True),
        lax.psum_scatter(gradients[3], ("row", "seq"), scatter_dimension=0, tiled=True),
        lax.psum_scatter(gradients[4], ("row", "seq"), scatter_dimension=0, tiled=True),
        lax.psum_scatter(gradients[5], ("row", "seq"), scatter_dimension=0, tiled=True),
    )
    return (
        output,
        d_tokens,
        reduced[0],
        reduced[1],
        reduced[2],
        reduced[3],
        reduced[4],
        reduced[5],
    )


def solution(mesh):
    placed = (
        P("row", "seq", None),
        P("row", None),
        P(("row", "seq"), None),
        P(("row", "seq"), None),
        P(("row", "seq"), None),
        P(("row", "seq"), None),
        P(("row", "seq")),
        P(("row", "seq")),
        P("row", "seq", None),
    )
    return jax.shard_map(
        body,
        mesh=mesh,
        in_specs=placed,
        out_specs=(
            P("row", "seq", None),
            P("row", "seq", None),
            P(("row", "seq"), None),
            P(("row", "seq"), None),
            P(("row", "seq"), None),
            P(("row", "seq"), None),
            P(("row", "seq")),
            P(("row", "seq")),
        ),
        check_vma=False,
    )
```

profile of v0, /device:TPU:0, one launch (start us, length us, event | category | flops | bytes accessed | tf_op | source)
XLA Modules:
  0.0 1605.5 jit_solution(10557759111727603566)
XLA Ops:
  15.8 42.2 %all-reduce.5 = (bf16[768]{0:T(1024)(128)(2,1)S(1)}, bf16[768]{0:T(1024)(128)(2,1)S(1)}) all-reduce(bf16[768]{0:T(1024)(128)(2,1)S(1)} %dynamic-update-slice.6, bf16[768]{0:T(1024)(128)(2,1)S(1)} %dynamic-update-slice.7), channel_id=1, replica_groups=mesh['row'=16,'seq'=2] {'row','seq'}, use_global_device_ids=true, to_apply=%add | all-reduce | flops 1536 | bytes 6144
  116.8 37.8 %broadcast_multiply_fusion = f32[2,12,1024,1024]{3,2,1,0:T(8,128)} fusion(bf16[2,1024,12,64]{1,3,2,0:T(8,128)(2,1)S(1)} %bitcast.229, bf16[2,1024,12,64]{1,3,2,0:T(8,128)(2,1)} %bitcast.240), kind=kOutput, calls=%fused_computation.17 | convolution fusion | flops 3246391296 | bytes 106954752 | tf_op jit(solution)/shard_map/rqhd,rkhd->rhqk/dot_general | solution.py:47
  154.6 89.5 %collective-permute-done = bf16[2,1024,1536]{2,1,0:T(8,128)(2,1)} collective-permute-done((bf16[2,1024,1536]{2,1,0:T(8,128)(2,1)}, bf16[2,1024,1536]{2,1,0:T(8,128)(2,1)}, u32[]{:S(2)}, u32[]{:S(2)}) %collective-permute-start) | collective-permute-done | bytes 6291488 | tf_op jit(solution)/shard_map/ppermute | solution.py:21
  254.8 37.4 %broadcast_multiply_fusion.1 = f32[2,12,1024,1024]{3,2,0,1:T(8,128)} fusion(bf16[2,1024,12,64]{1,3,2,0:T(8,128)(2,1)} %bitcast.238, bf16[2,1024,12,64]{1,3,2,0:T(8,128)(2,1)S(1)} %bitcast.230), kind=kOutput, calls=%fused_computation.25 | convolution fusion | flops 3246391296 | bytes 106954752 | tf_op jit(solution)/shard_map/rqhd,rkhd->rhqk/dot_general | solution.py:47
  292.2 19.7 %fusion.34 = (f32[2,1024,1024]{2,1,0:T(8,128)}, f32[2,1024,1024]{2,1,0:T(8,128)}) fusion(f32[2,12,1024,1024]{3,2,0,1:T(8,128)} %broadcast_multiply_fusion.1, s32[2,1024]{1,0:T(2,128)S(1)} %get-tuple-element.65, s32[2,1024]{1,0:T(2,128)S(1)} %get-tuple-element.66, pred[1024,1024]{1,0:T(8,128)(4,1)} %get-tuple-element.71, pred[]{:T(512)S(6)} %ge.9, ...), kind=kLoop, calls=%fused_computation.62 | loop fusion | flops 46137344 | bytes 35676160 | tf_op jit(solution)/shard_map/jit(_where)/select_n | solution.py:51
  366.6 74.7 %fusion.116 = (f32[2,12,1024]{2,1,0:T(8,128)S(1)}, f32[2,12,1024,1024]{3,2,1,0:T(8,128)}) fusion(f32[2,12,1024,1024]{3,2,1,0:T(8,128)} %broadcast_multiply_fusion, f32[2,1024,1024]{2,1,0:T(8,128)} %bitcast_subtract_fusion.5, pred[2,1024,1024]{2,1,0:T(8,128)(4,1)} %get-tuple-element.69), kind=kLoop, calls=%fused_computation.200 | loop fusion | flops 75472896 | bytes 211910656 | tf_op jit(solution)/shard_map/reduce_max | solution.py:103
  475.3 38.5 %fusion.8 = f32[2,12,1024]{2,0,1:T(2,128)S(1)} fusion(f32[2,12,1024,1024]{3,2,0,1:T(8,128)} %broadcast_multiply_fusion.1, f32[2,1024,1024]{2,1,0:T(8,128)} %bitcast_subtract_fusion.2, pred[2,1024,1024]{2,1,0:T(8,128)(4,1)S(1)} %copy-done), kind=kLoop, calls=%fused_computation.16 | loop fusion | flops 75472896 | bytes 111247360 | tf_op jit(solution)/shard_map/reduce_max | solution.py:103
  514.1 57.5 %fusion.3 = (bf16[2,12,1024,1024]{3,2,0,1:T(8,128)(2,1)}, f32[2,12,1024]{2,0,1:T(2,128)}) fusion(f32[2,12,1024,1024]{3,2,0,1:T(8,128)} %broadcast_multiply_fusion.1, f32[2,12,1024]{2,0,1:T(2,128)S(1)} %copy.160, f32[2,1024,1024]{2,1,0:T(8,128)} %bitcast_subtract_fusion.2, pred[2,1024,1024]{2,1,0:T(8,128)(4,1)S(1)} %copy-done), kind=kLoop, calls=%fused_computation.11 | loop fusion | flops 150970368 | bytes 161677312 | tf_op jit(solution)/shard_map/convert_element_type | solution.py:109
  571.6 49.2 %fusion.6 = (f32[2,12,1024]{2,0,1:T(2,128)S(1)}, bf16[2,12,1024,1024]{3,2,0,1:T(8,128)(2,1)}) fusion(f32[2,12,1024,1024]{3,2,1,0:T(8,128)} %get-tuple-element.50, f32[2,12,1024]{2,0,1:T(2,128)S(1)} %copy.150, pred[2,1024,1024]{2,1,0:T(8,128)(4,1)S(1)} %copy-done.12), kind=kLoop, calls=%fused_computation.14 | loop fusion | flops 100638720 | bytes 153288704 | tf_op jit(solution)/shard_map/reduce_sum | solution.py:106
  620.8 24.3 %fusion.13 = f32[2,12,64,1024]{3,2,1,0:T(8,128)} fusion(bf16[2,1024,12,64]{1,3,2,0:T(8,128)(2,1)} %bitcast.248, bf16[2,12,1024,1024]{3,2,0,1:T(8,128)(2,1)} %get-tuple-element.54), kind=kOutput, calls=%fused_computation.22 | convolution fusion | flops 3221225472 | bytes 59768832 | tf_op jit(solution)/shard_map/rhqk,rkhd->rqhd/dot_general | solution.py:107
  646.8 25.6 %fusion.119 = (bf16[2,1024,12,64]{1,3,2,0:T(8,128)(2,1)}, f32[2,1024,12,64]{1,3,2,0:T(8,128)}) fusion(f32[2,1024,12]{1,2,0:T(8,128)} %get-tuple-element.61, bf16[2,1024,12,64]{1,3,2,0:T(8,128)(2,1)S(1)} %bitcast.247, bf16[2,12,1024,1024]{3,2,0,1:T(8,128)(2,1)} %get-tuple-element.51, f32[2,1024,12]{1,2,0:T(8,128)} %get-tuple-element.60, ...), kind=kOutput, calls=%fused_computation.203 | convolution fusion | flops 3229089792 | bytes 69500928 | tf_op jit(solution)/shard_map/rhqk,rkhd->rqhd/dot_general | solution.py:107
  690.0 69.5 %multiply_convert_fusion = (bf16[2048,3072]{1,0:T(8,128)(2,1)S(1)}, f32[2048,3072]{1,0:T(8,128)}, f32[2048,3072]{1,0:T(8,128)}) fusion(bf16[768,3072]{1,0:T(8,128)(2,1)} %all-gather.9.cloned.1.call-done, f32[2048,768]{1,0:T(8,128)} %copy-done.15, f32[768]{0:T(1024)S(1)} %copy-done.61, f32[2048]{0:T(1024)S(1)} %fusion.104, f32[2048]{0:T(1024)S(1)} %broadcast_multiply_fusion.3), kind=kOutput, calls=%fused_computation.39 | convolution fusion | flops 10078912512 | bytes 73944064 | tf_op jit(solution)/shard_map/dot_general | solution.py:124
  777.4 26.6 %add_convert_fusion = bf16[2048,3072]{1,0:T(8,128)(2,1)} fusion(f32[2048,3072]{1,0:T(8,128)} %get-tuple-element.48, f32[2048,3072]{1,0:T(8,128)} %get-tuple-element.82, bf16[2048,768]{1,0:T(8,128)(2,1)S(1)} %bitcast.251, bf16[3072,768]{1,0:T(8,128)(2,1)} %all-gather.11.cloned.1.call-done), kind=kOutput, calls=%fused_computation.38 | convolution fusion | flops 9751756800 | bytes 70778880 | tf_op jit(solution)/shard_map/dot_general | solution.py:133
  851.7 37.2 %fusion.15 = f32[2,12,64,1024]{3,2,1,0:T(8,128)} fusion(f32[2,12,1024,1024]{3,2,1,0:T(8,128)} %get-tuple-element.50, f32[2,12,1024]{2,1,0:T(8,128)S(1)} %fusion.97, pred[2,1024,1024]{2,1,0:T(8,128)(4,1)} %get-tuple-element.69, bf16[2,1024,12,64]{1,0,3,2:T(2,128)(2,1)S(1)} %reshape.446), kind=kOutput, calls=%fused_computation.26 | convolution fusion | flops 3296722944 | bytes 112295936 | tf_op jit(solution)/shard_map/rhqk,rqhd->rkhd/dot_general | solution.py:160
  894.7 41.8 %fusion.87 = bf16[2,12,64,1024]{3,2,1,0:T(8,128)(2,1)} fusion(bf16[2,1024,12,64]{1,0,3,2:T(2,128)(2,1)} %copy-done.9, f32[2,12,1024,1024]{3,2,0,1:T(8,128)} %broadcast_multiply_fusion.1, f32[2,12,1024]{2,0,1:T(2,128)S(1)} %copy.167, f32[2,1024,1024]{2,1,0:T(8,128)} %bitcast_subtract_fusion.2, pred[2,1024,1024]{2,1,0:T(8,128)(4,1)S(1)} %copy-done.1), kind=kOutput, calls=%fused_computation.142 | convolution fusion | flops 3348627456 | bytes 117538816 | tf_op jit(solution)/shard_map/rhqk,rqhd->rkhd/dot_general | solution.py:160
  947.7 90.2 %fusion.112 = (f32[2,1024,1024]{2,1,0:T(8,128)}, f32[2,1024]{1,0:T(2,128)S(1)}, f32[2,12,1024,1024]{3,2,0,1:T(8,128)}) fusion(f32[2,12,1024]{2,0,1:T(2,128)S(1)} %copy.171, bf16[2,1024,12,64]{1,3,2,0:T(8,128)(2,1)} %bitcast.246, bf16[2,1024,12,64]{1,0,3,2:T(2,128)(2,1)} %copy-done.9, f32[2,12,1024]{2,0,1:T(2,128)S(1)} %copy.167, ...), kind=kOutput, calls=%fused_computation.197 | convolution fusion | flops 3420452864 | bytes 226697216 | tf_op jit(solution)/shard_map/rqhd,rkhd->rhqk/dot_general | solution.py:163
  1073.7 33.4 %multiply_convert_fusion.1 = bf16[2,12,64,1024]{3,2,1,0:T(8,128)(2,1)} fusion(bf16[2,1024,12,64]{1,3,2,0:T(8,128)(2,1)S(1)} %bitcast.231, f32[2,12,1024,1024]{3,2,0,1:T(8,128)} %fusion.36), kind=kOutput, calls=%fused_computation.116 | convolution fusion | flops 3249537024 | bytes 106954752 | tf_op jit(solution)/shard_map/rhqk,rqhd->rkhd/dot_general | solution.py:183
  1119.3 36.8 %broadcast_subtract_fusion = f32[2,12,1024,1024]{3,2,0,1:T(8,128)} fusion(f32[2,12,1024]{2,0,1:T(2,128)S(1)} %copy.171, bf16[2,1024,12,64]{1,3,2,0:T(8,128)(2,1)} %bitcast.249, bf16[2,1024,12,64]{1,0,3,2:T(2,128)(2,1)S(1)} %copy-done.10), kind=kOutput, calls=%fused_computation.24 | convolution fusion | flops 3246391296 | bytes 107053056 | tf_op jit(solution)/shard_map/rqhd,rkhd->rhqk/dot_general | solution.py:163
  1157.6 105.2 %fusion.113 = (f32[2,1024]{1,0:T(2,128)S(1)}, f32[2,1024,1024]{2,1,0:T(8,128)}, f32[2,12,1024,1024]{3,2,1,0:T(8,128)}) fusion(f32[2,12,1024,1024]{3,2,0,1:T(8,128)} %broadcast_subtract_fusion, f32[2,12,1024,1024]{3,2,1,0:T(8,128)} %get-tuple-element.50, f32[2,12,1024]{2,1,0:T(8,128)S(1)} %copy-done.33, pred[2,1024,1024]{2,1,0:T(8,128)(4,1)S(1)} %copy-done.13), kind=kLoop, calls=%fused_computation.198 | loop fusion | flops 123729920 | bytes 312582144 | tf_op jit(solution)/shard_map/reduce_sum | solution.py:168
  1321.3 41.1 %fusion.25 = f32[2,12,64,1024]{3,2,1,0:T(8,128)} fusion(bf16[2,1024,12,64]{1,3,2,0:T(8,128)(2,1)} %bitcast.241, f32[2,12,1024,1024]{3,2,1,0:T(8,128)} %fusion.35), kind=kOutput, calls=%fused_computation.36 | convolution fusion | flops 3246391296 | bytes 110100480 | tf_op jit(solution)/shard_map/rhqk,rkhd->rqhd/dot_general | solution.py:177
  1362.5 38.1 %fusion.70 = bf16[2,1024,12,64]{1,3,2,0:T(8,128)(2,1)} fusion(f32[2,12,64,1024]{3,2,1,0:T(8,128)} %fusion.25, bf16[2,1024,12,64]{1,3,2,0:T(8,128)(2,1)S(1)} %bitcast.239, f32[2,12,1024,1024]{3,2,0,1:T(8,128)} %fusion.36), kind=kOutput, calls=%fused_computation.132 | convolution fusion | flops 3251109888 | bytes 113246208 | tf_op jit(solution)/shard_map/rhqk,rkhd->rqhd/dot_general | solution.py:177
  1413.2 35.0 %broadcast_multiply_fusion.2 = f32[2,12,64,1024]{3,2,1,0:T(8,128)} fusion(bf16[2,1024,12,64]{1,3,2,0:T(8,128)(2,1)S(1)} %bitcast.232, f32[2,12,1024,1024]{3,2,1,0:T(8,128)} %fusion.35), kind=kOutput, calls=%fused_computation.137 | convolution fusion | flops 3247964160 | bytes 110100480 | tf_op jit(solution)/shard_map/rhqk,rqhd->rkhd/dot_general | solution.py:183
  1510.1 43.7 %all-reduce.4 = (f32[768]{0:T(1024)S(1)}, f32[768]{0:T(1024)S(1)}) all-reduce(f32[768]{0:T(1024)S(1)} %get-tuple-element.38, f32[768]{0:T(1024)S(1)} %copy-done.63), channel_id=6, replica_groups=mesh['row'=16,'seq'=2] {'row','seq'}, use_global_device_ids=true, to_apply=%region_30.31.clone | all-reduce | flops 1536 | bytes 12288
  1563.6 34.9 %reduce-scatter.5.cloned.1.call-done = f32[24,2304]{1,0:T(8,128)} async-done(((f32[768,2304]{1,0:T(8,128)}), f32[24,2304]{1,0:T(8,128)}) %reduce-scatter.5.cloned.1.call-update) | async-done | bytes 221200 | tf_op jit(solution)/shard_map/reduce_scatter | solution.py:212
  (267 shorter events, 460.2 us)
Async XLA Ops:
  7.2 67.3 %all-gather.5.cloned.1.call-start = ((), (), s32[]{:S(2)}) async-start(), calls=%async_computation.4 | async-start | bytes 3649536 | tf_op jit(solution)/shard_map/all_gather | solution.py:68
  9.0 671.5 %all-gather.7.cloned.1.call-start = ((), (), s32[]{:S(2)}) async-start(), calls=%async_computation.5 | async-start | bytes 1216512 | tf_op jit(solution)/shard_map/all_gather | solution.py:69
  10.6 679.3 %all-gather.9.cloned.1.call-start = ((), (), s32[]{:S(2)}) async-start(), calls=%async_computation.6 | async-start | bytes 4866048 | tf_op jit(solution)/shard_map/all_gather | solution.py:70
  12.3 765.1 %all-gather.11.cloned.1.call-start = ((), (), s32[]{:S(2)}) async-start(), calls=%async_computation.7 | async-start | bytes 4866048 | tf_op jit(solution)/shard_map/all_gather | solution.py:71
  14.0 1549.6 %reduce-scatter.7.cloned.1.call-start = ((), (), s32[]{:S(2)}) async-start(), calls=%async_computation.9 | async-start | bytes 2433024 | tf_op jit(solution)/shard_map/reduce_scatter | solution.py:213
  66.9 225.3 %copy-start.37 = (s32[2,1024]{1,0:T(2,128)}, s32[2,1024]{1,0:T(2,128)S(1)}, u32[]{:S(2)}) copy-start(s32[2,1024]{1,0:T(2,128)S(1)} %get-tuple-element.66) | copy-start | bytes 24580
  66.9 225.3 %copy-start.44 = (s32[2,1024]{1,0:T(2,128)}, s32[2,1024]{1,0:T(2,128)S(1)}, u32[]{:S(2)}) copy-start(s32[2,1024]{1,0:T(2,128)S(1)} %get-tuple-element.65) | copy-start | bytes 24580
  66.9 225.3 %copy-start.46 = (s32[2,1024]{1,0:T(2,128)}, s32[2,1024]{1,0:T(2,128)S(1)}, u32[]{:S(2)}) copy-start(s32[2,1024]{1,0:T(2,128)S(1)} %get-tuple-element.67) | copy-start | bytes 24580
  87.8 156.3 %collective-permute-start = (bf16[2,1024,1536]{2,1,0:T(8,128)(2,1)}, bf16[2,1024,1536]{2,1,0:T(8,128)(2,1)}, u32[]{:S(2)}, u32[]{:S(2)}) collective-permute-start(bf16[2,1024,1536]{2,1,0:T(8,128)(2,1)} %slice.140), channel_id=1, source_target_pairs={{0,1},{2,3},{4,5},{6,7},{8,9},{10,11},{12,13},{14,15},{16,17},{18,... | collective-permute-start | bytes 18874376 | tf_op jit(solution)/shard_map/ppermute | solution.py:21
  116.7 138.0 %copy-start.2 = (bf16[2,1024,768]{1,2,0:T(8,128)(2,1)}, bf16[2,1024,768]{1,2,0:T(8,128)(2,1)S(1)}, u32[]{:S(2)}) copy-start(bf16[2,1024,768]{1,2,0:T(8,128)(2,1)S(1)} %copy.141) | copy-start | bytes 9437188
  349.8 113.3 %collective-permute-start.1 = (f32[2,1024]{1,0:T(2,128)S(1)}, f32[2,1024]{1,0:T(2,128)S(1)}, u32[]{:S(2)}, u32[]{:S(2)}) collective-permute-start(f32[2,1024]{1,0:T(2,128)S(1)} %bitcast.267), channel_id=1, source_target_pairs={{0,1},{2,3},{4,5},{6,7},{8,9},{10,11},{12,13},{14,15},{16,17},{18,... | collective-permute-start | bytes 24584 | tf_op jit(solution)/shard_map/ppermute | solution.py:21
  366.6 75.9 %copy-start.11 = (f32[2,1024,8,128]{1,2,3,0:T(8,128)S(1)}, f32[2,1024,8,128]{1,2,3,0:T(8,128)}, u32[]{:S(2)}) copy-start(f32[2,1024,8,128]{1,2,3,0:T(8,128)} %fusion.47) | copy-start | bytes 25165828
  442.6 202.5 %copy-start.28 = (f32[2,12,1024]{2,1,0:T(8,128)}, f32[2,12,1024]{2,1,0:T(8,128)S(1)}, u32[]{:S(2)}) copy-start(f32[2,12,1024]{2,1,0:T(8,128)S(1)} %get-tuple-element.49) | copy-start | bytes 294916
  513.8 131.3 %copy-start.30 = (f32[2,12,1024]{2,0,1:T(2,128)}, f32[2,12,1024]{2,0,1:T(2,128)S(1)}, u32[]{:S(2)}) copy-start(f32[2,12,1024]{2,0,1:T(2,128)S(1)} %fusion.8) | copy-start | bytes 294916
  685.8 137.7 %copy-start.50 = (f32[2048]{0:T(1024)}, f32[2048]{0:T(1024)S(1)}, u32[]{:S(2)}) copy-start(f32[2048]{0:T(1024)S(1)} %broadcast_multiply_fusion.3) | copy-start | bytes 24580
  689.9 133.6 %copy-start.59 = (f32[2048]{0:T(1024)}, f32[2048]{0:T(1024)S(1)}, u32[]{:S(2)}) copy-start(f32[2048]{0:T(1024)S(1)} %fusion.104) | copy-start | bytes 24580
  689.9 69.6 %copy-start.29 = (f32[2,12,1024]{2,1,0:T(8,128)S(1)}, f32[2,12,1024]{2,1,0:T(8,128)}, u32[]{:S(2)}) copy-start(f32[2,12,1024]{2,1,0:T(8,128)} %copy-done.28) | copy-start | bytes 294916
  690.0 74.1 %copy-start.19 = (bf16[2,1024,768]{2,1,0:T(8,128)(2,1)S(1)}, bf16[2,1024,768]{2,1,0:T(8,128)(2,1)}, u32[]{:S(2)}) copy-start(bf16[2,1024,768]{2,1,0:T(8,128)(2,1)} %param.21) | copy-start | bytes 9437188
  759.7 90.4 %copy-start.32 = (f32[2,12,1024]{2,1,0:T(8,128)}, f32[2,12,1024]{2,1,0:T(8,128)S(1)}, u32[]{:S(2)}) copy-start(f32[2,12,1024]{2,1,0:T(8,128)S(1)} %fusion.97) | copy-start | bytes 294916
  894.6 669.0 %reduce-scatter.11.cloned.1.call-start = ((), (), s32[]{:S(2)}) async-start(), calls=%async_computation.11 | async-start | bytes 9732096 | tf_op jit(solution)/shard_map/reduce_scatter | solution.py:215
  1050.0 256.3 %collective-permute-start.2 = (bf16[2,1024]{1,0:T(2,128)(2,1)}, bf16[2,1024]{1,0:T(2,128)(2,1)}, u32[]{:S(2)}, u32[]{:S(2)}) collective-permute-start(bf16[2,1024]{1,0:T(2,128)(2,1)} %convert_element_type.116), channel_id=1, source_target_pairs={{1,0},{3,2},{5,4},{7,6},{9,8},{11,10},{13,12},{15,14},{17,16},{19,... | collective-permute-start | bytes 12296 | tf_op jit(solution)/shard_map/ppermute | solution.py:21
  1118.0 337.3 %collective-permute-start.3 = (bf16[2,1024,1536]{2,1,0:T(8,128)(2,1)}, bf16[2,1024,1536]{2,1,0:T(8,128)(2,1)}, u32[]{:S(2)}, u32[]{:S(2)}) collective-permute-start(bf16[2,1024,1536]{2,1,0:T(8,128)(2,1)} %pad_maximum_fusion.1), channel_id=1, source_target_pairs={{1,0},{3,2},{5,4},{7,6},{9,8},{11,10},{13,12},{15,14},{17,16},{19,... | collective-permute-start | bytes 18874376 | tf_op jit(solution)/shard_map/ppermute | solution.py:21
  1156.1 407.5 %reduce-scatter.9.cloned.1.call-start = ((), (), s32[]{:S(2)}) async-start(), calls=%async_computation.10 | async-start | bytes 9732096 | tf_op jit(solution)/shard_map/reduce_scatter | solution.py:214
  1306.2 292.3 %reduce-scatter.5.cloned.1.call-start = ((), (), s32[]{:S(2)}) async-start(), calls=%async_computation.8 | async-start | bytes 7299072 | tf_op jit(solution)/shard_map/reduce_scatter | solution.py:212
  (53 other events, 878.0 us)
Sparse Core Ops, SparseCore 0:
  11.5 62.8 all-gather.4
  77.9 53.0 all-gather.6
  134.5 64.5 all-gather.8
  202.4 71.7 all-gather.10
  894.7 97.5 reduce-scatter.6
  1156.2 153.8 reduce-scatter.10
  1316.6 134.6 reduce-scatter.8
  1476.1 122.3 reduce-scatter.4
where the time goes:
time: 1610 us
  matrix products  688 us (43%)
  other arithmetic  525 us (33%)
  local copies, waits for them, and re-layouts  146 us (9%)
  waiting for transfers between devices  132 us (8%)
  blocking collectives  85.9 us (5%)
    dot_general x2, matrix products, body(): jnp.einsum('rqhd,rkhd->rhqk', d_mixed, value_heads, preferred_element_typ...  127 us
    reduce_max x2, other arithmetic, body(): new_max = jnp.maximum(running_max, jnp.max(logits, axis=-1))  113 us
    reduce_sum x1, other arithmetic, body(): column = jnp.sum(summed, axis=1)  105 us
    ppermute x4, waiting for transfers between devices, from_behind(): lax.ppermute(value, axis, [(source, source + steps) for source in range(f...  89.5 us
    unnamed x2, blocking collectives  85.9 us
    dot_general x2, matrix products, body(): jnp.einsum('rhqk,rkhd->rqhd', grad_scores, key_heads, preferred_element_t...  79.2 us
    dot_general x2, matrix products, body(): jnp.einsum('rhqk,rqhd->rkhd', attention_low, d_mixed, preferred_element_t...  79 us
    dot_general x2, matrix products, block_logits(): jnp.einsum('rqhd,rkhd->rhqk', queries, key_heads, preferred_element_type=...  75.2 us
  transfers between devices with their start and end apart: 12, of which 3 were waited for; matrix products, arithmetic and copies ran while one was open for 76% of the time, Pallas kernels for 0%

commit v1 on v0

--- a/solution.py
+++ b/solution.py
@@ -4,15 +4,731 @@
 import jax
 import jax.numpy as jnp
 from jax import lax
+from jax.experimental import pallas as pl
+from jax.experimental.pallas import tpu as pltpu
 from jax.sharding import PartitionSpec as P
 
 H = 12
 HD = 64
 ROW_LEN = 2048
-
-
 EPSILON = 1e-05
 MASKED = -1e30
+BIG = 1e30
+LOG2E = 1.4426950408889634
+OFFSET = math.log(ROW_LEN / 2.0) + 0.5
+SAFE = 64.0
+B = 256
+BT = 512
+MIB = 2**20
+F32 = jnp.float32
+BF = jnp.bfloat16
+
+
+def dot(a, b):
+    return jnp.dot(a, b, preferred_element_type=F32)
+
+
+def dot_nt(a, b):
+    return lax.dot_general(a, b, (((1,), (1,)), ((), ())), preferred_element_type=F32)
+
+
+def dot_tn(a, b):
+    return lax.dot_general(a, b, (((0,), (0,)), ((), ())), preferred_element_type=F32)
+
+
+def iota(shape, dim):
+    return lax.broadcasted_iota(jnp.int32, shape, dim)
+
+
+def half_lanes(rows):
+    return iota((rows, 128), 1) < HD
+
+
+def pick_columns(c):
+    return (iota((512, 128), 0) == 4 * iota((512, 128), 1) + c).astype(F32).astype(BF)
+
+
+def pick_rows(piece, c):
+    return (iota((piece, 4 * piece), 1) == 4 * iota((piece, 4 * piece), 0) + c).astype(F32).astype(BF)
+
+
+def pack_kernel(qkv_ref, out_ref, up_ref, down_ref, ga_ref, gm_ref, o_ref):
+    piece, features = out_ref.shape
+    lane = iota((piece, 128), 1)
+    col = 3 * features
+    o_ref[:, :col] = qkv_ref[...].astype(BF)
+    o_ref[:, col : col + features] = out_ref[...].astype(BF)
+    col += features
+    for c in range(4):
+        pick = pick_columns(c)
+        for tile in range(features // 128):
+            part = up_ref[:, 512 * tile : 512 * tile + 512].astype(BF)
+            o_ref[:, col + 128 * tile : col + 128 * tile + 128] = dot(part, pick).astype(BF)
+        col += features
+    for c in range(4):
+        o_ref[:, col : col + features] = dot(pick_rows(piece, c), down_ref[...].astype(BF)).astype(BF)
+        col += features
+    gains = jnp.where(lane == 0, ga_ref[...], jnp.where(lane == 1, gm_ref[...], 0.0))
+    o_ref[:, col : col + 128] = gains.astype(BF)
+
+
+def pack(w_qkv, w_out, w_up, w_down, gain_attn, gain_mlp):
+    piece, features = w_out.shape
+    return pl.pallas_call(
+        pack_kernel,
+        out_shape=jax.ShapeDtypeStruct((piece, 12 * features + 128), BF),
+        name="pack_weights",
+    )(w_qkv, w_out, w_up, w_down, gain_attn[:, None], gain_mlp[:, None])
+
+
+def unpack_kernel(b_ref, out_ref, up_ref, down_ref):
+    piece, features = out_ref.shape
+    out_ref[...] = b_ref[:, :features].astype(F32)
+    for tile in range(features // 128):
+        total = None
+        for c in range(4):
+            col = features * (1 + c) + 128 * tile
+            part = dot_nt(b_ref[:, col : col + 128], pick_columns(c))
+            total = part if total is None else total + part
+        up_ref[:, 512 * tile : 512 * tile + 512] = total
+    total = None
+    for c in range(4):
+        col = features * (5 + c)
+        part = dot_tn(pick_rows(piece, c), b_ref[:, col : col + features])
+        total = part if total is None else total + part
+    down_ref[...] = total
+
+
+def unpack(buffer):
+    piece = buffer.shape[0]
+    features = (buffer.shape[1] - 128) // 9
+    return pl.pallas_call(
+        unpack_kernel,
+        out_shape=(
+            jax.ShapeDtypeStruct((piece, features), F32),
+            jax.ShapeDtypeStruct((piece, 4 * features), F32),
+            jax.ShapeDtypeStruct((4 * piece, features), F32),
+        ),
+        name="unpack_gradients",
+    )(buffer)
+
+
+def moments(values):
+    mean_value = jnp.mean(values, axis=-1, keepdims=True)
+    shifted = values - mean_value
+    spread = jnp.mean(shifted * shifted, axis=-1, keepdims=True)
+    return shifted, lax.rsqrt(spread + EPSILON)
+
+
+def qkv_kernel(x_ref, gain_ref, wq_ref, wk_ref, wv_ref, q_ref, k_ref, v_ref, qt_ref, rows_ref, size_ref):
+    features = x_ref.shape[1]
+
+    @pl.when(pl.program_id(0) == 0)
+    def _():
+        rows_ref[...] = gain_ref[...].astype(F32).T[:8]
+        size_ref[...] = jnp.zeros_like(size_ref)
+
+    shifted, scale = moments(x_ref[...].astype(F32))
+    normed = (shifted * scale * rows_ref[0:1, :]).astype(BF)
+    low = half_lanes(x_ref.shape[0])
+    heads = (iota((features, 128), 0) // HD == iota((features, 128), 1)).astype(F32).astype(BF)
+
+    def spread(ref, packed, other):
+        for p in range(H // 2):
+            pair = packed[:, 128 * p : 128 * p + 128]
+            ref[:, 256 * p : 256 * p + 128] = jnp.where(low, pair, other).astype(BF)
+            ref[:, 256 * p + 128 : 256 * p + 256] = jnp.where(low, other, pair).astype(BF)
+
+    q = dot(normed, wq_ref[...]) * (LOG2E / math.sqrt(HD))
+    qt_ref[...] = q.astype(BF).T
+    spread(q_ref, q, 0.0)
+    size_ref[0:1] = jnp.maximum(size_ref[0:1], jnp.max(dot((q * q).astype(BF), heads), axis=0, keepdims=True))
+    k = dot(normed, wk_ref[...])
+    spread(k_ref, k, 1.0)
+    size_ref[1:2] = jnp.maximum(size_ref[1:2], jnp.max(dot((k * k).astype(BF), heads), axis=0, keepdims=True))
+    spread(v_ref, dot(normed, wv_ref[...]), 1.0)
+
+
+def project_qkv(x, weights):
+    tokens, features = x.shape
+    last = weights.shape[1] // 128 - 1
+
+    def column(i):
+        return pl.BlockSpec((features, features), lambda t: (0, i))
+
+    def tall(cols):
+        return pl.BlockSpec((BT, cols), lambda t: (t, 0))
+
+    return pl.pallas_call(
+        qkv_kernel,
+        grid=(tokens // BT,),
+        in_specs=[
+            tall(features),
+            pl.BlockSpec((features, 128), lambda t: (0, last)),
+            column(0),
+            column(1),
+            column(2),
+        ],
+        out_specs=[
+            tall(2 * features),
+            tall(2 * features),
+            tall(2 * features),
+            pl.BlockSpec((features, BT), lambda t: (0, t)),
+            pl.BlockSpec((8, features), lambda t: (0, 0)),
+            pl.BlockSpec((8, 128), lambda t: (0, 0)),
+        ],
+        out_shape=[
+            jax.ShapeDtypeStruct((tokens, 2 * features), BF),
+            jax.ShapeDtypeStruct((tokens, 2 * features), BF),
+            jax.ShapeDtypeStruct((tokens, 2 * features), BF),
+            jax.ShapeDtypeStruct((features, tokens), BF),
+            jax.ShapeDtypeStruct((8, features), F32),
+            jax.ShapeDtypeStruct((8, 128), F32),
+        ],
+        compiler_params=pltpu.CompilerParams(vmem_limit_bytes=48 * MIB),
+        name="project_qkv",
+    )(x, weights, weights, weights, weights)
+
+
+def selection(scores, segq, segk, ib, jb):
+    rows = iota((B, B), 0) + ib * B
+    cols = iota((B, B), 1) + jb * B
+    same = segq == segk
+    x = scores - OFFSET * LOG2E
+    soft = jnp.maximum(x, 0.0) + jnp.log2(1.0 + jnp.exp2(-jnp.abs(x)))
+    return jnp.where(same & (cols < rows), soft, 0.0), same & (cols <= rows)
+
+
+def two_part(tri, values):
+    high = values.astype(BF)
+    rest = (values - high.astype(F32)).astype(BF)
+    return dot(tri, high) + dot(tri, rest)
+
+
+def forward_kernel(tab, q_ref, k_ref, v_ref, segq_ref, segk_ref, k_any, seg_any, o_ref, li_ref, e_ref,
+                   acc, carry, tri, qx, kbuf, segbuf, sem):
+    t = pl.program_id(0)
+    ib, jb = tab[3, t], tab[4, t]
+
+    @pl.when(t == 0)
+    def _():
+        carry[...] = jnp.zeros_like(carry)
+        tri[...] = (iota((B, B), 1) < iota((B, B), 0)).astype(F32).astype(BF)
+
+    @pl.when(jb == 0)
+    def _():
+        acc[...] = jnp.zeros_like(acc)
+        qx[...] = q_ref[...]
+
+        @pl.when(tab[6, t] != 0)
+        def _():
+            lane = iota((B, 128), 1)
+
+            def step(other, top):
+                base = tab[1, t + other]
+                copies = (
+                    pltpu.make_async_copy(k_any.at[pl.ds(pl.multiple_of(base * B, B), B), :], kbuf, sem.at[0]),
+                    pltpu.make_async_copy(seg_any.at[base], segbuf, sem.at[1]),
+                )
+                for copy in copies:
+                    copy.start()
+                for copy in copies:
+                    copy.wait()
+                first = dot_nt(q_ref[:, 0:128], kbuf[:, 0:128])
+                chosen, kept = selection(first, segq_ref[...], segbuf[0:1, :], ib, other)
+                penalty = jnp.where(kept, two_part(tri[...], chosen) + carry[other, 0:1, :], BIG)
+                for h in range(H):
+                    w = slice(128 * h, 128 * h + 128)
+                    z = dot_nt(q_ref[:, w], kbuf[:, w]) - penalty
+                    top = jnp.where(lane == h, jnp.maximum(top, jnp.max(z, axis=1, keepdims=True)), top)
+                return top
+
+            top = lax.fori_loop(0, ib + 1, step, jnp.full((B, 128), -BIG, F32))
+            for h in range(H):
+                shift = -jnp.sum(jnp.where(lane == h, top, 0.0), axis=1, keepdims=True)
+                one = shift.astype(BF).astype(F32)
+                two = (shift - one).astype(BF).astype(F32)
+                three = shift - one - two
+                at = lane - (HD if h % 2 == 0 else 0)
+                extra = jnp.where(at == 0, one, jnp.where(at == 1, two, jnp.where(at == 2, three, 0.0)))
+                w = slice(128 * h, 128 * h + 128)
+                keep = (lane < HD) if h % 2 == 0 else (lane >= HD)
+                qx[:, w] = jnp.where(keep, q_ref[:, w].astype(F32), extra).astype(BF)
+
+    @pl.when(tab[2, t] != 0)
+    def _():
+        first = dot_nt(q_ref[:, 0:128], k_ref[:, 0:128])
+        chosen, kept = selection(first, segq_ref[...], segk_ref[0, 0:1, :], ib, jb)
+        penalty = jnp.where(kept, two_part(tri[...], chosen) + carry[jb, 0:1, :], BIG)
+        carry[jb, 0:1, :] = carry[jb, 0:1, :] + jnp.sum(chosen, axis=0, keepdims=True)
+        for h in range(H):
+            w = slice(128 * h, 128 * h + 128)
+            e = jnp.exp2(dot_nt(qx[:, w], k_ref[:, w]) - penalty).astype(BF)
+            e_ref[0, h] = e
+            acc[:, w] += dot(e, v_ref[:, w])
+
+    @pl.when(jb == ib)
+    def _():
+        low = half_lanes(B)
+        for p in range(H // 2):
+            one = acc[:, 256 * p : 256 * p + 128]
+            two = acc[:, 256 * p + 128 : 256 * p + 256]
+            inverse = 1.0 / pltpu.roll(jnp.where(low, two, one), HD, 1)
+            o_ref[:, 128 * p : 128 * p + 128] = (jnp.where(low, one, two) * inverse).astype(BF)
+            li_ref[:, 128 * p : 128 * p + 128] = inverse
+
+
+def attention_forward(table, q, k, v, seg_col, seg_row):
+    tokens = q.shape[0]
+    blocks = tokens // B
+    tiles = table.shape[1]
+    wide = 128 * H
+    narrow = HD * H
+    return pl.pallas_call(
+        forward_kernel,
+        grid_spec=pltpu.PrefetchScalarGridSpec(
+            num_scalar_prefetch=1,
+            grid=(tiles,),
+            in_specs=[
+                pl.BlockSpec((B, wide), lambda t, tab: (tab[0, t], 0)),
+                pl.BlockSpec((B, wide), lambda t, tab: (tab[1, t], 0)),
+                pl.BlockSpec((B, wide), lambda t, tab: (tab[1, t], 0)),
+                pl.BlockSpec((B, 1), lambda t, tab: (tab[0, t], 0)),
+                pl.BlockSpec((1, 8, B), lambda t, tab: (tab[1, t], 0, 0)),
+                pl.BlockSpec(memory_space=pl.ANY),
+                pl.BlockSpec(memory_space=pl.ANY),
+            ],
+            out_specs=[
+                pl.BlockSpec((B, narrow), lambda t, tab: (tab[0, t], 0)),
+                pl.BlockSpec((B, narrow), lambda t, tab: (tab[0, t], 0)),
+                pl.BlockSpec((1, H, B, B), lambda t, tab: (tab[5, t], 0, 0, 0)),
+            ],
+            scratch_shapes=[
+                pltpu.VMEM((B, wide), F32),
+                pltpu.VMEM((blocks, 8, B), F32),
+                pltpu.VMEM((B, B), BF),
+                pltpu.VMEM((B, wide), BF),
+                pltpu.VMEM((B, wide), BF),
+                pltpu.VMEM((8, B), jnp.int32),
+                pltpu.SemaphoreType.DMA((2,)),
+            ],
+        ),
+        out_shape=[
+            jax.ShapeDtypeStruct((tokens, narrow), BF),
+            jax.ShapeDtypeStruct((tokens, narrow), F32),
+            jax.ShapeDtypeStruct((tiles, H, B, B), BF),
+        ],
+        compiler_params=pltpu.CompilerParams(vmem_limit_bytes=56 * MIB),
+        name="attention_forward",
+    )(table, q, k, v, seg_col, seg_row, k, seg_row)
+
+
+def backward_kernel(tab, e_ref, q_ref, k_ref, v_ref, d_ref, qt_ref, dt_ref, segq_ref, segk_ref, o_ref,
+                    dq, dkt, dvt, carry, tri):
+    t = pl.program_id(0)
+    ib, jb = tab[3, t], tab[4, t]
+    narrow = HD * H
+
+    @pl.when(t == 0)
+    def _():
+        carry[...] = jnp.zeros_like(carry)
+        tri[...] = (iota((B, B), 1) > iota((B, B), 0)).astype(F32).astype(BF)
+        dkt[...] = jnp.zeros_like(dkt)
+        dvt[...] = jnp.zeros_like(dvt)
+
+    @pl.when(jb == 0)
+    def _():
+        dq[...] = jnp.zeros_like(dq)
+
+    @pl.when(tab[2, t] != 0)
+    def _():
+        low = half_lanes(B)
+        cols = pl.ds(pl.multiple_of(jb * B, B), B)
+        total = None
+        parts = {}
+        for h in list(range(1, H)) + [0]:
+            w = slice(128 * h, 128 * h + 128)
+            own = slice(HD * h, HD * h + HD)
+            e = e_ref[0, h]
+            dz = e.astype(F32) * dot_nt(d_ref[:, w], v_ref[:, w])
+            total = dz if total is None else total + dz
+            dvt[own, cols] += dot(dt_ref[own, :], e)
+            if h == 0:
+                gate = jax.nn.sigmoid(dot_nt(q_ref[:, w], k_ref[:, w]) * (1.0 / LOG2E) - OFFSET)
+                rows = iota((B, B), 0) + ib * B
+                keys = iota((B, B), 1) + jb * B
+                kept = (segq_ref[...] == segk_ref[0, 0:1, :]) & (keys < rows)
+                later = carry[jb, 0:1, :] + two_part(tri[...], total)
+                carry[jb, 0:1, :] = carry[jb, 0:1, :] + jnp.sum(total, axis=0, keepdims=True)
+                dz = dz - jnp.where(kept, later * gate, 0.0)
+            ds = dz.astype(BF)
+            dkt[own, cols] += dot(qt_ref[own, :], ds)
+            parts[h] = dot(ds, k_ref[:, w])
+            if h ^ 1 in parts:
+                p = h // 2
+                dq[:, 128 * p : 128 * p + 128] += jnp.where(low, parts[2 * p], parts[2 * p + 1])
+
+    @pl.when(jb == ib)
+    def _():
+        cols = pl.ds(pl.multiple_of(ib * B, B), B)
+        o_ref[:, :narrow] = (dq[...] * (1.0 / math.sqrt(HD))).astype(BF)
+        o_ref[:, narrow : 2 * narrow] = (dkt[:, cols] * (1.0 / LOG2E)).astype(BF).T
+        o_ref[:, 2 * narrow :] = dvt[:, cols].astype(BF).T
+
+
+def attention_backward(table, e, q, k, v, d, qt, dt, seg_col, seg_row):
+    tokens = q.shape[0]
+    blocks = tokens // B
+    tiles = table.shape[1]
+    wide = 128 * H
+    narrow = HD * H
+    return pl.pallas_call(
+        backward_kernel,
+        grid_spec=pltpu.PrefetchScalarGridSpec(
+            num_scalar_prefetch=1,
+            grid=(tiles,),
+            in_specs=[
+                pl.BlockSpec((1, H, B, B), lambda t, tab: (tab[5, t], 0, 0, 0)),
+                pl.BlockSpec((B, wide), lambda t, tab: (tab[0, t], 0)),
+                pl.BlockSpec((B, wide), lambda t, tab: (tab[1, t], 0)),
+                pl.BlockSpec((B, wide), lambda t, tab: (tab[1, t], 0)),
+                pl.BlockSpec((B, wide), lambda t, tab: (tab[0, t], 0)),
+                pl.BlockSpec((narrow, B), lambda t, tab: (0, tab[0, t])),
+                pl.BlockSpec((narrow, B), lambda t, tab: (0, tab[0, t])),
+                pl.BlockSpec((B, 1), lambda t, tab: (tab[0, t], 0)),
+                pl.BlockSpec((1, 8, B), lambda t, tab: (tab[1, t], 0, 0)),
+            ],
+            out_specs=pl.BlockSpec((B, 3 * narrow), lambda t, tab: (tab[0, t], 0)),
+            scratch_shapes=[
+                pltpu.VMEM((B, narrow), F32),
+                pltpu.VMEM((narrow, tokens), F32),
+                pltpu.VMEM((narrow, tokens), F32),
+                pltpu.VMEM((blocks, 8, B), F32),
+                pltpu.VMEM((B, B), BF),
+            ],
+        ),
+        out_shape=jax.ShapeDtypeStruct((tokens, 3 * narrow), BF),
+        compiler_params=pltpu.CompilerParams(vmem_limit_bytes=60 * MIB),
+        name="attention_backward",
+    )(table, e, q, k, v, d, qt, dt, seg_col, seg_row)
+
+
+def tile_tables(segments, first, slow):
+    blocks = segments.shape[0] // B
+    ib = jnp.array([i for i in range(blocks) for j in range(i + 1)], jnp.int32)
+    jb = jnp.array([j for i in range(blocks) for j in range(i + 1)], jnp.int32)
+    back_ib = jnp.array([i for i in reversed(range(blocks)) for j in range(i + 1)], jnp.int32)
+    back_jb = jnp.array([j for i in reversed(range(blocks)) for j in range(i + 1)], jnp.int32)
+    heads = segments[::B]
+    tails = segments[B - 1 :: B]
+    touch = (heads[:, None] <= tails[None, :]).astype(jnp.int32)
+    shift = first * (blocks // 2)
+
+    def table(rows, keys):
+        active = touch[rows, keys]
+        return jnp.stack(
+            [
+                (rows + shift) % blocks,
+                (keys + shift) % blocks,
+                active,
+                rows,
+                keys,
+                rows * (rows + 1) // 2 + keys,
+                jnp.broadcast_to(slow, rows.shape),
+            ]
+        )
+
+    return table(ib, jb), table(back_ib, back_jb)
+
+
+def mlp_kernel(x_ref, ob_ref, dy_ref, li_ref, gain_ref, wo_ref, wu_ref, wd_ref, out_ref, dx_ref, d_ref, dt_ref, g_any,
+               xh, scales, y, dn, n2, gup, gdown, gout, gsum, stage, sem):
+    c, t = pl.program_id(0), pl.program_id(1)
+    chunks, steps = pl.num_programs(0), pl.num_programs(1)
+    rows = pl.ds(pl.multiple_of(t * BT, BT), BT)
+    features = x_ref.shape[1]
+
+    def send(slot, column):
+        start = pl.multiple_of(column, 128)
+        return pltpu.make_async_copy(stage.at[slot], g_any.at[:, pl.ds(start, features)], sem.at[slot])
+
+    @pl.when(c == 0)
+    def _():
+        middle = x_ref[...].astype(F32) + dot(ob_ref[...], wo_ref[...])
+        shifted, scale = moments(middle)
+        xh[rows, :] = (shifted * scale).astype(BF)
+        scales[rows, :] = jnp.broadcast_to(scale, (BT, 128))
+        y[rows, :] = middle
+        dn[rows, :] = jnp.zeros_like(middle)
+        n2[rows, :] = (shifted * scale * gain_ref[1:2, :]).astype(BF)
+
+    @pl.when(t == 0)
+    def _():
+        gup[...] = jnp.zeros_like(gup)
+        gdown[...] = jnp.zeros_like(gdown)
+
+    @pl.when((c == 0) & (t == 0))
+    def _():
+        gout[...] = jnp.zeros_like(gout)
+        gsum[...] = jnp.zeros_like(gsum)
+
+    n2_low = n2[rows, :]
+    dy_low = dy_ref[...]
+    u = dot(n2_low, wu_ref[...])
+    da = dot_nt(dy_low, wd_ref[...])
+    cdf = 0.5 * (1.0 + lax.erf(u * math.sqrt(0.5)))
+    density = jnp.exp(-0.5 * u * u) * (1.0 / math.sqrt(2.0 * math.pi))
+    active = (u * cdf).astype(BF)
+    du = ((cdf + u * density) * da).astype(BF)
+    y[rows, :] += dot(active, wd_ref[...])
+    gdown[...] += dot_tn(active, dy_low)
+    gup[...] += dot_tn(n2_low, du)
+    dn[rows, :] += dot_nt(du, wu_ref[...])
+
+    @pl.when(t == steps - 1)
+    def _():
+        @pl.when(c > 0)
+        def _():
+            send(0, c * features).wait()
+            send(1, (c + chunks) * features).wait()
+
+        stage[0] = gup[...].astype(BF)
+        stage[1] = gdown[...].astype(BF)
+        send(0, (1 + c) * features).start()
+        send(1, (1 + c + chunks) * features).start()
+
+    @pl.when(c == chunks - 1)
+    def _():
+        out_ref[...] = y[rows, :].astype(BF)
+        d_normed = dn[rows, :]
+        scale = scales[rows, 0:1]
+        unit = xh[rows, :].astype(F32)
+        product = d_normed * unit
+        gsum[...] += jnp.sum(product.reshape(BT // 8, 8, features), axis=0)
+        inner = d_normed * gain_ref[1:2, :]
+        dx = dy_low.astype(F32) + scale * (
+            inner - jnp.mean(inner, axis=-1, keepdims=True) - unit * jnp.mean(inner * unit, axis=-1, keepdims=True)
+        )
+        dx_ref[...] = dx
+        db = dx.astype(BF)
+        gout[...] += dot_tn(ob_ref[...], db)
+        scaled = dot_nt(db, wo_ref[...]) * li_ref[...]
+        dt_ref[...] = scaled.astype(BF).T
+        low = half_lanes(BT)
+        lane = iota((BT, 128), 1)
+        swap_row, swap_col = iota((128, 128), 0), iota((128, 128), 1)
+        swap = ((swap_row // HD != swap_col // HD) & (swap_col % HD < 2)).astype(F32).astype(BF)
+        for p in range(H // 2):
+            w = slice(128 * p, 128 * p + 128)
+            pair = scaled[:, w]
+            both = pair * ob_ref[:, w].astype(F32)
+            high = both.astype(BF)
+            delta = dot(high, swap) + dot((both - high.astype(F32)).astype(BF), swap)
+            top = delta.astype(BF).astype(F32)
+            extra = jnp.where((lane == 0) | (lane == HD), -top, top - delta)
+            d_ref[:, 256 * p : 256 * p + 128] = jnp.where(low, pair, extra).astype(BF)
+            d_ref[:, 256 * p + 128 : 256 * p + 256] = jnp.where(low, extra, pair).astype(BF)
+
+    @pl.when((c == chunks - 1) & (t == steps - 1))
+    def _():
+        stage[2] = gout[...].astype(BF)
+        column = jnp.broadcast_to(jnp.sum(gsum[...], axis=0, keepdims=True), (128, features))
+        stage[3, :, :128] = column.T.astype(BF)
+        last = pltpu.make_async_copy(
+            stage.at[3, :, pl.ds(0, 128)], g_any.at[:, pl.ds((1 + 2 * 4) * features, 128)], sem.at[3]
+        )
+        send(2, 0).start()
+        last.start()
+        send(0, chunks * features).wait()
+        send(1, 2 * chunks * features).wait()
+        send(2, 0).wait()
+        last.wait()
+
+
+def feed_forward(x, ob, dy, li, gains, weights):
+    tokens, features = x.shape
+    steps = tokens // BT
+    chunks = 4
+
+    def ends(c, t):
+        return (jnp.where((c == 0) | (c == chunks - 1), t, steps - 1), 0)
+
+    def at_first(c, t):
+        return (jnp.where(c == 0, t, steps - 1), 0)
+
+    def at_last(c, t):
+        return (jnp.where(c == chunks - 1, t, 0), 0)
+
+    block = (BT, features)
+    once = pl.Buffered(1)
+    return pl.pallas_call(
+        mlp_kernel,
+        grid=(chunks, steps),
+        in_specs=[
+            pl.BlockSpec(block, at_first, pipeline_mode=once),
+            pl.BlockSpec(block, ends),
+            pl.BlockSpec(block, lambda c, t: (t, 0)),
+            pl.BlockSpec(block, at_last, pipeline_mode=once),
+            pl.BlockSpec((8, features), lambda c, t: (0, 0)),
+            pl.BlockSpec((features, features), lambda c, t: (0, 3), pipeline_mode=once),
+            pl.BlockSpec((features, features), lambda c, t: (0, 4 + c)),
+            pl.BlockSpec((features, features), lambda c, t: (0, 8 + c)),
+        ],
+        out_specs=[
+            pl.BlockSpec(block, at_last),
+            pl.BlockSpec(block, at_last),
+            pl.BlockSpec((BT, 2 * features), at_last),
+            pl.BlockSpec((features, BT), lambda c, t: (0, at_last(c, t)[0])),
+            pl.BlockSpec(memory_space=pl.ANY),
+        ],
+        out_shape=[
+            jax.ShapeDtypeStruct((tokens, features), BF),
+            jax.ShapeDtypeStruct((tokens, features), F32),
+            jax.ShapeDtypeStruct((tokens, 2 * features), BF),
+            jax.ShapeDtypeStruct((features, tokens), BF),
+            jax.ShapeDtypeStruct((features, 9 * features + 128), BF),
+        ],
+        scratch_shapes=[
+            pltpu.VMEM((tokens, features), BF),
+            pltpu.VMEM((tokens, 128), F32),
+            pltpu.VMEM((tokens, features), F32),
+            pltpu.VMEM((tokens, features), F32),
+            pltpu.VMEM((tokens, features), BF),
+            pltpu.VMEM((features, features), F32),
+            pltpu.VMEM((features, features), F32),
+            pltpu.VMEM((features, features), F32),
+            pltpu.VMEM((8, features), F32),
+            pltpu.VMEM((4, features, features), BF),
+            pltpu.SemaphoreType.DMA((4,)),
+        ],
+        compiler_params=pltpu.CompilerParams(vmem_limit_bytes=63 * MIB),
+        name="feed_forward",
+    )(x, ob, dy, li, gains, weights, weights, weights)
+
+
+def first_kernel(x_ref, dqkv_ref, dx_ref, gain_ref, wq_ref, wk_ref, wv_ref, out_ref, low_ref, g_ref, acc, gsum):
+    t = pl.program_id(0)
+    features = x_ref.shape[1]
+
+    @pl.when(t == 0)
+    def _():
+        acc[...] = jnp.zeros_like(acc)
+        gsum[...] = jnp.zeros_like(gsum)
+
+    shifted, scale = moments(x_ref[...].astype(F32))
+    xh = shifted * scale
+    gain = gain_ref[0:1, :]
+    normed = (xh * gain).astype(BF)
+    acc[...] += dot_tn(normed, dqkv_ref[...])
+    d_normed = (
+        dot_nt(dqkv_ref[:, :features], wq_ref[...])
+        + dot_nt(dqkv_ref[:, features : 2 * features], wk_ref[...])
+        + dot_nt(dqkv_ref[:, 2 * features :], wv_ref[...])
+    )
+    gsum[...] += jnp.sum((d_normed * xh).reshape(BT // 8, 8, features), axis=0)
+    inner = d_normed * gain
+    dx = dx_ref[...] + scale * (
+        inner - jnp.mean(inner, axis=-1, keepdims=True) - xh * jnp.mean(inner * xh, axis=-1, keepdims=True)
+    )
+    out_ref[...] = dx
+    low_ref[...] = dx.astype(BF)
+
+    @pl.when(t == pl.num_programs(0) - 1)
+    def _():
+        g_ref[:, : 3 * features] = acc[...].astype(BF)
+        column = jnp.broadcast_to(jnp.sum(gsum[...], axis=0, keepdims=True), (128, features))
+        g_ref[:, 3 * features :] = column.T.astype(BF)
+
+
+def first_gradients(x, dqkv, dx, gains, weights):
+    tokens, features = x.shape
+
+    def tall(cols):
+        return pl.BlockSpec((BT, cols), lambda t: (t, 0))
+
+    def column(i):
+        return pl.BlockSpec((features, features), lambda t: (0, i))
+
+    return pl.pallas_call(
+        first_kernel,
+        grid=(tokens // BT,),
+        in_specs=[
+            tall(features),
+            tall(3 * features),
+            tall(features),
+            pl.BlockSpec((8, features), lambda t: (0, 0)),
+            column(0),
+            column(1),
+            column(2),
+        ],
+        out_specs=[
+            tall(features),
+            tall(features),
+            pl.BlockSpec((features, 3 * features + 128), lambda t: (0, 0)),
+        ],
+        out_shape=[
+            jax.ShapeDtypeStruct((tokens, features), F32),
+            jax.ShapeDtypeStruct((tokens, features), BF),
+            jax.ShapeDtypeStruct((features, 3 * features + 128), BF),
+        ],
+        scratch_shapes=[pltpu.VMEM((features, 3 * features), F32), pltpu.VMEM((8, features), F32)],
+        compiler_params=pltpu.CompilerParams(vmem_limit_bytes=60 * MIB),
+        name="first_gradients",
+    )(x, dqkv, dx, gains, weights, weights, weights)
+
+
+def swap(value):
+    return lax.ppermute(value, "seq", [(0, 1), (1, 0)])
+
+
+def own_and_other(pair, position):
+    return (
+        lax.dynamic_index_in_dim(pair, position, 0, keepdims=False),
+        lax.dynamic_index_in_dim(pair, 1 - position, 0, keepdims=False),
+    )
+
+
+def in_order(own, other, position):
+    return jnp.where(position == 0, jnp.stack([own, other]), jnp.stack([other, own]))
+
+
+def row_body(tokens, segments, w_qkv, w_out, w_up, w_down, gain_attn, gain_mlp, cotangent):
+    both = ("row", "seq")
+    position = lax.axis_index("seq")
+    _, half, features = tokens.shape
+    own, other = own_and_other(tokens, position)
+    x = jnp.concatenate([own, swap(other)])
+    packed = pack(w_qkv, w_out, w_up, w_down, gain_attn, gain_mlp)
+    weights = lax.all_gather(packed, both, axis=0, tiled=True)
+    own, other = own_and_other(cotangent, position)
+    dy = jnp.concatenate([own, swap(other)])
+    row_segments = lax.dynamic_index_in_dim(segments, position, 0, keepdims=False)
+    stored = jnp.roll(row_segments, position * half)
+    seg_col = stored[:, None]
+    seg_row = jnp.broadcast_to(stored.reshape(-1, 1, B), (stored.shape[0] // B, 8, B))
+    q, k, v, qt, gains, sizes = project_qkv(x, weights)
+    slow = jnp.any(sizes[0] * sizes[1] * 1.05 > SAFE * SAFE).astype(jnp.int32)
+    table, back_table = tile_tables(row_segments, position, slow)
+    ob, li, e = attention_forward(table, q, k, v, seg_col, seg_row)
+    output, dx, d, dt, g_later = feed_forward(x, ob, dy, li, gains, weights)
+    r_later = lax.psum_scatter(g_later, both, scatter_dimension=0, tiled=True)
+    output = in_order(output[:half], swap(output[half:]), position)
+    dqkv = attention_backward(back_table, e, q, k, v, d, qt, dt, seg_col, seg_row)
+    d_tokens, d_low, g_first = first_gradients(x, dqkv, dx, gains, weights)
+    g_first, r_later = lax.optimization_barrier((g_first, r_later))
+    r_first = lax.psum_scatter(g_first, both, scatter_dimension=0, tiled=True)
+    d_tokens = in_order(d_tokens[:half], swap(d_low[half:]).astype(F32), position)
+    g_out, g_up, g_down = unpack(r_later)
+    return (
+        output,
+        d_tokens,
+        r_first[:, : 3 * features].astype(F32),
+        g_out,
+        g_up,
+        g_down,
+        r_first[:, 3 * features].astype(F32),
+        r_later[:, 9 * features].astype(F32),
+    )
 
 
 def from_behind(value, axis, steps):
@@ -26,6 +742,12 @@
     shifted = values - mean_value
     spread = jnp.mean(shifted * shifted, axis=-1, keepdims=True)
     return shifted * lax.rsqrt(spread + EPSILON) * scaling
+
+
+def running_sums(values):
+    places = jnp.arange(values.shape[1], dtype=jnp.int32)
+    upto = (places[None, :] <= places[:, None]).astype(jnp.float32)
+    return jnp.einsum("im,rmj->rij", upto, values, precision=lax.Precision.HIGHEST)
 
 
 def block_masks(segments, position, source, block_len):
@@ -49,13 +771,13 @@
     ) * (1.0 / math.sqrt(HD))
     attend_mask, select_mask = block_masks(segments, position, source, block_len)
     chosen = jnp.where(select_mask, jax.nn.softplus(scores[:, 0] - offset), 0.0)
-    running = jnp.cumsum(chosen, axis=1)
+    running = running_sums(chosen)
     penalty = carried[:, None, :] + running - chosen
     logits = jnp.where(attend_mask[:, None], scores - penalty[:, None], MASKED)
     return (scores, logits, attend_mask, select_mask, carried + running[:, -1])
 
 
-def body(tokens, segments, w_qkv, w_out, w_up, w_down, gain_attn, gain_mlp, cotangent):
+def ring_body(tokens, segments, w_qkv, w_out, w_up, w_down, gain_attn, gain_mlp, cotangent):
     low_pieces = (
         w_qkv.astype(jnp.bfloat16),
         w_out.astype(jnp.bfloat16),
@@ -166,7 +888,7 @@
         grad_logits = attention * (grad_attention - correction[..., None])
         summed = jnp.sum(grad_logits, axis=1)
         column = jnp.sum(summed, axis=1)
-        running = jnp.cumsum(summed, axis=1)
+        running = running_sums(summed)
         grad_chosen = jnp.where(
             select_mask, running - column[:, None, :] - grads_column[:, None, :], 0.0
         )
@@ -226,6 +948,12 @@
         reduced[4],
         reduced[5],
     )
+
+
+def body(tokens, *rest):
+    if lax.axis_size("seq") == 2 and tokens.shape[0] == 2:
+        return row_body(tokens, *rest)
+    return ring_body(tokens, *rest)
 
 
 def solution(mesh):

time: 1610 us -> 651 us (0.40)
  matrix products: 688 us -> 0 us
  other arithmetic: 525 us -> 19.9 us
  Pallas kernels: 0 us -> 347 us
  local copies, waits for them, and re-layouts: 146 us -> 21.1 us
  waiting for transfers between devices: 132 us -> 242 us
  blocking collectives: 85.9 us -> 0 us
    dot_general x24 -> x0, matrix products: 688 us -> none  [the longest x2 127 us: body(): jnp.einsum('rqhd,rkhd->rhqk', d_mixed, value_heads, preferred_element_typ...]
    pallas_call x0 -> x7, Pallas kernels: none -> 347 us  [the longest x1 125 us: attention_backward(): pl.pallas_call(backward_kernel, grid_spec=pltpu.PrefetchScalarGridSpec(nu...]
    reduce_sum x8 -> x0, other arithmetic: 173 us -> none  [the longest x1 105 us: body(): column = jnp.sum(summed, axis=1)]
    reduce_max x2 -> x0, other arithmetic: 113 us -> none  [body(): new_max = jnp.maximum(running_max, jnp.max(logits, axis=-1))]
    unnamed x2 -> x0, blocking collectives: 85.9 us -> none
    ppermute x4, waiting for transfers between devices: 89.5 us -> 162 us  [swap(): return lax.ppermute(value, 'seq', [(0, 1), (1, 0)])]
    another operation x13 -> x3, other arithmetic: 72.5 us -> 1.66 us  [the longest x1 1.64 us: in_order(): jnp.stack([own, other])]
    convert_element_type x13 -> x4, other arithmetic: 70.4 us -> 4.37 us  [the longest x1 1.6 us: row_body(): r_first[:, :3 * features].astype(F32)]
  transfers between devices with their start and end apart: 12 -> 7, of which waited for: 3 -> 6; matrix products, arithmetic and copies ran while one was open for 76% -> 5% of each run, Pallas kernels for 0% -> 24%
where the time goes in v1:
time: 651 us; the launch traced here: 649 us
  Pallas kernels  347 us (53%)
  waiting for transfers between devices  242 us (37%)
  local copies, waits for them, and re-layouts  21.1 us (3%)
  other arithmetic  19.9 us (3%)
  between operations  14.6 us (2%)
    ppermute x4, waiting for transfers between devices, swap(): return lax.ppermute(value, 'seq', [(0, 1), (1, 0)])  162 us
    pallas_call x1, Pallas kernels, attention_backward(): pl.pallas_call(backward_kernel, grid_spec=pltpu.PrefetchScalarGridSpec(nu...  125 us
    pallas_call x1, Pallas kernels, feed_forward(): pl.pallas_call(mlp_kernel, grid=(chunks, steps), in_specs=[pl.BlockSpec(b...  101 us
    pallas_call x1, Pallas kernels, attention_forward(): pl.pallas_call(forward_kernel, grid_spec=pltpu.PrefetchScalarGridSpec(num...  71.1 us
    unnamed x4, waiting for transfers between devices  57.6 us
    pallas_call x1, Pallas kernels, first_gradients(): pl.pallas_call(first_kernel, grid=(tokens // BT,), in_specs=[tall(feature...  26.8 us
    all_gather x1, waiting for transfers between devices, row_body(): weights = lax.all_gather(packed, both, axis=0, tiled=True)  22.5 us
    pallas_call x1, Pallas kernels, project_qkv(): pl.pallas_call(qkv_kernel, grid=(tokens // BT,), in_specs=[tall(features)...  16.8 us
  transfers between devices with their start and end apart: 7, of which 6 were waited for; matrix products, arithmetic and copies ran while one was open for 5% of the time, Pallas kernels for 24%

profile of v1, /device:TPU:0, one launch (start us, length us, event | category | flops | bytes accessed | tf_op | source)
XLA Modules:
  0.0 649.3 jit_solution(12538799777635784229)
XLA Ops:
  9.9 2.6 pack_weights.1
  12.6 3.4 dynamic-slice_bitcast_fusion.3
  16.0 3.0 collective-permute-start
  22.9 41.2 %collective-permute-done = bf16[1024,768]{1,0:T(8,128)(2,1)} collective-permute-done((bf16[1024,768]{1,0:T(8,128)(2,1)}, bf16[1024,768]{1,0:T(8,128)(2,1)}, u32[]{:S(2)}, u32[]{:S(2)}) %collective-permute-start) | collective-permute-done | bytes 1572896 | tf_op jit(solution)/shard_map/ppermute | solution.py:681
  64.1 3.3 pad_maximum_fusion.x_ref
  67.4 48.9 %collective-permute-done.1 = bf16[1024,768]{1,0:T(8,128)(2,1)} collective-permute-done((bf16[1024,768]{1,0:T(8,128)(2,1)}, bf16[1024,768]{1,0:T(8,128)(2,1)}, u32[]{:S(2)}, u32[]{:S(2)}) %collective-permute-start.1) | collective-permute-done | bytes 1572896 | tf_op jit(solution)/shard_map/ppermute | solution.py:681
  116.2 3.3 pad_maximum_fusion.1.dy_ref
  119.5 22.5 %all-gather.2.cloned.1.call-done.gain_ref.wq_ref.wk_ref.wv_ref.wo_ref.wu_ref.wd_ref = bf16[768,9344]{1,0:T(8,128)(2,1)} async-done(((bf16[24,9344]{1,0:T(8,128)(2,1)}), bf16[768,9344]{1,0:T(8,128)(2,1)}) %all-gather.2.cloned.1.call-update) | async-done | bytes 14352400 | tf_op jit(solution)/shard_map/all_gather | solution.py:702
  142.0 16.8 %project_qkv.1 = (bf16[2048,1536]{1,0:T(8,128)(2,1)}, bf16[2048,1536]{1,0:T(8,128)(2,1)}, bf16[2048,1536]{1,0:T(8,128)(2,1)}, bf16[768,2048]{1,0:T(8,128)(2,1)S(...) custom-call(bf16[2048,768]{1,0:T(8,128)(2,1)} %pad_maximum_fusion.x_ref, ...), custom_call_target="tpu_custom_call" | custom-call | tf_op jit(solution)/shard_map/project_qkv/pallas_call | solution.py:162
  158.8 1.7 copy-done.2
  163.6 71.1 %attention_forward.1 = (bf16[2048,768]{1,0:T(8,128)(2,1)}, f32[2048,768]{1,0:T(8,128)}, bf16[36,12,256,256]{3,2,1,0:T(8,128)(2,1)}) custom-call(s32[7,36]{1,0:T(8,128)} %stack.79.tab, bf16[2048,1536]{1,0:T(8,128)(2,1)} %get-tuple-element.31.q_ref, bf16[2048,1536]{1,0:T(8,128)(2,1)} %get-tuple-element.32.k_ref.k_any, ...), custom_call_target="tpu_custom_call" | custom-call | tf_op jit(solution)/shard_map/attention_forward/pallas_call | solution.py:287
  234.7 101.3 %feed_forward.1 = (bf16[2048,768]{1,0:T(8,128)(2,1)}, f32[2048,768]{1,0:T(8,128)}, bf16[2048,1536]{1,0:T(8,128)(2,1)}, bf16[768,2048]{1,0:T(8,128)(2,1)}, bf16[768,7040]{1,0:T(8,128)(2,1)}) custom-call(bf16[2048,768]{1,0:T(8,128)(2,1)} %pad_maximum_fusion.x_ref, bf16[2048,768]{1,0:T(8,128)(2,1)} %get-tuple-element.34.ob_ref, ...), custom_call_target="tpu_custom_call" | custom-call | tf_op jit(solution)/shard_map/feed_forward/pallas_call | solution.py:564
  338.2 125.3 %attention_backward.1.dqkv_ref = bf16[2048,2304]{1,0:T(8,128)(2,1)} custom-call(s32[7,36]{1,0:T(8,128)} %stack.90.tab, bf16[36,12,256,256]{3,2,1,0:T(8,128)(2,1)} %get-tuple-element.38.e_ref, bf16[2048,1536]{1,0:T(8,128)(2,1)} %get-tuple-element.31.q_ref, bf16[2048,1536]{1,0:T(8,128)(2,1)} %get-tuple-element.32.k_ref.k_any, ...), custom_call_target="tpu_custom_call" | custom-call | tf_op jit(solution)/shard_map/attention_backward/pallas_call | solution.py:385
  463.5 26.8 %first_gradients.1 = (f32[2048,768]{1,0:T(8,128)}, bf16[2048,768]{1,0:T(8,128)(2,1)}, bf16[768,2432]{1,0:T(8,128)(2,1)}) custom-call(bf16[2048,768]{1,0:T(8,128)(2,1)} %pad_maximum_fusion.x_ref, bf16[2048,2304]{1,0:T(8,128)(2,1)} %attention_backward.1.dqkv_ref, f32[2048,768]{1,0:T(8,128)} %get-tuple-element.42.dx_ref, f32[8,768]{1,0:T(8,128)} %copy-done.3, ...), custom_call_target="tpu_custom_call" | custom-call | tf_op jit(solution)/shard_map/first_gradients/pallas_call | solution.py:652
  490.3 1.7 slice.40
  495.5 2.1 slice_bitcast_fusion
  497.6 39.5 %collective-permute-done.3 = bf16[1024,768]{1,0:T(8,128)(2,1)} collective-permute-done((bf16[1024,768]{1,0:T(8,128)(2,1)S(1)}, bf16[1024,768]{1,0:T(8,128)(2,1)}, u32[]{:S(2)}, u32[]{:S(2)}) %collective-permute-start.3) | collective-permute-done | bytes 1572896 | tf_op jit(solution)/shard_map/ppermute | solution.py:681
  537.0 1.6 bitcast_convert_fusion
  538.7 2.9 maximum_select_fusion
  541.6 32.5 %collective-permute-done.2 = bf16[1024,768]{1,0:T(8,128)(2,1)} collective-permute-done((bf16[1024,768]{1,0:T(8,128)(2,1)}, bf16[1024,768]{1,0:T(8,128)(2,1)}, u32[]{:S(2)}, u32[]{:S(2)}) %collective-permute-start.2) | collective-permute-done | bytes 1572896 | tf_op jit(solution)/shard_map/ppermute | solution.py:681
  574.1 3.8 maximum_select_fusion.1
  577.9 3.0 unpack_gradients.1
  582.2 57.6 %all-reduce.4.cloned.1.call-done = bf16[768,2432]{1,0:T(8,128)(2,1)} async-done(((bf16[768,2432]{1,0:T(8,128)(2,1)}), bf16[768,2432]{1,0:T(8,128)(2,1)}) %all-reduce.4.cloned.1.call-update) | async-done | bytes 3735568
  639.8 1.6 dynamic-slice_convert_fusion
  (67 shorter events, 17.4 us)
Async XLA Ops:
  7.2 13.2 %copy-start = (s32[2,2048]{1,0:T(2,128)S(1)}, s32[2,2048]{1,0:T(2,128)}, u32[]{:S(2)}) copy-start(s32[2,2048]{1,0:T(2,128)} %param.14) | copy-start | bytes 49156
  7.2 134.9 %all-gather.2.cloned.1.call-start = ((), (), s32[]{:S(2)}) async-start(), calls=%async_computation.1 | async-start | bytes 14800896 | tf_op jit(solution)/shard_map/all_gather | solution.py:702
  12.5 482.9 %reduce-scatter.4.cloned.1.call-start = ((), (), s32[]{:S(2)}) async-start(), calls=%async_computation.3 | async-start | bytes 11151360
  12.6 6.4 copy-start.5
  16.0 6.0 copy-start.7
  16.0 6.9 %copy-start.10 = (s32[36]{0:T(128)S(1)}, s32[36]{0:T(128)}, u32[]{:S(2)}) copy-start(s32[36]{0:T(128)} %constant.116.clone) | copy-start | bytes 436
  16.0 6.9 %copy-start.11 = (s32[36]{0:T(128)S(1)}, s32[36]{0:T(128)}, u32[]{:S(2)}) copy-start(s32[36]{0:T(128)} %constant.115.clone) | copy-start | bytes 436
  16.0 48.1 %collective-permute-start = (bf16[1024,768]{1,0:T(8,128)(2,1)}, bf16[1024,768]{1,0:T(8,128)(2,1)}, u32[]{:S(2)}, u32[]{:S(2)}) collective-permute-start(bf16[1024,768]{1,0:T(8,128)(2,1)} %get-tuple-element.57), channel_id=1, source_target_pairs={{0,1},{1,0},{2,3},{3,2},{4,5},{5,4},{6,7},{7,6},{8,9},{9,8},{10,11... | collective-permute-start | bytes 4718600 | tf_op jit(solution)/shard_map/ppermute | solution.py:681
  20.3 95.9 %collective-permute-start.1 = (bf16[1024,768]{1,0:T(8,128)(2,1)}, bf16[1024,768]{1,0:T(8,128)(2,1)}, u32[]{:S(2)}, u32[]{:S(2)}) collective-permute-start(bf16[1024,768]{1,0:T(8,128)(2,1)} %get-tuple-element.55), channel_id=1, source_target_pairs={{0,1},{1,0},{2,3},{3,2},{4,5},{5,4},{6,7},{7,6},{8,9},{9,8},{10,11... | collective-permute-start | bytes 4718600 | tf_op jit(solution)/shard_map/ppermute | solution.py:681
  119.5 42.9 %copy-start.15 = (s32[1,36]{1,0:T(1,128)S(1)}, s32[1,36]{1,0:T(1,128)}, u32[]{:S(2)}) copy-start(s32[1,36]{1,0:T(1,128)} %constant.156) | copy-start | bytes 436
  119.5 42.9 %copy-start.16 = (s32[1,36]{1,0:T(1,128)S(1)}, s32[1,36]{1,0:T(1,128)}, u32[]{:S(2)}) copy-start(s32[1,36]{1,0:T(1,128)} %constant.137) | copy-start | bytes 436
  119.5 42.9 %copy-start.17 = (s32[1,36]{1,0:T(1,128)S(1)}, s32[1,36]{1,0:T(1,128)}, u32[]{:S(2)}) copy-start(s32[1,36]{1,0:T(1,128)} %constant.136) | copy-start | bytes 436
  158.8 1.7 copy-start.2
  336.0 0.7 copy-start.6
  336.0 1.5 copy-start.8
  336.0 1.5 copy-start.9
  336.0 1.5 copy-start.12
  336.1 1.5 copy-start.13
  336.1 1.5 copy-start.14
  336.1 303.7 %all-reduce.4.cloned.1.call-start = ((), (), s32[]{:S(2)}) async-start(), calls=%async_computation.2 | async-start | bytes 7471104
  490.3 2.4 copy-start.4
  492.0 45.0 %collective-permute-start.3 = (bf16[1024,768]{1,0:T(8,128)(2,1)S(1)}, bf16[1024,768]{1,0:T(8,128)(2,1)}, u32[]{:S(2)}, u32[]{:S(2)}) collective-permute-start(bf16[1024,768]{1,0:T(8,128)(2,1)S(1)} %slice.40), channel_id=1, source_target_pairs={{0,1},{1,0},{2,3},{3,2},{4,5},{5,4},{6,7},{7,6},{8,9},{9,8},{10,11... | collective-permute-start | bytes 4718600 | tf_op jit(solution)/shard_map/ppermute | solution.py:681
  494.0 80.1 %collective-permute-start.2 = (bf16[1024,768]{1,0:T(8,128)(2,1)}, bf16[1024,768]{1,0:T(8,128)(2,1)}, u32[]{:S(2)}, u32[]{:S(2)}) collective-permute-start(bf16[1024,768]{1,0:T(8,128)(2,1)} %get-tuple-element.53), channel_id=1, source_target_pairs={{0,1},{1,0},{2,3},{3,2},{4,5},{5,4},{6,7},{7,6},{8,9},{9,8},{10,11... | collective-permute-start | bytes 4718600 | tf_op jit(solution)/shard_map/ppermute | solution.py:681
  574.1 68.7 %copy-start.1 = (s32[2,2048]{1,0:T(2,128)S(1)}, s32[2,2048]{1,0:T(2,128)}, u32[]{:S(2)}) copy-start(s32[2,2048]{1,0:T(2,128)} %param.14) | copy-start | bytes 49156
  (1 other events, 0.6 us)
Sparse Core Ops, SparseCore 0:
  12.6 129.3 all-gather.1
  336.2 141.5 reduce-scatter.3
  495.6 144.1 all-reduce.3

commit v2 on v1

--- a/solution.py
+++ b/solution.py
@@ -52,31 +52,31 @@
     return (iota((piece, 4 * piece), 1) == 4 * iota((piece, 4 * piece), 0) + c).astype(F32).astype(BF)
 
 
-def pack_kernel(qkv_ref, out_ref, up_ref, down_ref, ga_ref, gm_ref, o_ref):
+def pack_kernel(qkv_ref, out_ref, up_ref, down_ref, ga_ref, gm_ref, a_ref, b_ref, l_ref):
     piece, features = out_ref.shape
     lane = iota((piece, 128), 1)
-    col = 3 * features
-    o_ref[:, :col] = qkv_ref[...].astype(BF)
-    o_ref[:, col : col + features] = out_ref[...].astype(BF)
-    col += features
+    a_ref[...] = qkv_ref[:, : 2 * features].astype(BF)
+    b_ref[:, :features] = qkv_ref[:, 2 * features :].astype(BF)
+    gains = jnp.where(lane == 0, ga_ref[...], jnp.where(lane == 1, gm_ref[...], 0.0))
+    b_ref[:, features:] = gains.astype(BF)
+    l_ref[:, :features] = out_ref[...].astype(BF)
     for c in range(4):
         pick = pick_columns(c)
+        col = features * (1 + c)
         for tile in range(features // 128):
             part = up_ref[:, 512 * tile : 512 * tile + 512].astype(BF)
-            o_ref[:, col + 128 * tile : col + 128 * tile + 128] = dot(part, pick).astype(BF)
-        col += features
-    for c in range(4):
-        o_ref[:, col : col + features] = dot(pick_rows(piece, c), down_ref[...].astype(BF)).astype(BF)
-        col += features
-    gains = jnp.where(lane == 0, ga_ref[...], jnp.where(lane == 1, gm_ref[...], 0.0))
-    o_ref[:, col : col + 128] = gains.astype(BF)
+            l_ref[:, col + 128 * tile : col + 128 * tile + 128] = dot(part, pick).astype(BF)
+        col = features * (5 + c)
+        l_ref[:, col : col + features] = dot(pick_rows(piece, c), down_ref[...].astype(BF)).astype(BF)
 
 
 def pack(w_qkv, w_out, w_up, w_down, gain_attn, gain_mlp):
     piece, features = w_out.shape
     return pl.pallas_call(
         pack_kernel,
-        out_shape=jax.ShapeDtypeStruct((piece, 12 * features + 128), BF),
+        out_shape=[
+            jax.ShapeDtypeStruct((piece, cols), BF) for cols in (2 * features, features + 128, 9 * features)
+        ],
         name="pack_weights",
     )(w_qkv, w_out, w_up, w_down, gain_attn[:, None], gain_mlp[:, None])
 
@@ -120,15 +120,26 @@
     return shifted, lax.rsqrt(spread + EPSILON)
 
 
-def qkv_kernel(x_ref, gain_ref, wq_ref, wk_ref, wv_ref, q_ref, k_ref, v_ref, qt_ref, rows_ref, size_ref):
+def pick_half(own_ref, other_ref, step, steps):
+    return jnp.where(step < steps // 2, own_ref[...], other_ref[...])
+
+
+def halves(cols, steps):
+    return (
+        pl.BlockSpec((BT, cols), lambda t: (jnp.minimum(t, steps // 2 - 1), 0)),
+        pl.BlockSpec((BT, cols), lambda t: (jnp.maximum(t - steps // 2, 0), 0)),
+    )
+
+
+def qkv_kernel(x_ref, other_ref, w_ref, v_w_ref, q_ref, k_ref, v_ref, rows_ref, size_ref):
     features = x_ref.shape[1]
 
     @pl.when(pl.program_id(0) == 0)
     def _():
-        rows_ref[...] = gain_ref[...].astype(F32).T[:8]
+        rows_ref[...] = v_w_ref[:, features:].astype(F32).T[:8]
         size_ref[...] = jnp.zeros_like(size_ref)
 
-    shifted, scale = moments(x_ref[...].astype(F32))
+    shifted, scale = moments(pick_half(x_ref, other_ref, pl.program_id(0), pl.num_programs(0)).astype(F32))
     normed = (shifted * scale * rows_ref[0:1, :]).astype(BF)
     low = half_lanes(x_ref.shape[0])
     heads = (iota((features, 128), 0) // HD == iota((features, 128), 1)).astype(F32).astype(BF)
@@ -139,41 +150,37 @@
             ref[:, 256 * p : 256 * p + 128] = jnp.where(low, pair, other).astype(BF)
             ref[:, 256 * p + 128 : 256 * p + 256] = jnp.where(low, other, pair).astype(BF)
 
-    q = dot(normed, wq_ref[...]) * (LOG2E / math.sqrt(HD))
-    qt_ref[...] = q.astype(BF).T
+    def measure(row, value):
+        most = jnp.max(dot((value * value).astype(BF), heads), axis=0, keepdims=True)
+        size_ref[row : row + 1] = jnp.maximum(size_ref[row : row + 1], most)
+
+    q = dot(normed, w_ref[:, :features]) * (LOG2E / math.sqrt(HD))
     spread(q_ref, q, 0.0)
-    size_ref[0:1] = jnp.maximum(size_ref[0:1], jnp.max(dot((q * q).astype(BF), heads), axis=0, keepdims=True))
-    k = dot(normed, wk_ref[...])
+    measure(0, q)
+    k = dot(normed, w_ref[:, features:])
     spread(k_ref, k, 1.0)
-    size_ref[1:2] = jnp.maximum(size_ref[1:2], jnp.max(dot((k * k).astype(BF), heads), axis=0, keepdims=True))
-    spread(v_ref, dot(normed, wv_ref[...]), 1.0)
-
-
-def project_qkv(x, weights):
-    tokens, features = x.shape
-    last = weights.shape[1] // 128 - 1
-
-    def column(i):
-        return pl.BlockSpec((features, features), lambda t: (0, i))
+    measure(1, k)
+    spread(v_ref, dot(normed, v_w_ref[:, :features]), 1.0)
+
+
+def project_qkv(own, other, w_qk, w_v):
+    tokens, features = 2 * own.shape[0], own.shape[1]
+    steps = tokens // BT
 
     def tall(cols):
         return pl.BlockSpec((BT, cols), lambda t: (t, 0))
 
+    def whole(array):
+        return pl.BlockSpec(array.shape, lambda t: (0, 0))
+
     return pl.pallas_call(
         qkv_kernel,
-        grid=(tokens // BT,),
-        in_specs=[
-            tall(features),
-            pl.BlockSpec((features, 128), lambda t: (0, last)),
-            column(0),
-            column(1),
-            column(2),
-        ],
+        grid=(steps,),
+        in_specs=[*halves(features, steps), whole(w_qk), whole(w_v)],
         out_specs=[
             tall(2 * features),
             tall(2 * features),
             tall(2 * features),
-            pl.BlockSpec((features, BT), lambda t: (0, t)),
             pl.BlockSpec((8, features), lambda t: (0, 0)),
             pl.BlockSpec((8, 128), lambda t: (0, 0)),
         ],
@@ -181,22 +188,20 @@
             jax.ShapeDtypeStruct((tokens, 2 * features), BF),
             jax.ShapeDtypeStruct((tokens, 2 * features), BF),
             jax.ShapeDtypeStruct((tokens, 2 * features), BF),
-            jax.ShapeDtypeStruct((features, tokens), BF),
             jax.ShapeDtypeStruct((8, features), F32),
             jax.ShapeDtypeStruct((8, 128), F32),
         ],
         compiler_params=pltpu.CompilerParams(vmem_limit_bytes=48 * MIB),
         name="project_qkv",
-    )(x, weights, weights, weights, weights)
-
-
-def selection(scores, segq, segk, ib, jb):
-    rows = iota((B, B), 0) + ib * B
-    cols = iota((B, B), 1) + jb * B
-    same = segq == segk
-    x = scores - OFFSET * LOG2E
-    soft = jnp.maximum(x, 0.0) + jnp.log2(1.0 + jnp.exp2(-jnp.abs(x)))
-    return jnp.where(same & (cols < rows), soft, 0.0), same & (cols <= rows)
+    )(own, other, w_qk, w_v)
+
+
+def pick(h):
+    return slice(128 * h, 128 * h + 128)
+
+
+def block_rows(index):
+    return pl.ds(pl.multiple_of(index * B, B), B)
 
 
 def two_part(tri, values):
@@ -205,41 +210,115 @@
     return dot(tri, high) + dot(tri, rest)
 
 
-def forward_kernel(tab, q_ref, k_ref, v_ref, segq_ref, segk_ref, k_any, seg_any, o_ref, li_ref, e_ref,
-                   acc, carry, tri, qx, kbuf, segbuf, sem):
+def selection(scores, segq, segk, rows, cols):
+    earlier = (segq == segk) & (cols < rows)
+    x = scores - OFFSET * LOG2E
+    grown = jnp.exp2(jnp.minimum(x, 100.0))
+    more = 1.0 + grown
+    return jnp.where(earlier, jnp.maximum(x, jnp.log2(more)), 0.0), jnp.where(earlier, grown / more, 0.0)
+
+
+def mixed(first, second):
+    done = 0
+    for n, step in enumerate(first):
+        step()
+        upto = (n + 1) * len(second) // len(first)
+        for other in second[done:upto]:
+            other()
+        done = upto
+
+
+STRIP = 64
+
+
+def key_copies(block, stored, k_any, v_any, kx, vx, sem):
+    rows = block_rows(stored)
+    return (
+        pltpu.make_async_copy(k_any.at[rows, :], kx.at[block], sem.at[0, block]),
+        pltpu.make_async_copy(v_any.at[rows, :], vx.at[block], sem.at[1, block]),
+    )
+
+
+def forward_kernel(tab, slow, q_ref, q0_ref, k0_ref, segq_ref, segk_ref, k_any, v_any, o_ref, li_ref, e_ref,
+                   acc, carry, tri, qx, penalty, gate, work, high, kx, vx, sem):
     t = pl.program_id(0)
-    ib, jb = tab[3, t], tab[4, t]
+    ib, jb = tab[2, t], tab[3, t]
+
+    @pl.when(t == 0)
+    def _():
+        for block in range(kx.shape[0]):
+            for copy in key_copies(block, tab[1, block * (block + 3) // 2], k_any, v_any, kx, vx, sem):
+                copy.start()
+
+    def prepare(step, slot):
+        keys = block_rows(tab[1, step])
+        at = tab[3, step]
+        ahead = (tab[2, step] - at) * B
+        segk = segk_ref[tab[1, step], 0:1, :]
+        sums = []
+
+        def scores():
+            work[...] = dot_nt(q0_ref[block_rows(tab[0, step]), :], k0_ref[keys, :])
+
+        def strip(n):
+            part = slice(STRIP * n, STRIP * n + STRIP)
+            segq = segq_ref[pl.ds(pl.multiple_of(tab[0, step] * B + STRIP * n, STRIP), STRIP), :]
+            return part, segq, iota((STRIP, B), 0) + (ahead + STRIP * n), iota((STRIP, B), 1)
+
+        def choose(n):
+            part, segq, rows, cols = strip(n)
+            chosen, opened = selection(work[part, :], segq, segk, rows, cols)
+            gate[slot, part, :] = opened.astype(BF)
+            high[part, :] = chosen.astype(BF)
+            sums.append(jnp.sum(chosen, axis=0, keepdims=True))
+
+        def add():
+            before = carry[at, 0:1, :]
+            work[...] = dot(tri[...], high[...]) + before
+            carry[at, 0:1, :] = before + sum(sums[1:], sums[0])
+
+        def close(n):
+            part, segq, rows, cols = strip(n)
+            penalty[slot, part, :] = jnp.where((segq == segk) & (cols <= rows), work[part, :], BIG)
+
+        count = range(B // STRIP)
+        return [scores] + [partial(choose, n) for n in count] + [add] + [partial(close, n) for n in count]
 
     @pl.when(t == 0)
     def _():
         carry[...] = jnp.zeros_like(carry)
         tri[...] = (iota((B, B), 1) < iota((B, B), 0)).astype(F32).astype(BF)
+        for step in prepare(0, 0):
+            step()
 
     @pl.when(jb == 0)
     def _():
         acc[...] = jnp.zeros_like(acc)
         qx[...] = q_ref[...]
-
-        @pl.when(tab[6, t] != 0)
+        for copy in key_copies(ib, tab[0, t], k_any, v_any, kx, vx, sem):
+            copy.wait()
+
+        @pl.when(slow[0] != 0)
         def _():
             lane = iota((B, 128), 1)
+            segq = segq_ref[block_rows(tab[0, t]), :]
+            cols = iota((B, B), 1)
+
+            def chosen(other):
+                rows = iota((B, B), 0) + (ib - other) * B
+                base = tab[1, t + other]
+                first = dot_nt(q_ref[:, 0:128], k0_ref[block_rows(base), :])
+                return selection(first, segq, segk_ref[base, 0:1, :], rows, cols)[0]
+
+            own = jnp.sum(chosen(0), axis=0, keepdims=True)
 
             def step(other, top):
                 base = tab[1, t + other]
-                copies = (
-                    pltpu.make_async_copy(k_any.at[pl.ds(pl.multiple_of(base * B, B), B), :], kbuf, sem.at[0]),
-                    pltpu.make_async_copy(seg_any.at[base], segbuf, sem.at[1]),
-                )
-                for copy in copies:
-                    copy.start()
-                for copy in copies:
-                    copy.wait()
-                first = dot_nt(q_ref[:, 0:128], kbuf[:, 0:128])
-                chosen, kept = selection(first, segq_ref[...], segbuf[0:1, :], ib, other)
-                penalty = jnp.where(kept, two_part(tri[...], chosen) + carry[other, 0:1, :], BIG)
+                before = carry[other, 0:1, :] - jnp.where(other == 0, own, 0.0)
+                kept = (segq == segk_ref[base, 0:1, :]) & (cols <= iota((B, B), 0) + (ib - other) * B)
+                z_penalty = jnp.where(kept, dot(tri[...], chosen(other).astype(BF)) + before, BIG)
                 for h in range(H):
-                    w = slice(128 * h, 128 * h + 128)
-                    z = dot_nt(q_ref[:, w], kbuf[:, w]) - penalty
+                    z = dot_nt(q_ref[:, pick(h)], kx[other, :, pick(h)]) - z_penalty
                     top = jnp.where(lane == h, jnp.maximum(top, jnp.max(z, axis=1, keepdims=True)), top)
                 return top
 
@@ -251,198 +330,247 @@
                 three = shift - one - two
                 at = lane - (HD if h % 2 == 0 else 0)
                 extra = jnp.where(at == 0, one, jnp.where(at == 1, two, jnp.where(at == 2, three, 0.0)))
-                w = slice(128 * h, 128 * h + 128)
                 keep = (lane < HD) if h % 2 == 0 else (lane >= HD)
-                qx[:, w] = jnp.where(keep, q_ref[:, w].astype(F32), extra).astype(BF)
-
-    @pl.when(tab[2, t] != 0)
-    def _():
-        first = dot_nt(q_ref[:, 0:128], k_ref[:, 0:128])
-        chosen, kept = selection(first, segq_ref[...], segk_ref[0, 0:1, :], ib, jb)
-        penalty = jnp.where(kept, two_part(tri[...], chosen) + carry[jb, 0:1, :], BIG)
-        carry[jb, 0:1, :] = carry[jb, 0:1, :] + jnp.sum(chosen, axis=0, keepdims=True)
-        for h in range(H):
-            w = slice(128 * h, 128 * h + 128)
-            e = jnp.exp2(dot_nt(qx[:, w], k_ref[:, w]) - penalty).astype(BF)
-            e_ref[0, h] = e
-            acc[:, w] += dot(e, v_ref[:, w])
+                qx[:, pick(h)] = jnp.where(keep, q_ref[:, pick(h)].astype(F32), extra).astype(BF)
+
+    slot = t % 2
+
+    def head(h):
+        e = jnp.exp2(dot_nt(qx[:, pick(h)], kx[jb, :, pick(h)]) - penalty[slot]).astype(BF)
+        e_ref[0, h] = e
+        acc[:, pick(h)] += dot(e, vx[jb, :, pick(h)])
+
+    e_ref[0, H] = gate[slot]
+    mixed([partial(head, h) for h in range(H)], prepare(t + 1, 1 - slot))
 
     @pl.when(jb == ib)
     def _():
         low = half_lanes(B)
         for p in range(H // 2):
-            one = acc[:, 256 * p : 256 * p + 128]
-            two = acc[:, 256 * p + 128 : 256 * p + 256]
+            one = acc[:, pick(2 * p)]
+            two = acc[:, pick(2 * p + 1)]
             inverse = 1.0 / pltpu.roll(jnp.where(low, two, one), HD, 1)
-            o_ref[:, 128 * p : 128 * p + 128] = (jnp.where(low, one, two) * inverse).astype(BF)
-            li_ref[:, 128 * p : 128 * p + 128] = inverse
-
-
-def attention_forward(table, q, k, v, seg_col, seg_row):
+            o_ref[:, pick(p)] = (jnp.where(low, one, two) * inverse).astype(BF)
+            li_ref[:, pick(p)] = inverse
+
+
+def attention_forward(table, slow, q, k, v, seg_col, seg_row):
     tokens = q.shape[0]
     blocks = tokens // B
-    tiles = table.shape[1]
+    tiles = table.shape[1] - 1
     wide = 128 * H
     narrow = HD * H
+    once = pl.Buffered(1)
     return pl.pallas_call(
         forward_kernel,
         grid_spec=pltpu.PrefetchScalarGridSpec(
-            num_scalar_prefetch=1,
+            num_scalar_prefetch=2,
             grid=(tiles,),
             in_specs=[
-                pl.BlockSpec((B, wide), lambda t, tab: (tab[0, t], 0)),
-                pl.BlockSpec((B, wide), lambda t, tab: (tab[1, t], 0)),
-                pl.BlockSpec((B, wide), lambda t, tab: (tab[1, t], 0)),
-                pl.BlockSpec((B, 1), lambda t, tab: (tab[0, t], 0)),
-                pl.BlockSpec((1, 8, B), lambda t, tab: (tab[1, t], 0, 0)),
+                pl.BlockSpec((B, wide), lambda t, tab, slow: (tab[0, t], 0)),
+                pl.BlockSpec((tokens, 128), lambda t, tab, slow: (0, 0), pipeline_mode=once),
+                pl.BlockSpec((tokens, 128), lambda t, tab, slow: (0, 0), pipeline_mode=once),
+                pl.BlockSpec((tokens, 1), lambda t, tab, slow: (0, 0), pipeline_mode=once),
+                pl.BlockSpec((blocks, 8, B), lambda t, tab, slow: (0, 0, 0), pipeline_mode=once),
                 pl.BlockSpec(memory_space=pl.ANY),
                 pl.BlockSpec(memory_space=pl.ANY),
             ],
             out_specs=[
-                pl.BlockSpec((B, narrow), lambda t, tab: (tab[0, t], 0)),
-                pl.BlockSpec((B, narrow), lambda t, tab: (tab[0, t], 0)),
-                pl.BlockSpec((1, H, B, B), lambda t, tab: (tab[5, t], 0, 0, 0)),
+                pl.BlockSpec((B, narrow), lambda t, tab, slow: (tab[0, t], 0)),
+                pl.BlockSpec((B, narrow), lambda t, tab, slow: (tab[0, t], 0)),
+                pl.BlockSpec((1, H + 1, B, B), lambda t, tab, slow: (tab[4, t], 0, 0, 0)),
             ],
             scratch_shapes=[
                 pltpu.VMEM((B, wide), F32),
                 pltpu.VMEM((blocks, 8, B), F32),
                 pltpu.VMEM((B, B), BF),
                 pltpu.VMEM((B, wide), BF),
-                pltpu.VMEM((B, wide), BF),
-                pltpu.VMEM((8, B), jnp.int32),
-                pltpu.SemaphoreType.DMA((2,)),
+                pltpu.VMEM((2, B, B), F32),
+                pltpu.VMEM((2, B, B), BF),
+                pltpu.VMEM((B, B), F32),
+                pltpu.VMEM((B, B), BF),
+                pltpu.VMEM((blocks, B, wide), BF),
+                pltpu.VMEM((blocks, B, wide), BF),
+                pltpu.SemaphoreType.DMA((2, blocks)),
             ],
         ),
         out_shape=[
             jax.ShapeDtypeStruct((tokens, narrow), BF),
             jax.ShapeDtypeStruct((tokens, narrow), F32),
-            jax.ShapeDtypeStruct((tiles, H, B, B), BF),
+            jax.ShapeDtypeStruct((tiles, H + 1, B, B), BF),
         ],
-        compiler_params=pltpu.CompilerParams(vmem_limit_bytes=56 * MIB),
+        compiler_params=pltpu.CompilerParams(vmem_limit_bytes=48 * MIB),
         name="attention_forward",
-    )(table, q, k, v, seg_col, seg_row, k, seg_row)
-
-
-def backward_kernel(tab, e_ref, q_ref, k_ref, v_ref, d_ref, qt_ref, dt_ref, segq_ref, segk_ref, o_ref,
-                    dq, dkt, dvt, carry, tri):
+    )(table, slow, q, q, k, seg_col, seg_row, k, v)
+
+
+def backward_kernel(tab, e_ref, q_ref, d_ref, q0_ref, k0_ref, k_any, v_any, o_ref,
+                    dq, dkt, dvt, carry, tri, sums, first, gate, work, kx, vx, sem):
     t = pl.program_id(0)
-    ib, jb = tab[3, t], tab[4, t]
+    last = pl.num_programs(0) - 1
+    before = jnp.maximum(t - 1, 0)
     narrow = HD * H
+    low = half_lanes(B)
+    slot = t % 2
 
     @pl.when(t == 0)
     def _():
+        for block in range(kx.shape[0]):
+            for copy in key_copies(block, tab[1, block], k_any, v_any, kx, vx, sem):
+                copy.start()
         carry[...] = jnp.zeros_like(carry)
         tri[...] = (iota((B, B), 1) > iota((B, B), 0)).astype(F32).astype(BF)
         dkt[...] = jnp.zeros_like(dkt)
         dvt[...] = jnp.zeros_like(dvt)
-
-    @pl.when(jb == 0)
-    def _():
         dq[...] = jnp.zeros_like(dq)
-
-    @pl.when(tab[2, t] != 0)
-    def _():
-        low = half_lanes(B)
-        cols = pl.ds(pl.multiple_of(jb * B, B), B)
-        total = None
+        sums[...] = jnp.zeros_like(sums)
+        first[...] = jnp.zeros_like(first)
+        gate[...] = jnp.zeros_like(gate)
+
+    @pl.when((tab[3, t] == 0) & (t < last))
+    def _():
+        dq[tab[2, t] % 2] = jnp.zeros(dq.shape[1:], F32)
+
+    @pl.when(t < kx.shape[0])
+    def _():
+        for copy in key_copies(t, tab[1, t], k_any, v_any, kx, vx, sem):
+            copy.wait()
+
+    def finish():
+        at = tab[3, before]
+
+        def add():
+            total = sums[1 - slot]
+            later = carry[at, 0:1, :] + two_part(tri[...], total)
+            carry[at, 0:1, :] = carry[at, 0:1, :] + jnp.sum(total, axis=0, keepdims=True)
+            work[...] = (first[1 - slot] - later * gate[1 - slot].astype(F32)).astype(BF)
+
+        def keys():
+            dkt[:HD, block_rows(at)] += dot_tn(q0_ref[block_rows(tab[0, before]), :], work[...])[:HD]
+
+        def queries():
+            more = dot(work[...], k0_ref[block_rows(tab[1, before]), :])
+            dq[tab[2, before] % 2, :, :128] += jnp.where(low, more, 0.0)
+
+        return [add, keys, queries]
+
+    @pl.when(t == last)
+    def _():
+        for step in finish():
+            step()
+
+    @pl.when(t < last)
+    def _():
+        cols = block_rows(tab[3, t])
+        turn = tab[2, t] % 2
+        kept = {}
         parts = {}
-        for h in list(range(1, H)) + [0]:
-            w = slice(128 * h, 128 * h + 128)
+
+        def score(h):
+            e = e_ref[0, h]
+            dz = e.astype(F32) * dot_nt(d_ref[:, pick(h)], vx[tab[3, t], :, pick(h)])
+            if h == 0:
+                first[slot] = dz
+                sums[slot] = dz
+            else:
+                sums[slot] += dz
+                kept[h] = dz.astype(BF)
+
+        def products(h):
             own = slice(HD * h, HD * h + HD)
-            e = e_ref[0, h]
-            dz = e.astype(F32) * dot_nt(d_ref[:, w], v_ref[:, w])
-            total = dz if total is None else total + dz
-            dvt[own, cols] += dot(dt_ref[own, :], e)
+            data = slice(HD * (h % 2), HD * (h % 2) + HD)
+            dvt[own, cols] += dot_tn(d_ref[:, pick(h)], e_ref[0, h])[data]
             if h == 0:
-                gate = jax.nn.sigmoid(dot_nt(q_ref[:, w], k_ref[:, w]) * (1.0 / LOG2E) - OFFSET)
-                rows = iota((B, B), 0) + ib * B
-                keys = iota((B, B), 1) + jb * B
-                kept = (segq_ref[...] == segk_ref[0, 0:1, :]) & (keys < rows)
-                later = carry[jb, 0:1, :] + two_part(tri[...], total)
-                carry[jb, 0:1, :] = carry[jb, 0:1, :] + jnp.sum(total, axis=0, keepdims=True)
-                dz = dz - jnp.where(kept, later * gate, 0.0)
-            ds = dz.astype(BF)
-            dkt[own, cols] += dot(qt_ref[own, :], ds)
-            parts[h] = dot(ds, k_ref[:, w])
-            if h ^ 1 in parts:
-                p = h // 2
-                dq[:, 128 * p : 128 * p + 128] += jnp.where(low, parts[2 * p], parts[2 * p + 1])
-
-    @pl.when(jb == ib)
-    def _():
-        cols = pl.ds(pl.multiple_of(ib * B, B), B)
-        o_ref[:, :narrow] = (dq[...] * (1.0 / math.sqrt(HD))).astype(BF)
+                parts[0] = 0.0
+                return
+            ds = kept.pop(h)
+            dkt[own, cols] += dot_tn(q_ref[:, pick(h)], ds)[data]
+            parts[h] = dot(ds, kx[tab[3, t], :, pick(h)])
+            if h % 2:
+                dq[turn, :, pick(h // 2)] += jnp.where(low, parts.pop(h - 1), parts.pop(h))
+
+        gate[slot] = e_ref[0, H]
+        steps = [partial(score, 0)]
+        for h in range(H):
+            if h + 1 < H:
+                steps.append(partial(score, h + 1))
+            steps.append(partial(products, h))
+        mixed(steps, finish())
+
+    @pl.when((t > 0) & (tab[3, before] == tab[2, before]))
+    def _():
+        cols = block_rows(tab[2, before])
+        o_ref[:, :narrow] = (dq[tab[2, before] % 2] * (1.0 / math.sqrt(HD))).astype(BF)
         o_ref[:, narrow : 2 * narrow] = (dkt[:, cols] * (1.0 / LOG2E)).astype(BF).T
         o_ref[:, 2 * narrow :] = dvt[:, cols].astype(BF).T
 
 
-def attention_backward(table, e, q, k, v, d, qt, dt, seg_col, seg_row):
+def attention_backward(table, e, q, k, v, d):
     tokens = q.shape[0]
     blocks = tokens // B
-    tiles = table.shape[1]
+    tiles = table.shape[1] - 1
     wide = 128 * H
     narrow = HD * H
+    once = pl.Buffered(1)
     return pl.pallas_call(
         backward_kernel,
         grid_spec=pltpu.PrefetchScalarGridSpec(
             num_scalar_prefetch=1,
-            grid=(tiles,),
+            grid=(tiles + 1,),
             in_specs=[
-                pl.BlockSpec((1, H, B, B), lambda t, tab: (tab[5, t], 0, 0, 0)),
+                pl.BlockSpec((1, H + 1, B, B), lambda t, tab: (tab[4, t], 0, 0, 0)),
                 pl.BlockSpec((B, wide), lambda t, tab: (tab[0, t], 0)),
-                pl.BlockSpec((B, wide), lambda t, tab: (tab[1, t], 0)),
-                pl.BlockSpec((B, wide), lambda t, tab: (tab[1, t], 0)),
                 pl.BlockSpec((B, wide), lambda t, tab: (tab[0, t], 0)),
-                pl.BlockSpec((narrow, B), lambda t, tab: (0, tab[0, t])),
-                pl.BlockSpec((narrow, B), lambda t, tab: (0, tab[0, t])),
-                pl.BlockSpec((B, 1), lambda t, tab: (tab[0, t], 0)),
-                pl.BlockSpec((1, 8, B), lambda t, tab: (tab[1, t], 0, 0)),
+                pl.BlockSpec((tokens, 128), lambda t, tab: (0, 0), pipeline_mode=once),
+                pl.BlockSpec((tokens, 128), lambda t, tab: (0, 0), pipeline_mode=once),
+                pl.BlockSpec(memory_space=pl.ANY),
+                pl.BlockSpec(memory_space=pl.ANY),
             ],
-            out_specs=pl.BlockSpec((B, 3 * narrow), lambda t, tab: (tab[0, t], 0)),
+            out_specs=pl.BlockSpec((B, 3 * narrow), lambda t, tab: (tab[0, jnp.maximum(t - 1, 0)], 0)),
             scratch_shapes=[
-                pltpu.VMEM((B, narrow), F32),
+                pltpu.VMEM((2, B, narrow), F32),
                 pltpu.VMEM((narrow, tokens), F32),
                 pltpu.VMEM((narrow, tokens), F32),
                 pltpu.VMEM((blocks, 8, B), F32),
                 pltpu.VMEM((B, B), BF),
+                pltpu.VMEM((2, B, B), F32),
+                pltpu.VMEM((2, B, B), F32),
+                pltpu.VMEM((2, B, B), BF),
+                pltpu.VMEM((B, B), BF),
+                pltpu.VMEM((blocks, B, wide), BF),
+                pltpu.VMEM((blocks, B, wide), BF),
+                pltpu.SemaphoreType.DMA((2, blocks)),
             ],
         ),
         out_shape=jax.ShapeDtypeStruct((tokens, 3 * narrow), BF),
-        compiler_params=pltpu.CompilerParams(vmem_limit_bytes=60 * MIB),
+        compiler_params=pltpu.CompilerParams(vmem_limit_bytes=56 * MIB),
+        cost_estimate=pl.CostEstimate(flops=tiles * H * B * B * 1024, bytes_accessed=tiles * B * B, transcendentals=0),
         name="attention_backward",
-    )(table, e, q, k, v, d, qt, dt, seg_col, seg_row)
-
-
-def tile_tables(segments, first, slow):
-    blocks = segments.shape[0] // B
-    ib = jnp.array([i for i in range(blocks) for j in range(i + 1)], jnp.int32)
-    jb = jnp.array([j for i in range(blocks) for j in range(i + 1)], jnp.int32)
-    back_ib = jnp.array([i for i in reversed(range(blocks)) for j in range(i + 1)], jnp.int32)
-    back_jb = jnp.array([j for i in reversed(range(blocks)) for j in range(i + 1)], jnp.int32)
-    heads = segments[::B]
-    tails = segments[B - 1 :: B]
-    touch = (heads[:, None] <= tails[None, :]).astype(jnp.int32)
-    shift = first * (blocks // 2)
-
-    def table(rows, keys):
-        active = touch[rows, keys]
+    )(table, e, q, d, q, k, k, v)
+
+
+def tile_tables(blocks, position):
+    pairs = [(i, j) for i in range(blocks) for j in range(i + 1)]
+    back = [(i, j) for i in reversed(range(blocks)) for j in range(i + 1)]
+    shift = position * (blocks // 2)
+
+    def table(order):
+        order = order + order[-1:]
+        rows = jnp.array([i for i, _ in order], jnp.int32)
+        keys = jnp.array([j for _, j in order], jnp.int32)
         return jnp.stack(
-            [
-                (rows + shift) % blocks,
-                (keys + shift) % blocks,
-                active,
-                rows,
-                keys,
-                rows * (rows + 1) // 2 + keys,
-                jnp.broadcast_to(slow, rows.shape),
-            ]
+            [(rows + shift) % blocks, (keys + shift) % blocks, rows, keys, rows * (rows + 1) // 2 + keys]
         )
 
-    return table(ib, jb), table(back_ib, back_jb)
-
-
-def mlp_kernel(x_ref, ob_ref, dy_ref, li_ref, gain_ref, wo_ref, wu_ref, wd_ref, out_ref, dx_ref, d_ref, dt_ref, g_any,
-               xh, scales, y, dn, n2, gup, gdown, gout, gsum, stage, sem):
+    return table(pairs), table(back)
+
+
+PART = 256
+ROWS = 64
+
+
+def mlp_kernel(x_ref, x2_ref, ob_ref, dy1_ref, dy2_ref, li_ref, gain_ref, wo_ref, wu_ref, wd_ref, out_ref, dx_ref, d_ref, g_any,
+               xh, scales, y, dn, n2, gup, gdown, gout, gsum, stage, us, das, actives, dus, sem):
     c, t = pl.program_id(0), pl.program_id(1)
     chunks, steps = pl.num_programs(0), pl.num_programs(1)
     rows = pl.ds(pl.multiple_of(t * BT, BT), BT)
@@ -454,7 +582,7 @@
 
     @pl.when(c == 0)
     def _():
-        middle = x_ref[...].astype(F32) + dot(ob_ref[...], wo_ref[...])
+        middle = pick_half(x_ref, x2_ref, t, steps).astype(F32) + dot(ob_ref[...], wo_ref[...])
         shifted, scale = moments(middle)
         xh[rows, :] = (shifted * scale).astype(BF)
         scales[rows, :] = jnp.broadcast_to(scale, (BT, 128))
@@ -473,17 +601,49 @@
         gsum[...] = jnp.zeros_like(gsum)
 
     n2_low = n2[rows, :]
-    dy_low = dy_ref[...]
-    u = dot(n2_low, wu_ref[...])
-    da = dot_nt(dy_low, wd_ref[...])
-    cdf = 0.5 * (1.0 + lax.erf(u * math.sqrt(0.5)))
-    density = jnp.exp(-0.5 * u * u) * (1.0 / math.sqrt(2.0 * math.pi))
-    active = (u * cdf).astype(BF)
-    du = ((cdf + u * density) * da).astype(BF)
-    y[rows, :] += dot(active, wd_ref[...])
-    gdown[...] += dot_tn(active, dy_low)
-    gup[...] += dot_tn(n2_low, du)
-    dn[rows, :] += dot_nt(du, wu_ref[...])
+    dy_low = pick_half(dy1_ref, dy2_ref, t, steps)
+
+    def enter(p):
+        units = slice(PART * p, PART * p + PART)
+
+        def up():
+            us[p % 2] = dot(n2_low, wu_ref[:, units])
+
+        def down():
+            das[p % 2] = dot_nt(dy_low, wd_ref[units, :])
+
+        return [up, down]
+
+    def bend(p, n):
+        part = slice(ROWS * n, ROWS * n + ROWS)
+        u = us[p % 2, part, :]
+        cdf = 0.5 * (1.0 + lax.erf(u * math.sqrt(0.5)))
+        density = jnp.exp(-0.5 * u * u) * (1.0 / math.sqrt(2.0 * math.pi))
+        units = slice(PART * p, PART * p + PART)
+        actives[part, units] = (u * cdf).astype(BF)
+        dus[part, units] = ((cdf + u * density) * das[p % 2, part, :]).astype(BF)
+
+    def leave(p):
+        units = slice(PART * p, PART * p + PART)
+
+        def down():
+            y[rows, :] += dot(actives[:, units], wd_ref[units, :])
+
+        def up():
+            dn[rows, :] += dot_nt(dus[:, units], wu_ref[:, units])
+
+        return [down, up]
+
+    parts = features // PART
+    for step in enter(0):
+        step()
+    for p in range(parts):
+        products = (leave(p - 1) if p else []) + (enter(p + 1) if p + 1 < parts else [])
+        mixed(products, [partial(bend, p, n) for n in range(BT // ROWS)])
+    for step in leave(parts - 1):
+        step()
+    gdown[...] += dot_tn(actives[...], dy_low)
+    gup[...] += dot_tn(n2_low, dus[...])
 
     @pl.when(t == steps - 1)
     def _():
@@ -509,11 +669,10 @@
         dx = dy_low.astype(F32) + scale * (
             inner - jnp.mean(inner, axis=-1, keepdims=True) - unit * jnp.mean(inner * unit, axis=-1, keepdims=True)
         )
-        dx_ref[...] = dx
+        dx_ref[...] = dx.astype(BF)
         db = dx.astype(BF)
         gout[...] += dot_tn(ob_ref[...], db)
         scaled = dot_nt(db, wo_ref[...]) * li_ref[...]
-        dt_ref[...] = scaled.astype(BF).T
         low = half_lanes(BT)
         lane = iota((BT, 128), 1)
         swap_row, swap_col = iota((128, 128), 0), iota((128, 128), 1)
@@ -545,16 +704,19 @@
         last.wait()
 
 
-def feed_forward(x, ob, dy, li, gains, weights):
-    tokens, features = x.shape
+def feed_forward(x, x_other, ob, dy, dy_other, li, gains, weights):
+    tokens, features = ob.shape
     steps = tokens // BT
     chunks = 4
 
     def ends(c, t):
         return (jnp.where((c == 0) | (c == chunks - 1), t, steps - 1), 0)
 
-    def at_first(c, t):
-        return (jnp.where(c == 0, t, steps - 1), 0)
+    def own(t):
+        return jnp.minimum(t, steps // 2 - 1)
+
+    def other(t):
+        return jnp.maximum(t - steps // 2, 0)
 
     def at_last(c, t):
         return (jnp.where(c == chunks - 1, t, 0), 0)
@@ -565,27 +727,27 @@
         mlp_kernel,
         grid=(chunks, steps),
         in_specs=[
-            pl.BlockSpec(block, at_first, pipeline_mode=once),
+            pl.BlockSpec(block, lambda c, t: (own(jnp.where(c == 0, t, steps - 1)), 0), pipeline_mode=once),
+            pl.BlockSpec(block, lambda c, t: (other(jnp.where(c == 0, t, steps - 1)), 0), pipeline_mode=once),
             pl.BlockSpec(block, ends),
-            pl.BlockSpec(block, lambda c, t: (t, 0)),
+            pl.BlockSpec(block, lambda c, t: (own(t), 0)),
+            pl.BlockSpec(block, lambda c, t: (other(t), 0)),
             pl.BlockSpec(block, at_last, pipeline_mode=once),
             pl.BlockSpec((8, features), lambda c, t: (0, 0)),
-            pl.BlockSpec((features, features), lambda c, t: (0, 3), pipeline_mode=once),
-            pl.BlockSpec((features, features), lambda c, t: (0, 4 + c)),
-            pl.BlockSpec((features, features), lambda c, t: (0, 8 + c)),
+            pl.BlockSpec((features, features), lambda c, t: (0, 0), pipeline_mode=once),
+            pl.BlockSpec((features, features), lambda c, t: (0, 1 + c)),
+            pl.BlockSpec((features, features), lambda c, t: (0, 1 + chunks + c)),
         ],
         out_specs=[
             pl.BlockSpec(block, at_last),
             pl.BlockSpec(block, at_last),
             pl.BlockSpec((BT, 2 * features), at_last),
-            pl.BlockSpec((features, BT), lambda c, t: (0, at_last(c, t)[0])),
             pl.BlockSpec(memory_space=pl.ANY),
         ],
         out_shape=[
             jax.ShapeDtypeStruct((tokens, features), BF),
-            jax.ShapeDtypeStruct((tokens, features), F32),
+            jax.ShapeDtypeStruct((tokens, features), BF),
             jax.ShapeDtypeStruct((tokens, 2 * features), BF),
-            jax.ShapeDtypeStruct((features, tokens), BF),
             jax.ShapeDtypeStruct((features, 9 * features + 128), BF),
         ],
         scratch_shapes=[
@@ -599,82 +761,109 @@
             pltpu.VMEM((features, features), F32),
             pltpu.VMEM((8, features), F32),
             pltpu.VMEM((4, features, features), BF),
+            pltpu.VMEM((2, BT, PART), F32),
+            pltpu.VMEM((2, BT, PART), F32),
+            pltpu.VMEM((BT, features), BF),
+            pltpu.VMEM((BT, features), BF),
             pltpu.SemaphoreType.DMA((4,)),
         ],
         compiler_params=pltpu.CompilerParams(vmem_limit_bytes=63 * MIB),
         name="feed_forward",
-    )(x, ob, dy, li, gains, weights, weights, weights)
-
-
-def first_kernel(x_ref, dqkv_ref, dx_ref, gain_ref, wq_ref, wk_ref, wv_ref, out_ref, low_ref, g_ref, acc, gsum):
+    )(x, x_other, ob, dy, dy_other, li, gains, weights, weights, weights)
+
+
+def weight_order(bits, dims):
+    return [
+        sum(((place >> (bits - 1 - n)) & 1) << dim for n, dim in enumerate(dims)) for place in range(2**bits)
+    ]
+
+
+def weight_kernel(x_ref, other_ref, dqkv_ref, gain_ref, a_ref, b_ref, acc, *, orders):
     t = pl.program_id(0)
+
+    @pl.when(t == 0)
+    def _():
+        acc[...] = jnp.zeros_like(acc)
+
+    shifted, scale = moments(pick_half(x_ref, other_ref, t, pl.num_programs(0)).astype(F32))
+    normed = (shifted * scale * gain_ref[0:1, :]).astype(BF)
+    acc[...] += dot_tn(normed, dqkv_ref[...])
+
+    @pl.when(t == pl.num_programs(0) - 1)
+    def _():
+        _, piece, split = a_ref.shape
+        for place, block in enumerate(orders[0]):
+            a_ref[place] = acc[piece * block : piece * block + piece, :split].astype(BF)
+        for place, block in enumerate(orders[1]):
+            b_ref[place] = acc[piece * block : piece * block + piece, split:].astype(BF)
+
+
+def first_weight_gradient(x, x_other, dqkv, gains, orders):
+    tokens, features = dqkv.shape[0], x.shape[1]
+    steps = tokens // BT
+    blocks = len(orders[0])
+    shapes = [(blocks, features // blocks, cols) for cols in (2 * features, features)]
+    return pl.pallas_call(
+        partial(weight_kernel, orders=orders),
+        grid=(steps,),
+        in_specs=[
+            *halves(features, steps),
+            pl.BlockSpec((BT, 3 * features), lambda t: (t, 0)),
+            pl.BlockSpec(gains.shape, lambda t: (0, 0)),
+        ],
+        out_specs=[pl.BlockSpec(shape, lambda t: (0, 0, 0)) for shape in shapes],
+        out_shape=[jax.ShapeDtypeStruct(shape, BF) for shape in shapes],
+        scratch_shapes=[pltpu.VMEM((features, 3 * features), F32)],
+        compiler_params=pltpu.CompilerParams(vmem_limit_bytes=48 * MIB),
+        cost_estimate=pl.CostEstimate(
+            flops=12 * tokens * features * features, bytes_accessed=16 * tokens * features, transcendentals=0
+        ),
+        name="first_weight_gradient",
+    )(x, x_other, dqkv, gains)
+
+
+def tokens_kernel(x_ref, dqkv_ref, dx_ref, gain_ref, w_ref, v_w_ref, out_ref, gsum_ref):
     features = x_ref.shape[1]
 
-    @pl.when(t == 0)
-    def _():
-        acc[...] = jnp.zeros_like(acc)
-        gsum[...] = jnp.zeros_like(gsum)
+    @pl.when(pl.program_id(0) == 0)
+    def _():
+        gsum_ref[...] = jnp.zeros_like(gsum_ref)
 
     shifted, scale = moments(x_ref[...].astype(F32))
     xh = shifted * scale
-    gain = gain_ref[0:1, :]
-    normed = (xh * gain).astype(BF)
-    acc[...] += dot_tn(normed, dqkv_ref[...])
-    d_normed = (
-        dot_nt(dqkv_ref[:, :features], wq_ref[...])
-        + dot_nt(dqkv_ref[:, features : 2 * features], wk_ref[...])
-        + dot_nt(dqkv_ref[:, 2 * features :], wv_ref[...])
-    )
-    gsum[...] += jnp.sum((d_normed * xh).reshape(BT // 8, 8, features), axis=0)
-    inner = d_normed * gain
-    dx = dx_ref[...] + scale * (
+    d_normed = dot_nt(dqkv_ref[:, : 2 * features], w_ref[...])
+    d_normed += dot_nt(dqkv_ref[:, 2 * features :], v_w_ref[:, :features])
+    gsum_ref[...] += jnp.sum((d_normed * xh).reshape(BT // 8, 8, features), axis=0)
+    inner = d_normed * gain_ref[0:1, :]
+    dx = dx_ref[...].astype(F32) + scale * (
         inner - jnp.mean(inner, axis=-1, keepdims=True) - xh * jnp.mean(inner * xh, axis=-1, keepdims=True)
     )
-    out_ref[...] = dx
-    low_ref[...] = dx.astype(BF)
-
-    @pl.when(t == pl.num_programs(0) - 1)
-    def _():
-        g_ref[:, : 3 * features] = acc[...].astype(BF)
-        column = jnp.broadcast_to(jnp.sum(gsum[...], axis=0, keepdims=True), (128, features))
-        g_ref[:, 3 * features :] = column.T.astype(BF)
-
-
-def first_gradients(x, dqkv, dx, gains, weights):
+    out_ref[...] = dx.astype(out_ref.dtype)
+
+
+def first_token_gradient(x, dqkv, dx, gains, w_qk, w_v, half, dtype):
     tokens, features = x.shape
+    steps = tokens // BT
 
     def tall(cols):
-        return pl.BlockSpec((BT, cols), lambda t: (t, 0))
-
-    def column(i):
-        return pl.BlockSpec((features, features), lambda t: (0, i))
-
+        return pl.BlockSpec((BT, cols), lambda t: (t + half * steps, 0))
+
+    def whole(array):
+        return pl.BlockSpec(array.shape, lambda t: (0, 0))
+
+    own = pl.BlockSpec((BT, features), lambda t: (t, 0))
     return pl.pallas_call(
-        first_kernel,
-        grid=(tokens // BT,),
-        in_specs=[
-            tall(features),
-            tall(3 * features),
-            tall(features),
-            pl.BlockSpec((8, features), lambda t: (0, 0)),
-            column(0),
-            column(1),
-            column(2),
-        ],
-        out_specs=[
-            tall(features),
-            tall(features),
-            pl.BlockSpec((features, 3 * features + 128), lambda t: (0, 0)),
-        ],
-        out_shape=[
-            jax.ShapeDtypeStruct((tokens, features), F32),
-            jax.ShapeDtypeStruct((tokens, features), BF),
-            jax.ShapeDtypeStruct((features, 3 * features + 128), BF),
-        ],
-        scratch_shapes=[pltpu.VMEM((features, 3 * features), F32), pltpu.VMEM((8, features), F32)],
-        compiler_params=pltpu.CompilerParams(vmem_limit_bytes=60 * MIB),
-        name="first_gradients",
-    )(x, dqkv, dx, gains, weights, weights, weights)
+        tokens_kernel,
+        grid=(steps,),
+        in_specs=[own, tall(3 * features), tall(features), whole(gains), whole(w_qk), whole(w_v)],
+        out_specs=[own, pl.BlockSpec((8, features), lambda t: (0, 0))],
+        out_shape=[jax.ShapeDtypeStruct((tokens, features), dtype), jax.ShapeDtypeStruct((8, features), F32)],
+        compiler_params=pltpu.CompilerParams(vmem_limit_bytes=48 * MIB),
+        cost_estimate=pl.CostEstimate(
+            flops=12 * tokens * features * features, bytes_accessed=16 * tokens * features, transcendentals=0
+        ),
+        name="first_token_gradient",
+    )(x, dqkv, dx, gains, w_qk, w_v)
 
 
 def swap(value):
@@ -692,41 +881,114 @@
     return jnp.where(position == 0, jnp.stack([own, other]), jnp.stack([other, own]))
 
 
+def exchange(value, dim):
+    axis = "seq" if dim == 0 else "row"
+    step = 1 if dim == 0 else 1 << (dim - 1)
+    return lax.ppermute(value, axis, [(i, i ^ step) for i in range(lax.axis_size(axis))])
+
+
+def bit(dim):
+    return lax.axis_index("seq") if dim == 0 else (lax.axis_index("row") >> (dim - 1)) & 1
+
+
+def doubled(array, shape, held, dim):
+    other = exchange(array, dim)
+    outer = sum(1 for d in held if d > dim)
+    own = array.reshape(2**outer, -1, *shape)
+    other = other.reshape(own.shape)
+    both = jnp.where(bit(dim) == 0, jnp.stack([own, other], 1), jnp.stack([other, own], 1))
+    return both.reshape(-1, *shape)
+
+
+def halved(value, dim):
+    half = value.shape[0] // 2
+    mine = bit(dim)
+    keep = lax.dynamic_slice_in_dim(value, mine * half, half, 0)
+    send = lax.dynamic_slice_in_dim(value, (1 - mine) * half, half, 0)
+    return keep + exchange(send, dim)
+
+
+def cut(value, shares):
+    rows = value.shape[0] // sum(shares)
+    ends = [rows * sum(shares[: n + 1]) for n in range(len(shares))]
+    return [value[end - rows * share : end] for share, end in zip(shares, ends) if share]
+
+
+def after(value, *others):
+    return lax.optimization_barrier((value, *others))[0]
+
+
 def row_body(tokens, segments, w_qkv, w_out, w_up, w_down, gain_attn, gain_mlp, cotangent):
     both = ("row", "seq")
     position = lax.axis_index("seq")
+    devices = 2 * lax.axis_size("row")
+    bits = devices.bit_length() - 1
+    far = tuple(range(3, bits))
     _, half, features = tokens.shape
-    own, other = own_and_other(tokens, position)
-    x = jnp.concatenate([own, swap(other)])
-    packed = pack(w_qkv, w_out, w_up, w_down, gain_attn, gain_mlp)
-    weights = lax.all_gather(packed, both, axis=0, tiled=True)
-    own, other = own_and_other(cotangent, position)
-    dy = jnp.concatenate([own, swap(other)])
+    *pieces, later_piece = pack(w_qkv, w_out, w_up, w_down, gain_attn, gain_mlp)
+    x, other = own_and_other(tokens, position)
+    paths = ((0, *reversed(far), 2, 1), (0, 2, *reversed(far), 1))
+    gathered = [piece[None] for piece in pieces]
+    parts = cut(other, [0] * (bits - 4) + [2, 2, 3, 1])
+    x_parts = []
+    for stage in range(bits):
+        *gathered, x_parts, parts = lax.optimization_barrier((*gathered, x_parts, parts))
+        if stage == bits - 2:
+            later_piece = after(later_piece, *gathered)
+        for n, path in enumerate(paths):
+            gathered[n] = doubled(gathered[n], pieces[n].shape, path[:stage], path[stage])
+        if stage and parts:
+            x_parts = x_parts + [swap(parts[0])]
+            parts = parts[1:]
+    x_other = jnp.concatenate(x_parts)
+    w_qk, w_v = [array.reshape(-1, array.shape[-1]) for array in gathered]
+    w_later = lax.all_gather(later_piece, both, axis=0, tiled=True)
+    dy, other = own_and_other(cotangent, position)
+    dy_other = swap(after(other, w_qk, x_other))
     row_segments = lax.dynamic_index_in_dim(segments, position, 0, keepdims=False)
     stored = jnp.roll(row_segments, position * half)
     seg_col = stored[:, None]
     seg_row = jnp.broadcast_to(stored.reshape(-1, 1, B), (stored.shape[0] // B, 8, B))
-    q, k, v, qt, gains, sizes = project_qkv(x, weights)
-    slow = jnp.any(sizes[0] * sizes[1] * 1.05 > SAFE * SAFE).astype(jnp.int32)
-    table, back_table = tile_tables(row_segments, position, slow)
-    ob, li, e = attention_forward(table, q, k, v, seg_col, seg_row)
-    output, dx, d, dt, g_later = feed_forward(x, ob, dy, li, gains, weights)
+    q, k, v, gains, sizes = project_qkv(x, x_other, w_qk, w_v)
+    slow = jnp.any(sizes[0] * sizes[1] * 1.05 > SAFE * SAFE).astype(jnp.int32)[None]
+    table, back_table = tile_tables(2 * half // B, position)
+    ob, li, e = attention_forward(table, slow, q, k, v, seg_col, seg_row)
+    output, dx, d, g_later = feed_forward(x, x_other, ob, dy, dy_other, li, gains, w_later)
     r_later = lax.psum_scatter(g_later, both, scatter_dimension=0, tiled=True)
-    output = in_order(output[:half], swap(output[half:]), position)
-    dqkv = attention_backward(back_table, e, q, k, v, d, qt, dt, seg_col, seg_row)
-    d_tokens, d_low, g_first = first_gradients(x, dqkv, dx, gains, weights)
-    g_first, r_later = lax.optimization_barrier((g_first, r_later))
-    r_first = lax.psum_scatter(g_first, both, scatter_dimension=0, tiled=True)
-    d_tokens = in_order(d_tokens[:half], swap(d_low[half:]).astype(F32), position)
+    output_other = swap(output[half:])
+    dqkv = attention_backward(back_table, e, q, k, v, d)
+    dqkv, output_other = lax.optimization_barrier((dqkv, output_other))
+    paths = ((1, 2, *far, 0), (1, *far, 2, 0))
+    d_other, sum_other = first_token_gradient(x_other, dqkv, dx, gains, w_qk, w_v, 1, BF)
+    parts = cut(d_other, [1, 1, 1, 1])
+    d_parts = []
+    orders = [weight_order(bits, path) for path in paths]
+    summed = list(first_weight_gradient(x, x_other, after(dqkv, d_other), gains, orders))
+    d_own, sum_own = first_token_gradient(x, after(dqkv, *summed), dx, gains, w_qk, w_v, 0, F32)
+    sums = jnp.sum(sum_other + sum_own, axis=0)
+    g_gain = jnp.transpose(sums.reshape(*[2] * bits, -1), [bits - 1 - dim for dim in paths[0]] + [bits])
+    g_gain = g_gain.reshape(devices, 1, -1)
+    for stage in range(bits):
+        if stage == bits - 1:
+            summed[0], r_later = lax.optimization_barrier((summed[0], r_later))
+        *summed, d_parts, parts = lax.optimization_barrier((*summed, d_parts, parts))
+        for n, path in enumerate(paths):
+            summed[n] = halved(summed[n], path[stage])
+        if parts:
+            d_parts = d_parts + [swap(parts[0])]
+            parts = parts[1:]
+        g_gain = halved(g_gain, paths[0][stage])
+    output = in_order(output[:half], output_other, position)
+    d_tokens = in_order(d_own, jnp.concatenate(d_parts).astype(F32), position)
     g_out, g_up, g_down = unpack(r_later)
     return (
         output,
         d_tokens,
-        r_first[:, : 3 * features].astype(F32),
+        jnp.concatenate([summed[0][0], summed[1][0]], axis=1).astype(F32),
         g_out,
         g_up,
         g_down,
-        r_first[:, 3 * features].astype(F32),
+        g_gain[0, 0],
         r_later[:, 9 * features].astype(F32),
     )
 
@@ -951,7 +1213,8 @@
 
 
 def body(tokens, *rest):
-    if lax.axis_size("seq") == 2 and tokens.shape[0] == 2:
+    rows = lax.axis_size("row")
+    if lax.axis_size("seq") == 2 and tokens.shape[0] == 2 and rows >= 4 and rows & (rows - 1) == 0:
         return row_body(tokens, *rest)
     return ring_body(tokens, *rest)
 

time: 651 us -> 482 us (0.74); the launches traced: 649 us -> 473 us
  waiting for transfers between devices: 242 us -> 63.4 us
  Pallas kernels: 347 us -> 304 us
  starting transfers between devices: 4.59 us -> 47.1 us
    ppermute x4 -> x10, waiting for transfers between devices: 162 us -> 13.8 us  [swap(): return lax.ppermute(value, 'seq', [(0, 1), (1, 0)])]
    unnamed x4 -> x2, waiting for transfers between devices: 57.6 us -> 0.03 us
    ppermute x0 -> x25, waiting for transfers between devices: none -> 49.6 us  [exchange(): lax.ppermute(value, axis, [(i, i ^ step) for i in range(lax.axis_size(axi...]
    pallas_call x1, Pallas kernels: 125 us -> 82.4 us  [attention_backward(): pl.pallas_call(backward_kernel, grid_spec=pltpu.PrefetchScalarGridSpec(nu...]
    ppermute x0 -> x25, starting transfers between devices: none -> 36.5 us  [exchange(): lax.ppermute(value, axis, [(i, i ^ step) for i in range(lax.axis_size(axi...]
    all_gather x1, waiting for transfers between devices: 22.5 us -> 0.01 us  [row_body(): w_later = lax.all_gather(later_piece, both, axis=0, tiled=True)]
    select_n x0 -> x10, other arithmetic: none -> 13 us  [doubled(): jnp.where(bit(dim) == 0, jnp.stack([own, other], 1), jnp.stack([other, ow...]
    concatenate x2 -> x0, other arithmetic: 6.53 us -> none  [the longest x1 3.27 us: row_body(): x = jnp.concatenate([own, swap(other)])]
  transfers between devices with their start and end apart: 7 -> 37, of which waited for: 6 -> 24; matrix products, arithmetic and copies ran while one was open for 5% -> 6% of each run, Pallas kernels for 24% -> 43%
where the time goes in v2:
time: 482 us; the launch traced here: 473 us
  Pallas kernels  304 us (63%)
  waiting for transfers between devices  63.4 us (13%)
  starting transfers between devices  47.1 us (10%)
  other arithmetic  21.7 us (5%)
  local copies, waits for them, and re-layouts  20.6 us (4%)
  between operations  15.8 us (3%)
    pallas_call x1, Pallas kernels, feed_forward(): pl.pallas_call(mlp_kernel, grid=(chunks, steps), in_specs=[pl.BlockSpec(b...  99.6 us
    pallas_call x1, Pallas kernels, attention_backward(): pl.pallas_call(backward_kernel, grid_spec=pltpu.PrefetchScalarGridSpec(nu...  82.4 us
    pallas_call x1, Pallas kernels, attention_forward(): pl.pallas_call(forward_kernel, grid_spec=pltpu.PrefetchScalarGridSpec(num...  69.4 us
    ppermute x25, waiting for transfers between devices, exchange(): lax.ppermute(value, axis, [(i, i ^ step) for i in range(lax.axis_size(axi...  49.6 us
    ppermute x25, starting transfers between devices, exchange(): lax.ppermute(value, axis, [(i, i ^ step) for i in range(lax.axis_size(axi...  36.5 us
    pallas_call x1, Pallas kernels, project_qkv(): pl.pallas_call(qkv_kernel, grid=(steps,), in_specs=[*halves(features, ste...  16.6 us
    pallas_call x2, Pallas kernels, first_token_gradient(): pl.pallas_call(tokens_kernel, grid=(steps,), in_specs=[own, tall(3 * feat...  16.6 us
    pallas_call x1, Pallas kernels, first_weight_gradient(): pl.pallas_call(partial(weight_kernel, orders=orders), grid=(steps,), in_s...  14 us
  transfers between devices with their start and end apart: 37, of which 24 were waited for; matrix products, arithmetic and copies ran while one was open for 6% of the time, Pallas kernels for 43%

profile of v2, /device:TPU:0, one launch (start us, length us, event | category | flops | bytes accessed | tf_op | source)
XLA Modules:
  0.0 472.8 jit_solution(5502614088377272341)
XLA Ops:
  15.9 3.0 collective-permute-start.1
  26.7 2.6 collective-permute-start.2
  29.3 5.5 %collective-permute-done.2 = bf16[2,24,1536]{2,1,0:T(8,128)(2,1)S(1)} collective-permute-done((bf16[2,24,1536]{2,1,0:T(8,128)(2,1)S(1)}, bf16[2,24,1536]{2,1,0:T(8,128)(2,1)S(1)}, u32[]{:S(2)}, u32[]{:S(2)}) %collective-permute-start.2) | collective-permute-done | bytes 147488 | tf_op jit(solution)/shard_map/ppermute | solution.py:887
  37.1 2.6 collective-permute-start.6
  40.5 4.8 %collective-permute-done.6 = bf16[4,24,896]{2,1,0:T(8,128)(2,1)S(1)} collective-permute-done((bf16[4,24,896]{2,1,0:T(8,128)(2,1)S(1)}, bf16[4,24,896]{2,1,0:T(8,128)(2,1)S(1)}, u32[]{:S(2)}, u32[]{:S(2)}) %collective-permute-start.6) | collective-permute-done | bytes 172064 | tf_op jit(solution)/shard_map/ppermute | solution.py:887
  51.5 4.7 collective-permute-done.9
  57.2 5.7 %collective-permute-done.8 = bf16[8,24,1536]{2,1,0:T(8,128)(2,1)S(1)} collective-permute-done((bf16[8,24,1536]{2,1,0:T(8,128)(2,1)}, bf16[8,24,1536]{2,1,0:T(8,128)(2,1)S(1)}, u32[]{:S(2)}, u32[]{:S(2)}) %collective-permute-start.8) | collective-permute-done | bytes 589856 | tf_op jit(solution)/shard_map/ppermute | solution.py:887
  70.0 4.6 collective-permute-done.11
  74.6 4.9 %maximum_select_fusion.2 = bf16[8,2,2,24,1536]{4,3,2,1,0:T(8,128)(2,1)} fusion(bf16[8,1,2,24,1536]{4,3,2,1,0:T(8,128)(2,1)} %bitcast.40, bf16[8,1,2,24,1536]{4,3,2,1,0:T(8,128)(2,1)} %bitcast.38, pred[]{:T(512)S(6)} %eq.34), kind=kLoop, calls=%fused_computation.2 | loop fusion | flops 3538944 | bytes 4718593 | tf_op jit(solution)/shard_map/jit(_where)/select_n | solution.py:899
  85.4 16.6 %project_qkv.1 = (bf16[2048,1536]{1,0:T(8,128)(2,1)}, bf16[2048,1536]{1,0:T(8,128)(2,1)}, bf16[2048,1536]{1,0:T(8,128)(2,1)}, f32[8,768]{1,0:T(8,128)S(1)}, f32[8,128]{1,0:T(8,128)S(1)}) custom-call(bf16[1024,768]{1,0:T(8,128)(2,1)S(1)} %dynamic-slice_bitcast_fusion.2.x_ref, bf16[1024,768]{1,0:T(8,128)(2,1)S(1)} %constant_dynamic-update-slice_fusion.other_ref.x2_ref.x_ref, ...), custom_call_target="tpu_custom_call" | custom-call | tf_op jit(solution)/shard_map/project_qkv/pallas_call | solution.py:176
  104.0 69.4 %attention_forward.1 = (bf16[2048,768]{1,0:T(8,128)(2,1)S(1)}, f32[2048,768]{1,0:T(8,128)}, bf16[36,13,256,256]{3,2,1,0:T(8,128)(2,1)}) custom-call(s32[5,37]{1,0:T(8,128)S(1)} %stack.161.tab, s32[1]{0:T(128)} %bitcast.47.slow, bf16[2048,1536]{1,0:T(8,128)(2,1)} %get-tuple-element.133.q_ref.q0_ref, bf16[2048,1536]{1,0:T(8,128)(2,1)} %get-tuple-element.133.q_ref.q0_ref, ...), custom_call_target="tpu_custom_call" | custom-call | tf_op jit(solution)/shard_map/attention_forward/pallas_call | solution.py:364
  175.1 99.6 %feed_forward.1 = (bf16[2048,768]{1,0:T(8,128)(2,1)}, bf16[2048,768]{1,0:T(8,128)(2,1)}, bf16[2048,1536]{1,0:T(8,128)(2,1)}, bf16[768,7040]{1,0:T(8,128)(2,1)}) custom-call(bf16[1024,768]{1,0:T(8,128)(2,1)} %copy-done.2, bf16[1024,768]{1,0:T(8,128)(2,1)} %copy-done.5, bf16[2048,768]{1,0:T(8,128)(2,1)} %copy-done.9, ...), custom_call_target="tpu_custom_call" | custom-call | tf_op jit(solution)/shard_map/feed_forward/pallas_call | solution.py:726
  278.5 82.4 %attention_backward.1.dqkv_ref = bf16[2048,2304]{1,0:T(8,128)(2,1)} custom-call(s32[5,37]{1,0:T(8,128)} %stack.172.tab, bf16[36,13,256,256]{3,2,1,0:T(8,128)(2,1)} %get-tuple-element.143.e_ref, bf16[2048,1536]{1,0:T(8,128)(2,1)} %get-tuple-element.133.q_ref.q0_ref, bf16[2048,1536]{1,0:T(8,128)(2,1)} %get-tuple-element.144.d_ref, ...), custom_call_target="tpu_custom_call" | custom-call | flops 28991029248 | bytes 2359296 | tf_op jit(solution)/shard_map/attention_backward/pallas_call | solution.py:515
  362.1 8.1 %first_token_gradient.2 = (bf16[1024,768]{1,0:T(8,128)(2,1)S(1)}, f32[8,768]{1,0:T(8,128)S(1)}) custom-call(bf16[1024,768]{1,0:T(8,128)(2,1)S(1)} %copy-done.6, bf16[2048,2304]{1,0:T(8,128)(2,1)} %attention_backward.1.dqkv_ref, bf16[2048,768]{1,0:T(8,128)(2,1)} %get-tuple-element.147.dx_ref, f32[8,768]{1,0:T(8,128)S(1)} %copy-done.11, ...), custom_call_target="tpu_custom_call" | custom-call | flops 7247757312 | bytes 12582912 | tf_op jit(solution)/shard_map/first_token_gradient/pallas_call | solution.py:855
  370.2 14.0 %first_weight_gradient.1 = (bf16[32,24,1536]{2,1,0:T(8,128)(2,1)}, bf16[32,24,768]{2,1,0:T(8,128)(2,1)S(1)}) custom-call(bf16[1024,768]{1,0:T(8,128)(2,1)S(1)} %copy-done.3, bf16[1024,768]{1,0:T(8,128)(2,1)S(1)} %copy-done.6, bf16[2048,2304]{1,0:T(8,128)(2,1)} %attention_backward.1.dqkv_ref, f32[8,768]{1,0:T(8,128)S(1)} %copy-done.11), custom_call_target="tpu_custom_call" | custom-call | flops 14495514624 | bytes 25165824 | tf_op jit(solution)/shard_map/first_weight_gradient/pallas_call | solution.py:806
  384.3 8.5 %first_token_gradient.3 = (f32[1024,768]{1,0:T(8,128)}, f32[8,768]{1,0:T(8,128)S(1)}) custom-call(bf16[1024,768]{1,0:T(8,128)(2,1)S(1)} %copy-done.3, bf16[2048,2304]{1,0:T(8,128)(2,1)} %attention_backward.1.dqkv_ref, bf16[2048,768]{1,0:T(8,128)(2,1)} %get-tuple-element.147.dx_ref, f32[8,768]{1,0:T(8,128)S(1)} %copy-done.11, bf16[768,1536]{1,0:T(8,128)(2,1)S(1)} %bitcast.83, ...), custom_call_target="tpu_custom_call" | custom-call | flops 7247757312 | bytes 12582912 | tf_op jit(solution)/shard_map/first_token_gradient/pallas_call | solution.py:855
  402.3 3.9 collective-permute-start.33
  415.3 6.7 %collective-permute-done.20 = bf16[8,24,768]{2,1,0:T(8,128)(2,1)S(1)} collective-permute-done((bf16[8,24,768]{2,1,0:T(8,128)(2,1)S(1)}, bf16[8,24,768]{2,1,0:T(8,128)(2,1)S(1)}, u32[]{:S(2)}, u32[]{:S(2)}) %collective-permute-start.20) | collective-permute-done | bytes 294944 | tf_op jit(solution)/shard_map/ppermute | solution.py:887
  425.0 3.5 collective-permute-start.23
  434.5 3.4 collective-permute-done.22
  444.4 4.7 collective-permute-done.25
  453.2 2.9 maximum_select_fusion
  457.5 3.0 unpack_gradients.1
  461.7 3.1 collective-permute-done.28
  (206 shorter events, 88.8 us)
Async XLA Ops:
  7.2 167.9 %all-gather.2.cloned.1.call-start = ((), (), s32[]{:S(2)}) async-start(), calls=%async_computation.1 | async-start | bytes 10948608 | tf_op jit(solution)/shard_map/all_gather | solution.py:945
  26.0 9.5 %collective-permute-start.4 = (bf16[256,768]{1,0:T(8,128)(2,1)S(1)}, bf16[256,768]{1,0:T(8,128)(2,1)S(1)}, u32[]{:S(2)}, u32[]{:S(2)}) collective-permute-start(bf16[256,768]{1,0:T(8,128)(2,1)S(1)} %get-tuple-element.110), channel_id=1, source_target_pairs={{0,1},{1,0},{2,3},{3,2},{4,5},{5,4},{6,7},{7,6},{8,9},{9,8},{10,11... | collective-permute-start | bytes 1179656 | tf_op jit(solution)/shard_map/ppermute | solution.py:870
  35.5 10.2 %collective-permute-start.5 = (bf16[4,24,1536]{2,1,0:T(8,128)(2,1)S(1)}, bf16[4,24,1536]{2,1,0:T(8,128)(2,1)S(1)}, u32[]{:S(2)}, u32[]{:S(2)}) collective-permute-start(bf16[4,24,1536]{2,1,0:T(8,128)(2,1)S(1)} %bitcast.93), channel_id=1, source_target_pairs={{0,8},{2,10},{4,12},{6,14},{8,0},{10,2},{12,4},{14,6},{16,24},{18,... | collective-permute-start | bytes 884744 | tf_op jit(solution)/shard_map/ppermute | solution.py:887
  37.1 8.2 %collective-permute-start.6 = (bf16[4,24,896]{2,1,0:T(8,128)(2,1)S(1)}, bf16[4,24,896]{2,1,0:T(8,128)(2,1)S(1)}, u32[]{:S(2)}, u32[]{:S(2)}) collective-permute-start(bf16[4,24,896]{2,1,0:T(8,128)(2,1)S(1)} %bitcast.95), channel_id=1, source_target_pairs={{0,16},{2,18},{4,20},{6,22},{8,24},{10,26},{12,28},{14,30},{16,0},... | collective-permute-start | bytes 516104 | tf_op jit(solution)/shard_map/ppermute | solution.py:887
  39.7 8.6 %collective-permute-start.7 = (bf16[256,768]{1,0:T(8,128)(2,1)S(1)}, bf16[256,768]{1,0:T(8,128)(2,1)S(1)}, u32[]{:S(2)}, u32[]{:S(2)}) collective-permute-start(bf16[256,768]{1,0:T(8,128)(2,1)S(1)} %get-tuple-element.117), channel_id=1, source_target_pairs={{0,1},{1,0},{2,3},{3,2},{4,5},{5,4},{6,7},{7,6},{8,9},{9,8},{10,11... | collective-permute-start | bytes 1179656 | tf_op jit(solution)/shard_map/ppermute | solution.py:870
  48.3 400.9 %reduce-scatter.4.cloned.1.call-start = ((), (), s32[]{:S(2)}) async-start(), calls=%async_computation.2 | async-start | bytes 11151360
  48.4 14.5 %collective-permute-start.8 = (bf16[8,24,1536]{2,1,0:T(8,128)(2,1)}, bf16[8,24,1536]{2,1,0:T(8,128)(2,1)S(1)}, u32[]{:S(2)}, u32[]{:S(2)}) collective-permute-start(bf16[8,24,1536]{2,1,0:T(8,128)(2,1)} %bitcast.17), channel_id=1, source_target_pairs={{0,4},{2,6},{4,0},{6,2},{8,12},{10,14},{12,8},{14,10},{16,20},{18,... | collective-permute-start | bytes 1769480 | tf_op jit(solution)/shard_map/ppermute | solution.py:887
  50.3 15.0 %collective-permute-start.10 = (bf16[384,768]{1,0:T(8,128)(2,1)}, bf16[384,768]{1,0:T(8,128)(2,1)}, u32[]{:S(2)}, u32[]{:S(2)}) collective-permute-start(bf16[384,768]{1,0:T(8,128)(2,1)} %dynamic-slice_bitcast_fusion.3), channel_id=1, source_target_pairs={{0,1},{1,0},{2,3},{3,2},{4,5},{5,4},{6,7},{7,6},{8,9},{9,8},{10,11... | collective-permute-start | bytes 1769480 | tf_op jit(solution)/shard_map/ppermute | solution.py:870
  65.3 9.2 %collective-permute-start.12 = (bf16[16,24,1536]{2,1,0:T(8,128)(2,1)}, bf16[16,24,1536]{2,1,0:T(8,128)(2,1)}, u32[]{:S(2)}, u32[]{:S(2)}) collective-permute-start(bf16[16,24,1536]{2,1,0:T(8,128)(2,1)} %bitcast.27), channel_id=1, source_target_pairs={{0,2},{2,0},{4,6},{6,4},{8,10},{10,8},{12,14},{14,12},{16,18},{18,... | collective-permute-start | bytes 3538952 | tf_op jit(solution)/shard_map/ppermute | solution.py:887
  79.6 95.5 %collective-permute-start.14 = (bf16[1024,768]{1,0:T(8,128)(2,1)}, bf16[1024,768]{1,0:T(8,128)(2,1)}, u32[]{:S(2)}, u32[]{:S(2)}) collective-permute-start(bf16[1024,768]{1,0:T(8,128)(2,1)} %get-tuple-element.137), channel_id=1, source_target_pairs={{0,1},{1,0},{2,3},{3,2},{4,5},{5,4},{6,7},{7,6},{8,9},{9,8},{10,11... | collective-permute-start | bytes 4718600 | tf_op jit(solution)/shard_map/ppermute | solution.py:870
  278.5 82.4 %collective-permute-start.15 = (bf16[1024,768]{1,0:T(8,128)(2,1)}, bf16[1024,768]{1,0:T(8,128)(2,1)S(1)}, u32[]{:S(2)}, u32[]{:S(2)}) collective-permute-start(bf16[1024,768]{1,0:T(8,128)(2,1)} %get-tuple-element.193), channel_id=1, source_target_pairs={{0,1},{1,0},{2,3},{3,2},{4,5},{5,4},{6,7},{7,6},{8,9},{9,8},{10,11... | collective-permute-start | bytes 4718600 | tf_op jit(solution)/shard_map/ppermute | solution.py:870
  393.4 12.8 %collective-permute-start.17 = (bf16[16,24,768]{2,1,0:T(8,128)(2,1)S(1)}, bf16[16,24,768]{2,1,0:T(8,128)(2,1)S(1)}, u32[]{:S(2)}, u32[]{:S(2)}) collective-permute-start(bf16[16,24,768]{2,1,0:T(8,128)(2,1)S(1)} %constant_dynamic-slice_fusion.18), channel_id=1, source_target_pairs={{0,2},{2,0},{4,6},{6,4},{8,10},{10,8},{12,14},{14,12},{16,18},{18,... | collective-permute-start | bytes 1769480 | tf_op jit(solution)/shard_map/ppermute | solution.py:887
  394.9 11.3 %collective-permute-start.16 = (bf16[16,24,1536]{2,1,0:T(8,128)(2,1)S(1)}, bf16[16,24,1536]{2,1,0:T(8,128)(2,1)S(1)}, u32[]{:S(2)}, u32[]{:S(2)}) collective-permute-start(bf16[16,24,1536]{2,1,0:T(8,128)(2,1)S(1)} %constant_dynamic-slice_fusion.19), channel_id=1, source_target_pairs={{0,2},{2,0},{4,6},{6,4},{8,10},{10,8},{12,14},{14,12},{16,18},{18,... | collective-permute-start | bytes 3538952 | tf_op jit(solution)/shard_map/ppermute | solution.py:887
  395.0 13.9 %collective-permute-start.18 = (bf16[256,768]{1,0:T(8,128)(2,1)S(1)}, bf16[256,768]{1,0:T(8,128)(2,1)S(1)}, u32[]{:S(2)}, u32[]{:S(2)}) collective-permute-start(bf16[256,768]{1,0:T(8,128)(2,1)S(1)} %get-tuple-element.156), channel_id=1, source_target_pairs={{0,1},{1,0},{2,3},{3,2},{4,5},{5,4},{6,7},{7,6},{8,9},{9,8},{10,11... | collective-permute-start | bytes 1179656 | tf_op jit(solution)/shard_map/ppermute | solution.py:870
  402.3 10.9 %collective-permute-start.33 = (f32[2,1,24]{2,0,1:T(2,128)S(1)}, f32[2,1,24]{2,0,1:T(2,128)S(1)}, u32[]{:S(2)}, u32[]{:S(2)}) collective-permute-start(f32[2,1,24]{2,0,1:T(2,128)S(1)} %constant_dynamic-slice_fusion.2), channel_id=1, source_target_pairs={{0,16},{2,18},{4,20},{6,22},{8,24},{10,26},{12,28},{14,30},{16,0},... | collective-permute-start | bytes 584 | tf_op jit(solution)/shard_map/ppermute | solution.py:887
  409.0 15.0 %collective-permute-start.19 = (bf16[8,24,1536]{2,1,0:T(8,128)(2,1)S(1)}, bf16[8,24,1536]{2,1,0:T(8,128)(2,1)S(1)}, u32[]{:S(2)}, u32[]{:S(2)}) collective-permute-start(bf16[8,24,1536]{2,1,0:T(8,128)(2,1)S(1)} %constant_dynamic-slice_fusion.17), channel_id=1, source_target_pairs={{0,4},{2,6},{4,0},{6,2},{8,12},{10,14},{12,8},{14,10},{16,20},{18,... | collective-permute-start | bytes 1769480 | tf_op jit(solution)/shard_map/ppermute | solution.py:887
  410.7 11.3 %collective-permute-start.20 = (bf16[8,24,768]{2,1,0:T(8,128)(2,1)S(1)}, bf16[8,24,768]{2,1,0:T(8,128)(2,1)S(1)}, u32[]{:S(2)}, u32[]{:S(2)}) collective-permute-start(bf16[8,24,768]{2,1,0:T(8,128)(2,1)S(1)} %constant_dynamic-slice_fusion.16), channel_id=1, source_target_pairs={{0,8},{2,10},{4,12},{6,14},{8,0},{10,2},{12,4},{14,6},{16,24},{18,... | collective-permute-start | bytes 884744 | tf_op jit(solution)/shard_map/ppermute | solution.py:887
  413.2 17.1 %collective-permute-start.34 = (f32[1,1,24]{2,0,1:T(1,128)S(1)}, f32[1,1,24]{2,0,1:T(1,128)S(1)}, u32[]{:S(2)}, u32[]{:S(2)}) collective-permute-start(f32[1,1,24]{2,0,1:T(1,128)S(1)} %constant_dynamic-slice_fusion), channel_id=1, source_target_pairs={{0,1},{1,0},{2,3},{3,2},{4,5},{5,4},{6,7},{7,6},{8,9},{9,8},{10,11... | collective-permute-start | bytes 296 | tf_op jit(solution)/shard_map/ppermute | solution.py:887
  415.1 10.0 %collective-permute-start.21 = (bf16[256,768]{1,0:T(8,128)(2,1)S(1)}, bf16[256,768]{1,0:T(8,128)(2,1)S(1)}, u32[]{:S(2)}, u32[]{:S(2)}) collective-permute-start(bf16[256,768]{1,0:T(8,128)(2,1)S(1)} %get-tuple-element.163), channel_id=1, source_target_pairs={{0,1},{1,0},{2,3},{3,2},{4,5},{5,4},{6,7},{7,6},{8,9},{9,8},{10,11... | collective-permute-start | bytes 1179656 | tf_op jit(solution)/shard_map/ppermute | solution.py:870
  425.0 9.5 %collective-permute-start.23 = (bf16[4,24,768]{2,1,0:T(8,128)(2,1)S(1)}, bf16[4,24,768]{2,1,0:T(8,128)(2,1)S(1)}, u32[]{:S(2)}, u32[]{:S(2)}) collective-permute-start(bf16[4,24,768]{2,1,0:T(8,128)(2,1)S(1)} %constant_dynamic-slice_fusion.14), channel_id=1, source_target_pairs={{0,16},{2,18},{4,20},{6,22},{8,24},{10,26},{12,28},{14,30},{16,0},... | collective-permute-start | bytes 442376 | tf_op jit(solution)/shard_map/ppermute | solution.py:887
  428.6 9.4 %collective-permute-start.22 = (bf16[4,24,1536]{2,1,0:T(8,128)(2,1)S(1)}, bf16[4,24,1536]{2,1,0:T(8,128)(2,1)S(1)}, u32[]{:S(2)}, u32[]{:S(2)}) collective-permute-start(bf16[4,24,1536]{2,1,0:T(8,128)(2,1)S(1)} %constant_dynamic-slice_fusion.15), channel_id=1, source_target_pairs={{0,8},{2,10},{4,12},{6,14},{8,0},{10,2},{12,4},{14,6},{16,24},{18,... | collective-permute-start | bytes 884744 | tf_op jit(solution)/shard_map/ppermute | solution.py:887
  430.9 9.2 %collective-permute-start.24 = (bf16[256,768]{1,0:T(8,128)(2,1)S(1)}, bf16[256,768]{1,0:T(8,128)(2,1)S(1)}, u32[]{:S(2)}, u32[]{:S(2)}) collective-permute-start(bf16[256,768]{1,0:T(8,128)(2,1)S(1)} %get-tuple-element.170), channel_id=1, source_target_pairs={{0,1},{1,0},{2,3},{3,2},{4,5},{5,4},{6,7},{7,6},{8,9},{9,8},{10,11... | collective-permute-start | bytes 1179656 | tf_op jit(solution)/shard_map/ppermute | solution.py:870
  442.1 8.4 %collective-permute-start.27 = (bf16[256,768]{1,0:T(8,128)(2,1)S(1)}, bf16[256,768]{1,0:T(8,128)(2,1)S(1)}, u32[]{:S(2)}, u32[]{:S(2)}) collective-permute-start(bf16[256,768]{1,0:T(8,128)(2,1)S(1)} %get-tuple-element.179), channel_id=1, source_target_pairs={{0,1},{1,0},{2,3},{3,2},{4,5},{5,4},{6,7},{7,6},{8,9},{9,8},{10,11... | collective-permute-start | bytes 1179656 | tf_op jit(solution)/shard_map/ppermute | solution.py:870
  450.5 11.2 %collective-permute-start.29 = (bf16[1,24,768]{2,1,0:T(8,128)(2,1)S(1)}, bf16[1,24,768]{2,1,0:T(8,128)(2,1)S(1)}, u32[]{:S(2)}, u32[]{:S(2)}) collective-permute-start(bf16[1,24,768]{2,1,0:T(8,128)(2,1)S(1)} %constant_dynamic-slice_fusion.10), channel_id=1, source_target_pairs={{0,1},{1,0},{2,3},{3,2},{4,5},{5,4},{6,7},{7,6},{8,9},{9,8},{10,11... | collective-permute-start | bytes 110600 | tf_op jit(solution)/shard_map/ppermute | solution.py:887
  (50 other events, 596.1 us)
Sparse Core Ops, SparseCore 0:
  48.4 101.5 all-gather.1
  274.9 144.6 reduce-scatter.3

commit v3 on v2

--- a/solution.py
+++ b/solution.py
@@ -229,6 +229,7 @@
 
 
 STRIP = 64
+LEAD = 2
 
 
 def key_copies(block, stored, k_any, v_any, kx, vx, sem):
@@ -338,10 +339,17 @@
     def head(h):
         e = jnp.exp2(dot_nt(qx[:, pick(h)], kx[jb, :, pick(h)]) - penalty[slot]).astype(BF)
         e_ref[0, h] = e
-        acc[:, pick(h)] += dot(e, vx[jb, :, pick(h)])
+
+    def value(h):
+        acc[:, pick(h)] += dot(e_ref[0, h], vx[jb, :, pick(h)])
 
     e_ref[0, H] = gate[slot]
-    mixed([partial(head, h) for h in range(H)], prepare(t + 1, 1 - slot))
+    steps = [partial(head, h) for h in range(LEAD)]
+    for h in range(H):
+        if h + LEAD < H:
+            steps.append(partial(head, h + LEAD))
+        steps.append(partial(value, h))
+    mixed(steps, prepare(t + 1, 1 - slot))
 
     @pl.when(jb == ib)
     def _():
@@ -490,10 +498,10 @@
                 dq[turn, :, pick(h // 2)] += jnp.where(low, parts.pop(h - 1), parts.pop(h))
 
         gate[slot] = e_ref[0, H]
-        steps = [partial(score, 0)]
+        steps = [partial(score, h) for h in range(LEAD)]
         for h in range(H):
-            if h + 1 < H:
-                steps.append(partial(score, h + 1))
+            if h + LEAD < H:
+                steps.append(partial(score, h + LEAD))
             steps.append(partial(products, h))
         mixed(steps, finish())
 
@@ -932,7 +940,8 @@
     parts = cut(other, [0] * (bits - 4) + [2, 2, 3, 1])
     x_parts = []
     for stage in range(bits):
-        *gathered, x_parts, parts = lax.optimization_barrier((*gathered, x_parts, parts))
+        if stage:
+            *gathered, x_parts, parts = lax.optimization_barrier((*gathered, x_parts, parts))
         if stage == bits - 2:
             later_piece = after(later_piece, *gathered)
         for n, path in enumerate(paths):
@@ -969,9 +978,11 @@
     g_gain = jnp.transpose(sums.reshape(*[2] * bits, -1), [bits - 1 - dim for dim in paths[0]] + [bits])
     g_gain = g_gain.reshape(devices, 1, -1)
     for stage in range(bits):
-        if stage == bits - 1:
+        if stage == bits - 2:
             summed[0], r_later = lax.optimization_barrier((summed[0], r_later))
         *summed, d_parts, parts = lax.optimization_barrier((*summed, d_parts, parts))
+        if stage:
+            summed[0], g_gain = lax.optimization_barrier((summed[0], g_gain))
         for n, path in enumerate(paths):
             summed[n] = halved(summed[n], path[stage])
         if parts:

time: 482 us -> 454 us (0.942); the launches traced: 473 us -> 452 us
  Pallas kernels: 304 us -> 288 us
  starting transfers between devices: 47.1 us -> 34.8 us
    pallas_call x1, Pallas kernels: 69.4 us -> 57.7 us  [attention_forward(): pl.pallas_call(forward_kernel, grid_spec=pltpu.PrefetchScalarGridSpec(num...]
    ppermute x25, starting transfers between devices: 36.5 us -> 28.9 us  [exchange(): lax.ppermute(value, axis, [(i, i ^ step) for i in range(lax.axis_size(axi...]
    ppermute x10, waiting for transfers between devices: 13.8 us -> 19.8 us  [swap(): return lax.ppermute(value, 'seq', [(0, 1), (1, 0)])]
  transfers between devices with their start and end apart: 37 -> 37, of which waited for: 24 -> 18; matrix products, arithmetic and copies ran while one was open for 6% -> 8% of each run, Pallas kernels for 43% -> 41%
where the time goes in v3:
time: 454 us; the launch traced here: 452 us
  Pallas kernels  288 us (63%)
  waiting for transfers between devices  67.2 us (15%)
  starting transfers between devices  34.8 us (8%)
  local copies, waits for them, and re-layouts  24.4 us (5%)
  other arithmetic  22.4 us (5%)
  between operations  15.4 us (3%)
    pallas_call x1, Pallas kernels, feed_forward(): pl.pallas_call(mlp_kernel, grid=(chunks, steps), in_specs=[pl.BlockSpec(b...  99.6 us
    pallas_call x1, Pallas kernels, attention_backward(): pl.pallas_call(backward_kernel, grid_spec=pltpu.PrefetchScalarGridSpec(nu...  78.4 us
    pallas_call x1, Pallas kernels, attention_forward(): pl.pallas_call(forward_kernel, grid_spec=pltpu.PrefetchScalarGridSpec(num...  57.7 us
    ppermute x25, waiting for transfers between devices, exchange(): lax.ppermute(value, axis, [(i, i ^ step) for i in range(lax.axis_size(axi...  47.3 us
    ppermute x25, starting transfers between devices, exchange(): lax.ppermute(value, axis, [(i, i ^ step) for i in range(lax.axis_size(axi...  28.9 us
    ppermute x10, waiting for transfers between devices, swap(): return lax.ppermute(value, 'seq', [(0, 1), (1, 0)])  19.8 us
    pallas_call x1, Pallas kernels, project_qkv(): pl.pallas_call(qkv_kernel, grid=(steps,), in_specs=[*halves(features, ste...  16.5 us
    pallas_call x2, Pallas kernels, first_token_gradient(): pl.pallas_call(tokens_kernel, grid=(steps,), in_specs=[own, tall(3 * feat...  16.3 us
  transfers between devices with their start and end apart: 37, of which 18 were waited for; matrix products, arithmetic and copies ran while one was open for 8% of the time, Pallas kernels for 41%

profile of v3, /device:TPU:0, one launch (start us, length us, event | category | flops | bytes accessed | tf_op | source)
XLA Modules:
  0.0 452.4 jit_solution(14745437983182913261)
XLA Ops:
  12.5 3.0 collective-permute-start
  23.9 2.6 collective-permute-start.2
  26.5 5.9 %collective-permute-done.2 = bf16[2,24,1536]{2,1,0:T(8,128)(2,1)S(1)} collective-permute-done((bf16[2,24,1536]{2,1,0:T(8,128)(2,1)S(1)}, bf16[2,24,1536]{2,1,0:T(8,128)(2,1)S(1)}, u32[]{:S(2)}, u32[]{:S(2)}) %collective-permute-start.2) | collective-permute-done | bytes 147488 | tf_op jit(solution)/shard_map/ppermute | solution.py:895
  33.9 2.6 collective-permute-start.6
  38.0 4.5 %collective-permute-done.6 = bf16[4,24,896]{2,1,0:T(8,128)(2,1)S(1)} collective-permute-done((bf16[4,24,896]{2,1,0:T(8,128)(2,1)S(1)}, bf16[4,24,896]{2,1,0:T(8,128)(2,1)S(1)}, u32[]{:S(2)}, u32[]{:S(2)}) %collective-permute-start.6) | collective-permute-done | bytes 172064 | tf_op jit(solution)/shard_map/ppermute | solution.py:895
  48.8 5.6 %collective-permute-done.9 = bf16[8,24,896]{2,1,0:T(8,128)(2,1)S(1)} collective-permute-done((bf16[8,24,896]{2,1,0:T(8,128)(2,1)S(1)}, bf16[8,24,896]{2,1,0:T(8,128)(2,1)S(1)}, u32[]{:S(2)}, u32[]{:S(2)}) %collective-permute-start.9) | collective-permute-done | bytes 344096 | tf_op jit(solution)/shard_map/ppermute | solution.py:895
  55.4 6.6 %collective-permute-done.8 = bf16[8,24,1536]{2,1,0:T(8,128)(2,1)S(1)} collective-permute-done((bf16[8,24,1536]{2,1,0:T(8,128)(2,1)}, bf16[8,24,1536]{2,1,0:T(8,128)(2,1)S(1)}, u32[]{:S(2)}, u32[]{:S(2)}) %collective-permute-start.8) | collective-permute-done | bytes 589856 | tf_op jit(solution)/shard_map/ppermute | solution.py:895
  67.6 6.1 %collective-permute-done.11 = bf16[128,768]{1,0:T(8,128)(2,1)S(1)} collective-permute-done((bf16[128,768]{1,0:T(8,128)(2,1)S(1)}, bf16[128,768]{1,0:T(8,128)(2,1)S(1)}, u32[]{:S(2)}, u32[]{:S(2)}) %collective-permute-start.11) | collective-permute-done | bytes 196640 | tf_op jit(solution)/shard_map/ppermute | solution.py:878
  73.8 4.8 %maximum_select_fusion.2 = bf16[8,2,2,24,1536]{4,3,2,1,0:T(8,128)(2,1)} fusion(bf16[8,1,2,24,1536]{4,3,2,1,0:T(8,128)(2,1)} %bitcast.40, bf16[8,1,2,24,1536]{4,3,2,1,0:T(8,128)(2,1)} %bitcast.38, pred[]{:T(512)S(6)} %eq.34), kind=kLoop, calls=%fused_computation.2 | loop fusion | flops 3538944 | bytes 4718593 | tf_op jit(solution)/shard_map/jit(_where)/select_n | solution.py:907
  83.2 16.5 %project_qkv.1 = (bf16[2048,1536]{1,0:T(8,128)(2,1)}, bf16[2048,1536]{1,0:T(8,128)(2,1)}, bf16[2048,1536]{1,0:T(8,128)(2,1)}, f32[8,768]{1,0:T(8,128)S(1)}, f32[8,128]{1,0:T(8,128)S(1)}) custom-call(bf16[1024,768]{1,0:T(8,128)(2,1)S(1)} %dynamic-slice_bitcast_fusion.2.x_ref, bf16[1024,768]{1,0:T(8,128)(2,1)S(1)} %constant_dynamic-update-slice_fusion.other_ref.x2_ref.x_ref, ...), custom_call_target="tpu_custom_call" | custom-call | tf_op jit(solution)/shard_map/project_qkv/pallas_call | solution.py:176
  101.6 57.7 %attention_forward.1 = (bf16[2048,768]{1,0:T(8,128)(2,1)S(1)}, f32[2048,768]{1,0:T(8,128)}, bf16[36,13,256,256]{3,2,1,0:T(8,128)(2,1)}) custom-call(s32[5,37]{1,0:T(8,128)S(1)} %stack.167.tab, s32[1]{0:T(128)} %bitcast.47.slow, bf16[2048,1536]{1,0:T(8,128)(2,1)} %get-tuple-element.129.q_ref.q0_ref, bf16[2048,1536]{1,0:T(8,128)(2,1)} %get-tuple-element.129.q_ref.q0_ref, ...), custom_call_target="tpu_custom_call" | custom-call | tf_op jit(solution)/shard_map/attention_forward/pallas_call | solution.py:372
  161.0 99.6 %feed_forward.1 = (bf16[2048,768]{1,0:T(8,128)(2,1)}, bf16[2048,768]{1,0:T(8,128)(2,1)}, bf16[2048,1536]{1,0:T(8,128)(2,1)}, bf16[768,7040]{1,0:T(8,128)(2,1)}) custom-call(bf16[1024,768]{1,0:T(8,128)(2,1)} %copy-done.2, bf16[1024,768]{1,0:T(8,128)(2,1)} %copy-done.5, bf16[2048,768]{1,0:T(8,128)(2,1)} %copy-done.9, ...), custom_call_target="tpu_custom_call" | custom-call | tf_op jit(solution)/shard_map/feed_forward/pallas_call | solution.py:734
  265.9 78.4 %attention_backward.1.dqkv_ref = bf16[2048,2304]{1,0:T(8,128)(2,1)} custom-call(s32[5,37]{1,0:T(8,128)} %stack.178.tab, bf16[36,13,256,256]{3,2,1,0:T(8,128)(2,1)} %get-tuple-element.139.e_ref, bf16[2048,1536]{1,0:T(8,128)(2,1)} %get-tuple-element.129.q_ref.q0_ref, bf16[2048,1536]{1,0:T(8,128)(2,1)} %get-tuple-element.140.d_ref, ...), custom_call_target="tpu_custom_call" | custom-call | flops 28991029248 | bytes 2359296 | tf_op jit(solution)/shard_map/attention_backward/pallas_call | solution.py:523
  345.4 8.1 %first_token_gradient.2 = (bf16[1024,768]{1,0:T(8,128)(2,1)S(1)}, f32[8,768]{1,0:T(8,128)S(1)}) custom-call(bf16[1024,768]{1,0:T(8,128)(2,1)S(1)} %copy-done.6, bf16[2048,2304]{1,0:T(8,128)(2,1)} %attention_backward.1.dqkv_ref, bf16[2048,768]{1,0:T(8,128)(2,1)} %get-tuple-element.143.dx_ref, f32[8,768]{1,0:T(8,128)S(1)} %copy-done.11, ...), custom_call_target="tpu_custom_call" | custom-call | flops 7247757312 | bytes 12582912 | tf_op jit(solution)/shard_map/first_token_gradient/pallas_call | solution.py:863
  353.5 14.0 %first_weight_gradient.1 = (bf16[32,24,1536]{2,1,0:T(8,128)(2,1)}, bf16[32,24,768]{2,1,0:T(8,128)(2,1)S(1)}) custom-call(bf16[1024,768]{1,0:T(8,128)(2,1)S(1)} %copy-done.3, bf16[1024,768]{1,0:T(8,128)(2,1)S(1)} %copy-done.6, bf16[2048,2304]{1,0:T(8,128)(2,1)} %attention_backward.1.dqkv_ref, f32[8,768]{1,0:T(8,128)S(1)} %copy-done.11), custom_call_target="tpu_custom_call" | custom-call | flops 14495514624 | bytes 25165824 | tf_op jit(solution)/shard_map/first_weight_gradient/pallas_call | solution.py:814
  370.9 8.3 %first_token_gradient.3 = (f32[1024,768]{1,0:T(8,128)}, f32[8,768]{1,0:T(8,128)S(1)}) custom-call(bf16[1024,768]{1,0:T(8,128)(2,1)S(1)} %copy-done.3, bf16[2048,2304]{1,0:T(8,128)(2,1)} %attention_backward.1.dqkv_ref, bf16[2048,768]{1,0:T(8,128)(2,1)} %get-tuple-element.143.dx_ref, f32[8,768]{1,0:T(8,128)S(1)} %copy-done.11, bf16[768,1536]{1,0:T(8,128)(2,1)S(1)} %bitcast.83, ...), custom_call_target="tpu_custom_call" | custom-call | flops 7247757312 | bytes 12582912 | tf_op jit(solution)/shard_map/first_token_gradient/pallas_call | solution.py:863
  383.6 8.6 %collective-permute-done.18 = bf16[256,768]{1,0:T(8,128)(2,1)S(1)} collective-permute-done((bf16[256,768]{1,0:T(8,128)(2,1)}, bf16[256,768]{1,0:T(8,128)(2,1)S(1)}, u32[]{:S(2)}, u32[]{:S(2)}) %collective-permute-start.18) | collective-permute-done | bytes 393248 | tf_op jit(solution)/shard_map/ppermute | solution.py:878
  397.2 7.8 %collective-permute-done.21 = bf16[8,24,768]{2,1,0:T(8,128)(2,1)S(1)} collective-permute-done((bf16[8,24,768]{2,1,0:T(8,128)(2,1)S(1)}, bf16[8,24,768]{2,1,0:T(8,128)(2,1)S(1)}, u32[]{:S(2)}, u32[]{:S(2)}) %collective-permute-start.21) | collective-permute-done | bytes 294944 | tf_op jit(solution)/shard_map/ppermute | solution.py:895
  408.5 3.3 collective-permute-start.25
  415.7 4.1 collective-permute-done.24
  419.9 3.0 unpack_gradients.1
  430.2 3.4 collective-permute-done.28
  433.6 3.8 collective-permute-done.30
  441.3 2.9 maximum_select_fusion
  (212 shorter events, 75.9 us)
Async XLA Ops:
  7.2 153.8 %all-gather.2.cloned.1.call-start = ((), (), s32[]{:S(2)}) async-start(), calls=%async_computation.1 | async-start | bytes 10948608 | tf_op jit(solution)/shard_map/all_gather | solution.py:954
  12.5 7.8 %collective-permute-start = (bf16[1,24,1536]{2,1,0:T(8,128)(2,1)}, bf16[1,24,1536]{2,1,0:T(8,128)(2,1)S(1)}, u32[]{:S(2)}, u32[]{:S(2)}) collective-permute-start(bf16[1,24,1536]{2,1,0:T(8,128)(2,1)} %bitcast.110), channel_id=1, source_target_pairs={{0,1},{1,0},{2,3},{3,2},{4,5},{5,4},{6,7},{7,6},{8,9},{9,8},{10,11... | collective-permute-start | bytes 221192 | tf_op jit(solution)/shard_map/ppermute | solution.py:895
  22.3 10.1 %collective-permute-start.4 = (bf16[256,768]{1,0:T(8,128)(2,1)S(1)}, bf16[256,768]{1,0:T(8,128)(2,1)S(1)}, u32[]{:S(2)}, u32[]{:S(2)}) collective-permute-start(bf16[256,768]{1,0:T(8,128)(2,1)S(1)} %get-tuple-element.106), channel_id=1, source_target_pairs={{0,1},{1,0},{2,3},{3,2},{4,5},{5,4},{6,7},{7,6},{8,9},{9,8},{10,11... | collective-permute-start | bytes 1179656 | tf_op jit(solution)/shard_map/ppermute | solution.py:878
  23.9 8.5 %collective-permute-start.2 = (bf16[2,24,1536]{2,1,0:T(8,128)(2,1)S(1)}, bf16[2,24,1536]{2,1,0:T(8,128)(2,1)S(1)}, u32[]{:S(2)}, u32[]{:S(2)}) collective-permute-start(bf16[2,24,1536]{2,1,0:T(8,128)(2,1)S(1)} %maximum_select_fusion.10), channel_id=1, source_target_pairs={{0,16},{2,18},{4,20},{6,22},{8,24},{10,26},{12,28},{14,30},{16,0},... | collective-permute-start | bytes 442376 | tf_op jit(solution)/shard_map/ppermute | solution.py:895
  32.4 11.6 %collective-permute-start.5 = (bf16[4,24,1536]{2,1,0:T(8,128)(2,1)S(1)}, bf16[4,24,1536]{2,1,0:T(8,128)(2,1)S(1)}, u32[]{:S(2)}, u32[]{:S(2)}) collective-permute-start(bf16[4,24,1536]{2,1,0:T(8,128)(2,1)S(1)} %bitcast.93), channel_id=1, source_target_pairs={{0,8},{2,10},{4,12},{6,14},{8,0},{10,2},{12,4},{14,6},{16,24},{18,... | collective-permute-start | bytes 884744 | tf_op jit(solution)/shard_map/ppermute | solution.py:895
  33.9 8.6 %collective-permute-start.6 = (bf16[4,24,896]{2,1,0:T(8,128)(2,1)S(1)}, bf16[4,24,896]{2,1,0:T(8,128)(2,1)S(1)}, u32[]{:S(2)}, u32[]{:S(2)}) collective-permute-start(bf16[4,24,896]{2,1,0:T(8,128)(2,1)S(1)} %bitcast.95), channel_id=1, source_target_pairs={{0,16},{2,18},{4,20},{6,22},{8,24},{10,26},{12,28},{14,30},{16,0},... | collective-permute-start | bytes 516104 | tf_op jit(solution)/shard_map/ppermute | solution.py:895
  36.6 9.7 %collective-permute-start.7 = (bf16[256,768]{1,0:T(8,128)(2,1)S(1)}, bf16[256,768]{1,0:T(8,128)(2,1)S(1)}, u32[]{:S(2)}, u32[]{:S(2)}) collective-permute-start(bf16[256,768]{1,0:T(8,128)(2,1)S(1)} %get-tuple-element.113), channel_id=1, source_target_pairs={{0,1},{1,0},{2,3},{3,2},{4,5},{5,4},{6,7},{7,6},{8,9},{9,8},{10,11... | collective-permute-start | bytes 1179656 | tf_op jit(solution)/shard_map/ppermute | solution.py:878
  46.3 373.6 %reduce-scatter.4.cloned.1.call-start = ((), (), s32[]{:S(2)}) async-start(), calls=%async_computation.2 | async-start | bytes 11151360
  46.4 15.7 %collective-permute-start.8 = (bf16[8,24,1536]{2,1,0:T(8,128)(2,1)}, bf16[8,24,1536]{2,1,0:T(8,128)(2,1)S(1)}, u32[]{:S(2)}, u32[]{:S(2)}) collective-permute-start(bf16[8,24,1536]{2,1,0:T(8,128)(2,1)} %bitcast.17), channel_id=1, source_target_pairs={{0,4},{2,6},{4,0},{6,2},{8,12},{10,14},{12,8},{14,10},{16,20},{18,... | collective-permute-start | bytes 1769480 | tf_op jit(solution)/shard_map/ppermute | solution.py:895
  47.0 7.5 %collective-permute-start.9 = (bf16[8,24,896]{2,1,0:T(8,128)(2,1)S(1)}, bf16[8,24,896]{2,1,0:T(8,128)(2,1)S(1)}, u32[]{:S(2)}, u32[]{:S(2)}) collective-permute-start(bf16[8,24,896]{2,1,0:T(8,128)(2,1)S(1)} %bitcast.91), channel_id=1, source_target_pairs={{0,8},{2,10},{4,12},{6,14},{8,0},{10,2},{12,4},{14,6},{16,24},{18,... | collective-permute-start | bytes 1032200 | tf_op jit(solution)/shard_map/ppermute | solution.py:895
  48.3 16.2 %collective-permute-start.10 = (bf16[384,768]{1,0:T(8,128)(2,1)}, bf16[384,768]{1,0:T(8,128)(2,1)}, u32[]{:S(2)}, u32[]{:S(2)}) collective-permute-start(bf16[384,768]{1,0:T(8,128)(2,1)} %dynamic-slice_bitcast_fusion.3), channel_id=1, source_target_pairs={{0,1},{1,0},{2,3},{3,2},{4,5},{5,4},{6,7},{7,6},{8,9},{9,8},{10,11... | collective-permute-start | bytes 1769480 | tf_op jit(solution)/shard_map/ppermute | solution.py:878
  64.5 9.2 %collective-permute-start.12 = (bf16[16,24,1536]{2,1,0:T(8,128)(2,1)}, bf16[16,24,1536]{2,1,0:T(8,128)(2,1)}, u32[]{:S(2)}, u32[]{:S(2)}) collective-permute-start(bf16[16,24,1536]{2,1,0:T(8,128)(2,1)} %bitcast.27), channel_id=1, source_target_pairs={{0,2},{2,0},{4,6},{6,4},{8,10},{10,8},{12,14},{14,12},{16,18},{18,... | collective-permute-start | bytes 3538952 | tf_op jit(solution)/shard_map/ppermute | solution.py:895
  78.5 82.4 %collective-permute-start.14 = (bf16[1024,768]{1,0:T(8,128)(2,1)}, bf16[1024,768]{1,0:T(8,128)(2,1)}, u32[]{:S(2)}, u32[]{:S(2)}) collective-permute-start(bf16[1024,768]{1,0:T(8,128)(2,1)} %get-tuple-element.133), channel_id=1, source_target_pairs={{0,1},{1,0},{2,3},{3,2},{4,5},{5,4},{6,7},{7,6},{8,9},{9,8},{10,11... | collective-permute-start | bytes 4718600 | tf_op jit(solution)/shard_map/ppermute | solution.py:878
  264.0 80.3 %collective-permute-start.15 = (bf16[1024,768]{1,0:T(8,128)(2,1)S(1)}, bf16[1024,768]{1,0:T(8,128)(2,1)S(1)}, u32[]{:S(2)}, u32[]{:S(2)}) collective-permute-start(bf16[1024,768]{1,0:T(8,128)(2,1)S(1)} %get-tuple-element.197), channel_id=1, source_target_pairs={{0,1},{1,0},{2,3},{3,2},{4,5},{5,4},{6,7},{7,6},{8,9},{9,8},{10,11... | collective-permute-start | bytes 4718600 | tf_op jit(solution)/shard_map/ppermute | solution.py:878
  368.8 12.0 %collective-permute-start.17 = (bf16[16,24,768]{2,1,0:T(8,128)(2,1)S(1)}, bf16[16,24,768]{2,1,0:T(8,128)(2,1)}, u32[]{:S(2)}, u32[]{:S(2)}) collective-permute-start(bf16[16,24,768]{2,1,0:T(8,128)(2,1)S(1)} %constant_dynamic-slice_fusion.18), channel_id=1, source_target_pairs={{0,2},{2,0},{4,6},{6,4},{8,10},{10,8},{12,14},{14,12},{16,18},{18,... | collective-permute-start | bytes 1769480 | tf_op jit(solution)/shard_map/ppermute | solution.py:895
  370.9 10.9 %collective-permute-start.16 = (bf16[16,24,1536]{2,1,0:T(8,128)(2,1)}, bf16[16,24,1536]{2,1,0:T(8,128)(2,1)}, u32[]{:S(2)}, u32[]{:S(2)}) collective-permute-start(bf16[16,24,1536]{2,1,0:T(8,128)(2,1)} %constant_dynamic-slice_fusion.19), channel_id=1, source_target_pairs={{0,2},{2,0},{4,6},{6,4},{8,10},{10,8},{12,14},{14,12},{16,18},{18,... | collective-permute-start | bytes 3538952 | tf_op jit(solution)/shard_map/ppermute | solution.py:895
  379.9 12.3 %collective-permute-start.18 = (bf16[256,768]{1,0:T(8,128)(2,1)}, bf16[256,768]{1,0:T(8,128)(2,1)S(1)}, u32[]{:S(2)}, u32[]{:S(2)}) collective-permute-start(bf16[256,768]{1,0:T(8,128)(2,1)} %get-tuple-element.152), channel_id=1, source_target_pairs={{0,1},{1,0},{2,3},{3,2},{4,5},{5,4},{6,7},{7,6},{8,9},{9,8},{10,11... | collective-permute-start | bytes 1179656 | tf_op jit(solution)/shard_map/ppermute | solution.py:878
  392.2 12.8 %collective-permute-start.21 = (bf16[8,24,768]{2,1,0:T(8,128)(2,1)S(1)}, bf16[8,24,768]{2,1,0:T(8,128)(2,1)S(1)}, u32[]{:S(2)}, u32[]{:S(2)}) collective-permute-start(bf16[8,24,768]{2,1,0:T(8,128)(2,1)S(1)} %constant_dynamic-slice_fusion.14), channel_id=1, source_target_pairs={{0,8},{2,10},{4,12},{6,14},{8,0},{10,2},{12,4},{14,6},{16,24},{18,... | collective-permute-start | bytes 884744 | tf_op jit(solution)/shard_map/ppermute | solution.py:895
  393.1 14.4 %collective-permute-start.20 = (bf16[8,24,1536]{2,1,0:T(8,128)(2,1)S(1)}, bf16[8,24,1536]{2,1,0:T(8,128)(2,1)S(1)}, u32[]{:S(2)}, u32[]{:S(2)}) collective-permute-start(bf16[8,24,1536]{2,1,0:T(8,128)(2,1)S(1)} %constant_dynamic-slice_fusion.15), channel_id=1, source_target_pairs={{0,4},{2,6},{4,0},{6,2},{8,12},{10,14},{12,8},{14,10},{16,20},{18,... | collective-permute-start | bytes 1769480 | tf_op jit(solution)/shard_map/ppermute | solution.py:895
  397.1 10.5 %collective-permute-start.22 = (bf16[256,768]{1,0:T(8,128)(2,1)S(1)}, bf16[256,768]{1,0:T(8,128)(2,1)S(1)}, u32[]{:S(2)}, u32[]{:S(2)}) collective-permute-start(bf16[256,768]{1,0:T(8,128)(2,1)S(1)} %copy-done.22), channel_id=1, source_target_pairs={{0,1},{1,0},{2,3},{3,2},{4,5},{5,4},{6,7},{7,6},{8,9},{9,8},{10,11... | collective-permute-start | bytes 1179656 | tf_op jit(solution)/shard_map/ppermute | solution.py:878
  411.8 8.1 %collective-permute-start.24 = (bf16[4,24,1536]{2,1,0:T(8,128)(2,1)S(1)}, bf16[4,24,1536]{2,1,0:T(8,128)(2,1)S(1)}, u32[]{:S(2)}, u32[]{:S(2)}) collective-permute-start(bf16[4,24,1536]{2,1,0:T(8,128)(2,1)S(1)} %constant_dynamic-slice_fusion.11), channel_id=1, source_target_pairs={{0,8},{2,10},{4,12},{6,14},{8,0},{10,2},{12,4},{14,6},{16,24},{18,... | collective-permute-start | bytes 884744 | tf_op jit(solution)/shard_map/ppermute | solution.py:895
  413.2 11.1 %collective-permute-start.26 = (bf16[256,768]{1,0:T(8,128)(2,1)S(1)}, bf16[256,768]{1,0:T(8,128)(2,1)S(1)}, u32[]{:S(2)}, u32[]{:S(2)}) collective-permute-start(bf16[256,768]{1,0:T(8,128)(2,1)S(1)} %copy-done.19), channel_id=1, source_target_pairs={{0,1},{1,0},{2,3},{3,2},{4,5},{5,4},{6,7},{7,6},{8,9},{9,8},{10,11... | collective-permute-start | bytes 1179656 | tf_op jit(solution)/shard_map/ppermute | solution.py:878
  425.8 7.7 %collective-permute-start.28 = (bf16[2,24,1536]{2,1,0:T(8,128)(2,1)S(1)}, bf16[2,24,1536]{2,1,0:T(8,128)(2,1)S(1)}, u32[]{:S(2)}, u32[]{:S(2)}) collective-permute-start(bf16[2,24,1536]{2,1,0:T(8,128)(2,1)S(1)} %constant_dynamic-slice_fusion.7), channel_id=1, source_target_pairs={{0,16},{2,18},{4,20},{6,22},{8,24},{10,26},{12,28},{14,30},{16,0},... | collective-permute-start | bytes 442376 | tf_op jit(solution)/shard_map/ppermute | solution.py:895
  428.3 9.0 %collective-permute-start.30 = (bf16[256,768]{1,0:T(8,128)(2,1)S(1)}, bf16[256,768]{1,0:T(8,128)(2,1)S(1)}, u32[]{:S(2)}, u32[]{:S(2)}) collective-permute-start(bf16[256,768]{1,0:T(8,128)(2,1)S(1)} %copy-done.18), channel_id=1, source_target_pairs={{0,1},{1,0},{2,3},{3,2},{4,5},{5,4},{6,7},{7,6},{8,9},{9,8},{10,11... | collective-permute-start | bytes 1179656 | tf_op jit(solution)/shard_map/ppermute | solution.py:878
  (53 other events, 620.5 us)
Sparse Core Ops, SparseCore 0:
  46.4 101.9 all-gather.1
  260.7 145.1 reduce-scatter.3

commit v4 on v3

--- a/solution.py
+++ b/solution.py
@@ -52,12 +52,12 @@
     return (iota((piece, 4 * piece), 1) == 4 * iota((piece, 4 * piece), 0) + c).astype(F32).astype(BF)
 
 
-def pack_kernel(qkv_ref, out_ref, up_ref, down_ref, ga_ref, gm_ref, a_ref, b_ref, l_ref):
+def pack_kernel(qkv_ref, out_ref, up_ref, down_ref, gain_ref, a_ref, b_ref, l_ref):
     piece, features = out_ref.shape
     lane = iota((piece, 128), 1)
     a_ref[...] = qkv_ref[:, : 2 * features].astype(BF)
     b_ref[:, :features] = qkv_ref[:, 2 * features :].astype(BF)
-    gains = jnp.where(lane == 0, ga_ref[...], jnp.where(lane == 1, gm_ref[...], 0.0))
+    gains = jnp.where(lane == 0, gain_ref[:, 0:1], jnp.where(lane == 1, gain_ref[:, 1:2], 0.0))
     b_ref[:, features:] = gains.astype(BF)
     l_ref[:, :features] = out_ref[...].astype(BF)
     for c in range(4):
@@ -78,7 +78,7 @@
             jax.ShapeDtypeStruct((piece, cols), BF) for cols in (2 * features, features + 128, 9 * features)
         ],
         name="pack_weights",
-    )(w_qkv, w_out, w_up, w_down, gain_attn[:, None], gain_mlp[:, None])
+    )(w_qkv, w_out, w_up, w_down, jnp.stack([gain_attn, gain_mlp], axis=1))
 
 
 def unpack_kernel(b_ref, out_ref, up_ref, down_ref):
@@ -578,7 +578,7 @@
 
 
 def mlp_kernel(x_ref, x2_ref, ob_ref, dy1_ref, dy2_ref, li_ref, gain_ref, wo_ref, wu_ref, wd_ref, out_ref, dx_ref, d_ref, g_any,
-               xh, scales, y, dn, n2, gup, gdown, gout, gsum, stage, us, das, actives, dus, sem):
+               xh, scales, y, dn, n2, gup, gdown, gout, gsum, stage, gcol, us, das, actives, dus, sem):
     c, t = pl.program_id(0), pl.program_id(1)
     chunks, steps = pl.num_programs(0), pl.num_programs(1)
     rows = pl.ds(pl.multiple_of(t * BT, BT), BT)
@@ -700,9 +700,9 @@
     def _():
         stage[2] = gout[...].astype(BF)
         column = jnp.broadcast_to(jnp.sum(gsum[...], axis=0, keepdims=True), (128, features))
-        stage[3, :, :128] = column.T.astype(BF)
+        gcol[...] = column.T.astype(BF)
         last = pltpu.make_async_copy(
-            stage.at[3, :, pl.ds(0, 128)], g_any.at[:, pl.ds((1 + 2 * 4) * features, 128)], sem.at[3]
+            gcol, g_any.at[:, pl.ds((1 + 2 * 4) * features, 128)], sem.at[3]
         )
         send(2, 0).start()
         last.start()
@@ -740,7 +740,7 @@
             pl.BlockSpec(block, ends),
             pl.BlockSpec(block, lambda c, t: (own(t), 0)),
             pl.BlockSpec(block, lambda c, t: (other(t), 0)),
-            pl.BlockSpec(block, at_last, pipeline_mode=once),
+            pl.BlockSpec(block, at_last),
             pl.BlockSpec((8, features), lambda c, t: (0, 0)),
             pl.BlockSpec((features, features), lambda c, t: (0, 0), pipeline_mode=once),
             pl.BlockSpec((features, features), lambda c, t: (0, 1 + c)),
@@ -768,7 +768,8 @@
             pltpu.VMEM((features, features), F32),
             pltpu.VMEM((features, features), F32),
             pltpu.VMEM((8, features), F32),
-            pltpu.VMEM((4, features, features), BF),
+            pltpu.VMEM((3, features, features), BF),
+            pltpu.VMEM((features, 128), BF),
             pltpu.VMEM((2, BT, PART), F32),
             pltpu.VMEM((2, BT, PART), F32),
             pltpu.VMEM((BT, features), BF),
@@ -968,24 +969,27 @@
     dqkv = attention_backward(back_table, e, q, k, v, d)
     dqkv, output_other = lax.optimization_barrier((dqkv, output_other))
     paths = ((1, 2, *far, 0), (1, *far, 2, 0))
-    d_other, sum_other = first_token_gradient(x_other, dqkv, dx, gains, w_qk, w_v, 1, BF)
-    parts = cut(d_other, [1, 1, 1, 1])
-    d_parts = []
     orders = [weight_order(bits, path) for path in paths]
-    summed = list(first_weight_gradient(x, x_other, after(dqkv, d_other), gains, orders))
-    d_own, sum_own = first_token_gradient(x, after(dqkv, *summed), dx, gains, w_qk, w_v, 0, F32)
+    summed = list(first_weight_gradient(x, x_other, dqkv, gains, orders))
+    d_other, sum_other = first_token_gradient(x_other, after(dqkv, *summed), dx, gains, w_qk, w_v, 1, BF)
+    d_own, sum_own = first_token_gradient(x, after(dqkv, d_other), dx, gains, w_qk, w_v, 0, F32)
     sums = jnp.sum(sum_other + sum_own, axis=0)
     g_gain = jnp.transpose(sums.reshape(*[2] * bits, -1), [bits - 1 - dim for dim in paths[0]] + [bits])
     g_gain = g_gain.reshape(devices, 1, -1)
+    parts = cut(d_other, [0] * (bits - 5) + [1, 1, 1, 1])
+    d_parts = []
     for stage in range(bits):
         if stage == bits - 2:
             summed[0], r_later = lax.optimization_barrier((summed[0], r_later))
-        *summed, d_parts, parts = lax.optimization_barrier((*summed, d_parts, parts))
         if stage:
+            *summed, d_parts, parts = lax.optimization_barrier((*summed, d_parts, parts))
+        else:
+            summed = list(lax.optimization_barrier(tuple(summed)))
+        if stage > 1:
             summed[0], g_gain = lax.optimization_barrier((summed[0], g_gain))
         for n, path in enumerate(paths):
             summed[n] = halved(summed[n], path[stage])
-        if parts:
+        if stage and parts:
             d_parts = d_parts + [swap(parts[0])]
             parts = parts[1:]
         g_gain = halved(g_gain, paths[0][stage])

time: 454 us -> 449 us (0.989)
  Pallas kernels: 288 us -> 281 us
    pallas_call x1, Pallas kernels: 99.6 us -> 92.4 us  [feed_forward(): pl.pallas_call(mlp_kernel, grid=(chunks, steps), in_specs=[pl.BlockSpec(b...]
    ppermute x25, waiting for transfers between devices: 47.3 us -> 52.9 us  [exchange(): lax.ppermute(value, axis, [(i, i ^ step) for i in range(lax.axis_size(axi...]
    ppermute x10, waiting for transfers between devices: 19.8 us -> 14.7 us  [swap(): return lax.ppermute(value, 'seq', [(0, 1), (1, 0)])]
  transfers between devices with their start and end apart: 37 -> 37, of which waited for: 18 -> 18; matrix products, arithmetic and copies ran while one was open for 8% -> 8% of each run, Pallas kernels for 41% -> 42%
where the time goes in v4:
time: 449 us; the launch traced here: 447 us
  Pallas kernels  281 us (63%)
  waiting for transfers between devices  67.7 us (15%)
  starting transfers between devices  38.6 us (9%)
  local copies, waits for them, and re-layouts  23.1 us (5%)
  other arithmetic  21.8 us (5%)
  between operations  15.4 us (3%)
    pallas_call x1, Pallas kernels, feed_forward(): pl.pallas_call(mlp_kernel, grid=(chunks, steps), in_specs=[pl.BlockSpec(b...  92.4 us
    pallas_call x1, Pallas kernels, attention_backward(): pl.pallas_call(backward_kernel, grid_spec=pltpu.PrefetchScalarGridSpec(nu...  78.5 us
    pallas_call x1, Pallas kernels, attention_forward(): pl.pallas_call(forward_kernel, grid_spec=pltpu.PrefetchScalarGridSpec(num...  57.7 us
    ppermute x25, waiting for transfers between devices, exchange(): lax.ppermute(value, axis, [(i, i ^ step) for i in range(lax.axis_size(axi...  52.9 us
    ppermute x25, starting transfers between devices, exchange(): lax.ppermute(value, axis, [(i, i ^ step) for i in range(lax.axis_size(axi...  29.1 us
    pallas_call x1, Pallas kernels, project_qkv(): pl.pallas_call(qkv_kernel, grid=(steps,), in_specs=[*halves(features, ste...  16.5 us
    pallas_call x2, Pallas kernels, first_token_gradient(): pl.pallas_call(tokens_kernel, grid=(steps,), in_specs=[own, tall(3 * feat...  16.3 us
    ppermute x10, waiting for transfers between devices, swap(): return lax.ppermute(value, 'seq', [(0, 1), (1, 0)])  14.7 us
  transfers between devices with their start and end apart: 37, of which 18 were waited for; matrix products, arithmetic and copies ran while one was open for 8% of the time, Pallas kernels for 42%

profile of v4, /device:TPU:0, one launch (start us, length us, event | category | flops | bytes accessed | tf_op | source)
XLA Modules:
  0.0 447.4 jit_solution(16231400846815292620)
XLA Ops:
  11.2 3.0 collective-permute-start
  25.2 5.9 %collective-permute-done.2 = bf16[2,24,1536]{2,1,0:T(8,128)(2,1)S(1)} collective-permute-done((bf16[2,24,1536]{2,1,0:T(8,128)(2,1)S(1)}, bf16[2,24,1536]{2,1,0:T(8,128)(2,1)S(1)}, u32[]{:S(2)}, u32[]{:S(2)}) %collective-permute-start.2) | collective-permute-done | bytes 147488 | tf_op jit(solution)/shard_map/ppermute | solution.py:896
  32.6 2.6 collective-permute-start.6
  36.7 4.5 %collective-permute-done.6 = bf16[4,24,896]{2,1,0:T(8,128)(2,1)S(1)} collective-permute-done((bf16[4,24,896]{2,1,0:T(8,128)(2,1)S(1)}, bf16[4,24,896]{2,1,0:T(8,128)(2,1)S(1)}, u32[]{:S(2)}, u32[]{:S(2)}) %collective-permute-start.6) | collective-permute-done | bytes 172064 | tf_op jit(solution)/shard_map/ppermute | solution.py:896
  47.5 5.6 %collective-permute-done.9 = bf16[8,24,896]{2,1,0:T(8,128)(2,1)S(1)} collective-permute-done((bf16[8,24,896]{2,1,0:T(8,128)(2,1)S(1)}, bf16[8,24,896]{2,1,0:T(8,128)(2,1)S(1)}, u32[]{:S(2)}, u32[]{:S(2)}) %collective-permute-start.9) | collective-permute-done | bytes 344096 | tf_op jit(solution)/shard_map/ppermute | solution.py:896
  54.1 6.6 %collective-permute-done.8 = bf16[8,24,1536]{2,1,0:T(8,128)(2,1)S(1)} collective-permute-done((bf16[8,24,1536]{2,1,0:T(8,128)(2,1)}, bf16[8,24,1536]{2,1,0:T(8,128)(2,1)S(1)}, u32[]{:S(2)}, u32[]{:S(2)}) %collective-permute-start.8) | collective-permute-done | bytes 589856 | tf_op jit(solution)/shard_map/ppermute | solution.py:896
  66.3 6.1 %collective-permute-done.11 = bf16[128,768]{1,0:T(8,128)(2,1)S(1)} collective-permute-done((bf16[128,768]{1,0:T(8,128)(2,1)S(1)}, bf16[128,768]{1,0:T(8,128)(2,1)S(1)}, u32[]{:S(2)}, u32[]{:S(2)}) %collective-permute-start.11) | collective-permute-done | bytes 196640 | tf_op jit(solution)/shard_map/ppermute | solution.py:879
  72.5 4.8 %maximum_select_fusion.2 = bf16[8,2,2,24,1536]{4,3,2,1,0:T(8,128)(2,1)} fusion(bf16[8,1,2,24,1536]{4,3,2,1,0:T(8,128)(2,1)} %bitcast.40, bf16[8,1,2,24,1536]{4,3,2,1,0:T(8,128)(2,1)} %bitcast.38, pred[]{:T(512)S(6)} %eq.34), kind=kLoop, calls=%fused_computation.2 | loop fusion | flops 3538944 | bytes 4718593 | tf_op jit(solution)/shard_map/jit(_where)/select_n | solution.py:908
  81.9 16.5 %project_qkv.1 = (bf16[2048,1536]{1,0:T(8,128)(2,1)}, bf16[2048,1536]{1,0:T(8,128)(2,1)}, bf16[2048,1536]{1,0:T(8,128)(2,1)}, f32[8,768]{1,0:T(8,128)S(1)}, f32[8,128]{1,0:T(8,128)S(1)}) custom-call(bf16[1024,768]{1,0:T(8,128)(2,1)S(1)} %dynamic-slice_bitcast_fusion.2.x_ref, bf16[1024,768]{1,0:T(8,128)(2,1)S(1)} %constant_dynamic-update-slice_fusion.other_ref.x2_ref.x_ref, ...), custom_call_target="tpu_custom_call" | custom-call | tf_op jit(solution)/shard_map/project_qkv/pallas_call | solution.py:176
  100.3 57.7 %attention_forward.1 = (bf16[2048,768]{1,0:T(8,128)(2,1)S(1)}, f32[2048,768]{1,0:T(8,128)}, bf16[36,13,256,256]{3,2,1,0:T(8,128)(2,1)}) custom-call(s32[5,37]{1,0:T(8,128)S(1)} %stack.179.tab, s32[1]{0:T(128)} %bitcast.47.slow, bf16[2048,1536]{1,0:T(8,128)(2,1)} %get-tuple-element.120.q_ref.q0_ref, bf16[2048,1536]{1,0:T(8,128)(2,1)} %get-tuple-element.120.q_ref.q0_ref, ...), custom_call_target="tpu_custom_call" | custom-call | tf_op jit(solution)/shard_map/attention_forward/pallas_call | solution.py:372
  159.6 92.4 %feed_forward.1 = (bf16[2048,768]{1,0:T(8,128)(2,1)}, bf16[2048,768]{1,0:T(8,128)(2,1)}, bf16[2048,1536]{1,0:T(8,128)(2,1)}, bf16[768,7040]{1,0:T(8,128)(2,1)}) custom-call(bf16[1024,768]{1,0:T(8,128)(2,1)} %copy-done.2, bf16[1024,768]{1,0:T(8,128)(2,1)} %copy-done.5, bf16[2048,768]{1,0:T(8,128)(2,1)} %copy-done.9, ...), custom_call_target="tpu_custom_call" | custom-call | tf_op jit(solution)/shard_map/feed_forward/pallas_call | solution.py:734
  257.7 78.5 %attention_backward.1.dqkv_ref = bf16[2048,2304]{1,0:T(8,128)(2,1)} custom-call(s32[5,37]{1,0:T(8,128)} %stack.190.tab, bf16[36,13,256,256]{3,2,1,0:T(8,128)(2,1)} %get-tuple-element.130.e_ref, bf16[2048,1536]{1,0:T(8,128)(2,1)} %get-tuple-element.120.q_ref.q0_ref, bf16[2048,1536]{1,0:T(8,128)(2,1)} %get-tuple-element.131.d_ref, ...), custom_call_target="tpu_custom_call" | custom-call | flops 28991029248 | bytes 2359296 | tf_op jit(solution)/shard_map/attention_backward/pallas_call | solution.py:523
  337.4 8.1 %first_token_gradient.2 = (bf16[1024,768]{1,0:T(8,128)(2,1)S(1)}, f32[8,768]{1,0:T(8,128)S(1)}) custom-call(bf16[1024,768]{1,0:T(8,128)(2,1)S(1)} %copy-done.6, bf16[2048,2304]{1,0:T(8,128)(2,1)} %attention_backward.1.dqkv_ref, bf16[2048,768]{1,0:T(8,128)(2,1)} %get-tuple-element.134.dx_ref, f32[8,768]{1,0:T(8,128)S(1)} %copy-done.11, ...), custom_call_target="tpu_custom_call" | custom-call | flops 7247757312 | bytes 12582912 | tf_op jit(solution)/shard_map/first_token_gradient/pallas_call | solution.py:864
  345.5 13.9 %first_weight_gradient.1 = (bf16[32,24,1536]{2,1,0:T(8,128)(2,1)}, bf16[32,24,768]{2,1,0:T(8,128)(2,1)S(1)}) custom-call(bf16[1024,768]{1,0:T(8,128)(2,1)S(1)} %copy-done.3, bf16[1024,768]{1,0:T(8,128)(2,1)S(1)} %copy-done.6, bf16[2048,2304]{1,0:T(8,128)(2,1)} %attention_backward.1.dqkv_ref, f32[8,768]{1,0:T(8,128)S(1)} %copy-done.11), custom_call_target="tpu_custom_call" | custom-call | flops 14495514624 | bytes 25165824 | tf_op jit(solution)/shard_map/first_weight_gradient/pallas_call | solution.py:815
  362.1 8.2 %first_token_gradient.3 = (f32[1024,768]{1,0:T(8,128)}, f32[8,768]{1,0:T(8,128)S(1)}) custom-call(bf16[1024,768]{1,0:T(8,128)(2,1)S(1)} %copy-done.3, bf16[2048,2304]{1,0:T(8,128)(2,1)} %attention_backward.1.dqkv_ref, bf16[2048,768]{1,0:T(8,128)(2,1)} %get-tuple-element.134.dx_ref, f32[8,768]{1,0:T(8,128)S(1)} %copy-done.11, bf16[768,1536]{1,0:T(8,128)(2,1)S(1)} %bitcast.83, ...), custom_call_target="tpu_custom_call" | custom-call | flops 7247757312 | bytes 12582912 | tf_op jit(solution)/shard_map/first_token_gradient/pallas_call | solution.py:864
  379.8 6.6 %collective-permute-done.19 = bf16[8,24,768]{2,1,0:T(8,128)(2,1)S(1)} collective-permute-done((bf16[8,24,768]{2,1,0:T(8,128)(2,1)S(1)}, bf16[8,24,768]{2,1,0:T(8,128)(2,1)S(1)}, u32[]{:S(2)}, u32[]{:S(2)}) %collective-permute-start.19) | collective-permute-done | bytes 294944 | tf_op jit(solution)/shard_map/ppermute | solution.py:896
  386.5 7.4 %collective-permute-done.18 = bf16[8,24,1536]{2,1,0:T(8,128)(2,1)S(1)} collective-permute-done((bf16[8,24,1536]{2,1,0:T(8,128)(2,1)S(1)}, bf16[8,24,1536]{2,1,0:T(8,128)(2,1)S(1)}, u32[]{:S(2)}, u32[]{:S(2)}) %collective-permute-start.18) | collective-permute-done | bytes 589856 | tf_op jit(solution)/shard_map/ppermute | solution.py:896
  399.4 4.3 collective-permute-done.24
  403.7 3.3 collective-permute-done.23
  407.1 3.0 unpack_gradients.1
  417.5 3.7 collective-permute-done.27
  421.3 3.7 collective-permute-done.29
  432.1 3.6 collective-permute-done.30
  437.6 2.9 maximum_select_fusion
  (206 shorter events, 79.1 us)
Async XLA Ops:
  7.2 152.5 %all-gather.2.cloned.1.call-start = ((), (), s32[]{:S(2)}) async-start(), calls=%async_computation.1 | async-start | bytes 10948608 | tf_op jit(solution)/shard_map/all_gather | solution.py:955
  11.2 7.8 %collective-permute-start = (bf16[1,24,1536]{2,1,0:T(8,128)(2,1)}, bf16[1,24,1536]{2,1,0:T(8,128)(2,1)S(1)}, u32[]{:S(2)}, u32[]{:S(2)}) collective-permute-start(bf16[1,24,1536]{2,1,0:T(8,128)(2,1)} %bitcast.110), channel_id=1, source_target_pairs={{0,1},{1,0},{2,3},{3,2},{4,5},{5,4},{6,7},{7,6},{8,9},{9,8},{10,11... | collective-permute-start | bytes 221192 | tf_op jit(solution)/shard_map/ppermute | solution.py:896
  21.0 10.1 %collective-permute-start.4 = (bf16[256,768]{1,0:T(8,128)(2,1)S(1)}, bf16[256,768]{1,0:T(8,128)(2,1)S(1)}, u32[]{:S(2)}, u32[]{:S(2)}) collective-permute-start(bf16[256,768]{1,0:T(8,128)(2,1)S(1)} %get-tuple-element.97), channel_id=1, source_target_pairs={{0,1},{1,0},{2,3},{3,2},{4,5},{5,4},{6,7},{7,6},{8,9},{9,8},{10,11... | collective-permute-start | bytes 1179656 | tf_op jit(solution)/shard_map/ppermute | solution.py:879
  22.6 8.5 %collective-permute-start.2 = (bf16[2,24,1536]{2,1,0:T(8,128)(2,1)S(1)}, bf16[2,24,1536]{2,1,0:T(8,128)(2,1)S(1)}, u32[]{:S(2)}, u32[]{:S(2)}) collective-permute-start(bf16[2,24,1536]{2,1,0:T(8,128)(2,1)S(1)} %maximum_select_fusion.10), channel_id=1, source_target_pairs={{0,16},{2,18},{4,20},{6,22},{8,24},{10,26},{12,28},{14,30},{16,0},... | collective-permute-start | bytes 442376 | tf_op jit(solution)/shard_map/ppermute | solution.py:896
  31.1 11.6 %collective-permute-start.5 = (bf16[4,24,1536]{2,1,0:T(8,128)(2,1)S(1)}, bf16[4,24,1536]{2,1,0:T(8,128)(2,1)S(1)}, u32[]{:S(2)}, u32[]{:S(2)}) collective-permute-start(bf16[4,24,1536]{2,1,0:T(8,128)(2,1)S(1)} %bitcast.93), channel_id=1, source_target_pairs={{0,8},{2,10},{4,12},{6,14},{8,0},{10,2},{12,4},{14,6},{16,24},{18,... | collective-permute-start | bytes 884744 | tf_op jit(solution)/shard_map/ppermute | solution.py:896
  32.6 8.6 %collective-permute-start.6 = (bf16[4,24,896]{2,1,0:T(8,128)(2,1)S(1)}, bf16[4,24,896]{2,1,0:T(8,128)(2,1)S(1)}, u32[]{:S(2)}, u32[]{:S(2)}) collective-permute-start(bf16[4,24,896]{2,1,0:T(8,128)(2,1)S(1)} %bitcast.95), channel_id=1, source_target_pairs={{0,16},{2,18},{4,20},{6,22},{8,24},{10,26},{12,28},{14,30},{16,0},... | collective-permute-start | bytes 516104 | tf_op jit(solution)/shard_map/ppermute | solution.py:896
  35.3 9.7 %collective-permute-start.7 = (bf16[256,768]{1,0:T(8,128)(2,1)S(1)}, bf16[256,768]{1,0:T(8,128)(2,1)S(1)}, u32[]{:S(2)}, u32[]{:S(2)}) collective-permute-start(bf16[256,768]{1,0:T(8,128)(2,1)S(1)} %get-tuple-element.104), channel_id=1, source_target_pairs={{0,1},{1,0},{2,3},{3,2},{4,5},{5,4},{6,7},{7,6},{8,9},{9,8},{10,11... | collective-permute-start | bytes 1179656 | tf_op jit(solution)/shard_map/ppermute | solution.py:879
  45.0 362.1 %reduce-scatter.4.cloned.1.call-start = ((), (), s32[]{:S(2)}) async-start(), calls=%async_computation.2 | async-start | bytes 11151360
  45.1 15.7 %collective-permute-start.8 = (bf16[8,24,1536]{2,1,0:T(8,128)(2,1)}, bf16[8,24,1536]{2,1,0:T(8,128)(2,1)S(1)}, u32[]{:S(2)}, u32[]{:S(2)}) collective-permute-start(bf16[8,24,1536]{2,1,0:T(8,128)(2,1)} %bitcast.17), channel_id=1, source_target_pairs={{0,4},{2,6},{4,0},{6,2},{8,12},{10,14},{12,8},{14,10},{16,20},{18,... | collective-permute-start | bytes 1769480 | tf_op jit(solution)/shard_map/ppermute | solution.py:896
  45.7 7.5 %collective-permute-start.9 = (bf16[8,24,896]{2,1,0:T(8,128)(2,1)S(1)}, bf16[8,24,896]{2,1,0:T(8,128)(2,1)S(1)}, u32[]{:S(2)}, u32[]{:S(2)}) collective-permute-start(bf16[8,24,896]{2,1,0:T(8,128)(2,1)S(1)} %bitcast.91), channel_id=1, source_target_pairs={{0,8},{2,10},{4,12},{6,14},{8,0},{10,2},{12,4},{14,6},{16,24},{18,... | collective-permute-start | bytes 1032200 | tf_op jit(solution)/shard_map/ppermute | solution.py:896
  47.0 16.1 %collective-permute-start.10 = (bf16[384,768]{1,0:T(8,128)(2,1)}, bf16[384,768]{1,0:T(8,128)(2,1)}, u32[]{:S(2)}, u32[]{:S(2)}) collective-permute-start(bf16[384,768]{1,0:T(8,128)(2,1)} %dynamic-slice_bitcast_fusion.3), channel_id=1, source_target_pairs={{0,1},{1,0},{2,3},{3,2},{4,5},{5,4},{6,7},{7,6},{8,9},{9,8},{10,11... | collective-permute-start | bytes 1769480 | tf_op jit(solution)/shard_map/ppermute | solution.py:879
  63.2 9.2 %collective-permute-start.12 = (bf16[16,24,1536]{2,1,0:T(8,128)(2,1)}, bf16[16,24,1536]{2,1,0:T(8,128)(2,1)}, u32[]{:S(2)}, u32[]{:S(2)}) collective-permute-start(bf16[16,24,1536]{2,1,0:T(8,128)(2,1)} %bitcast.27), channel_id=1, source_target_pairs={{0,2},{2,0},{4,6},{6,4},{8,10},{10,8},{12,14},{14,12},{16,18},{18,... | collective-permute-start | bytes 3538952 | tf_op jit(solution)/shard_map/ppermute | solution.py:896
  77.2 82.4 %collective-permute-start.14 = (bf16[1024,768]{1,0:T(8,128)(2,1)}, bf16[1024,768]{1,0:T(8,128)(2,1)}, u32[]{:S(2)}, u32[]{:S(2)}) collective-permute-start(bf16[1024,768]{1,0:T(8,128)(2,1)} %get-tuple-element.124), channel_id=1, source_target_pairs={{0,1},{1,0},{2,3},{3,2},{4,5},{5,4},{6,7},{7,6},{8,9},{9,8},{10,11... | collective-permute-start | bytes 4718600 | tf_op jit(solution)/shard_map/ppermute | solution.py:879
  255.9 80.3 %collective-permute-start.15 = (bf16[1024,768]{1,0:T(8,128)(2,1)}, bf16[1024,768]{1,0:T(8,128)(2,1)S(1)}, u32[]{:S(2)}, u32[]{:S(2)}) collective-permute-start(bf16[1024,768]{1,0:T(8,128)(2,1)} %get-tuple-element.179), channel_id=1, source_target_pairs={{0,1},{1,0},{2,3},{3,2},{4,5},{5,4},{6,7},{7,6},{8,9},{9,8},{10,11... | collective-permute-start | bytes 4718600 | tf_op jit(solution)/shard_map/ppermute | solution.py:879
  362.0 11.2 %collective-permute-start.16 = (bf16[16,24,1536]{2,1,0:T(8,128)(2,1)}, bf16[16,24,1536]{2,1,0:T(8,128)(2,1)}, u32[]{:S(2)}, u32[]{:S(2)}) collective-permute-start(bf16[16,24,1536]{2,1,0:T(8,128)(2,1)} %constant_dynamic-slice_fusion.19), channel_id=1, source_target_pairs={{0,2},{2,0},{4,6},{6,4},{8,10},{10,8},{12,14},{14,12},{16,18},{18,... | collective-permute-start | bytes 3538952 | tf_op jit(solution)/shard_map/ppermute | solution.py:896
  374.8 11.7 %collective-permute-start.19 = (bf16[8,24,768]{2,1,0:T(8,128)(2,1)S(1)}, bf16[8,24,768]{2,1,0:T(8,128)(2,1)S(1)}, u32[]{:S(2)}, u32[]{:S(2)}) collective-permute-start(bf16[8,24,768]{2,1,0:T(8,128)(2,1)S(1)} %constant_dynamic-slice_fusion.16), channel_id=1, source_target_pairs={{0,8},{2,10},{4,12},{6,14},{8,0},{10,2},{12,4},{14,6},{16,24},{18,... | collective-permute-start | bytes 884744 | tf_op jit(solution)/shard_map/ppermute | solution.py:896
  376.2 17.7 %collective-permute-start.18 = (bf16[8,24,1536]{2,1,0:T(8,128)(2,1)S(1)}, bf16[8,24,1536]{2,1,0:T(8,128)(2,1)S(1)}, u32[]{:S(2)}, u32[]{:S(2)}) collective-permute-start(bf16[8,24,1536]{2,1,0:T(8,128)(2,1)S(1)} %constant_dynamic-slice_fusion.17), channel_id=1, source_target_pairs={{0,4},{2,6},{4,0},{6,2},{8,12},{10,14},{12,8},{14,10},{16,20},{18,... | collective-permute-start | bytes 1769480 | tf_op jit(solution)/shard_map/ppermute | solution.py:896
  379.2 14.8 %collective-permute-start.20 = (bf16[256,768]{1,0:T(8,128)(2,1)S(1)}, bf16[256,768]{1,0:T(8,128)(2,1)S(1)}, u32[]{:S(2)}, u32[]{:S(2)}) collective-permute-start(bf16[256,768]{1,0:T(8,128)(2,1)S(1)} %get-tuple-element.142), channel_id=1, source_target_pairs={{0,1},{1,0},{2,3},{3,2},{4,5},{5,4},{6,7},{7,6},{8,9},{9,8},{10,11... | collective-permute-start | bytes 1179656 | tf_op jit(solution)/shard_map/ppermute | solution.py:879
  394.8 8.9 %collective-permute-start.24 = (bf16[4,24,768]{2,1,0:T(8,128)(2,1)S(1)}, bf16[4,24,768]{2,1,0:T(8,128)(2,1)S(1)}, u32[]{:S(2)}, u32[]{:S(2)}) collective-permute-start(bf16[4,24,768]{2,1,0:T(8,128)(2,1)S(1)} %constant_dynamic-slice_fusion.10), channel_id=1, source_target_pairs={{0,16},{2,18},{4,20},{6,22},{8,24},{10,26},{12,28},{14,30},{16,0},... | collective-permute-start | bytes 442376 | tf_op jit(solution)/shard_map/ppermute | solution.py:896
  397.3 9.7 %collective-permute-start.23 = (bf16[4,24,1536]{2,1,0:T(8,128)(2,1)S(1)}, bf16[4,24,1536]{2,1,0:T(8,128)(2,1)S(1)}, u32[]{:S(2)}, u32[]{:S(2)}) collective-permute-start(bf16[4,24,1536]{2,1,0:T(8,128)(2,1)S(1)} %constant_dynamic-slice_fusion.11), channel_id=1, source_target_pairs={{0,8},{2,10},{4,12},{6,14},{8,0},{10,2},{12,4},{14,6},{16,24},{18,... | collective-permute-start | bytes 884744 | tf_op jit(solution)/shard_map/ppermute | solution.py:896
  398.7 12.7 %collective-permute-start.25 = (bf16[256,768]{1,0:T(8,128)(2,1)}, bf16[256,768]{1,0:T(8,128)(2,1)S(1)}, u32[]{:S(2)}, u32[]{:S(2)}) collective-permute-start(bf16[256,768]{1,0:T(8,128)(2,1)} %get-tuple-element.154), channel_id=1, source_target_pairs={{0,1},{1,0},{2,3},{3,2},{4,5},{5,4},{6,7},{7,6},{8,9},{9,8},{10,11... | collective-permute-start | bytes 1179656 | tf_op jit(solution)/shard_map/ppermute | solution.py:879
  413.5 7.8 %collective-permute-start.27 = (bf16[2,24,1536]{2,1,0:T(8,128)(2,1)S(1)}, bf16[2,24,1536]{2,1,0:T(8,128)(2,1)S(1)}, u32[]{:S(2)}, u32[]{:S(2)}) collective-permute-start(bf16[2,24,1536]{2,1,0:T(8,128)(2,1)S(1)} %constant_dynamic-slice_fusion.7), channel_id=1, source_target_pairs={{0,16},{2,18},{4,20},{6,22},{8,24},{10,26},{12,28},{14,30},{16,0},... | collective-permute-start | bytes 442376 | tf_op jit(solution)/shard_map/ppermute | solution.py:896
  415.8 9.1 %collective-permute-start.29 = (bf16[256,768]{1,0:T(8,128)(2,1)S(1)}, bf16[256,768]{1,0:T(8,128)(2,1)S(1)}, u32[]{:S(2)}, u32[]{:S(2)}) collective-permute-start(bf16[256,768]{1,0:T(8,128)(2,1)S(1)} %get-tuple-element.163), channel_id=1, source_target_pairs={{0,1},{1,0},{2,3},{3,2},{4,5},{5,4},{6,7},{7,6},{8,9},{9,8},{10,11... | collective-permute-start | bytes 1179656 | tf_op jit(solution)/shard_map/ppermute | solution.py:879
  427.2 8.5 %collective-permute-start.30 = (bf16[256,768]{1,0:T(8,128)(2,1)S(1)}, bf16[256,768]{1,0:T(8,128)(2,1)S(1)}, u32[]{:S(2)}, u32[]{:S(2)}) collective-permute-start(bf16[256,768]{1,0:T(8,128)(2,1)S(1)} %get-tuple-element.168), channel_id=1, source_target_pairs={{0,1},{1,0},{2,3},{3,2},{4,5},{5,4},{6,7},{7,6},{8,9},{9,8},{10,11... | collective-permute-start | bytes 1179656 | tf_op jit(solution)/shard_map/ppermute | solution.py:879
  (50 other events, 539.1 us)
Sparse Core Ops, SparseCore 0:
  45.1 101.9 all-gather.1
  252.3 145.1 reduce-scatter.3

commit v5 on v4

--- a/solution.py
+++ b/solution.py
@@ -831,7 +831,7 @@
     )(x, x_other, dqkv, gains)
 
 
-def tokens_kernel(x_ref, dqkv_ref, dx_ref, gain_ref, w_ref, v_w_ref, out_ref, gsum_ref):
+def tokens_kernel(x_ref, dqkv_ref, dx_ref, gain_ref, w_ref, v_w_ref, first_ref, out_ref, gsum_ref):
     features = x_ref.shape[1]
 
     @pl.when(pl.program_id(0) == 0)
@@ -850,7 +850,7 @@
     out_ref[...] = dx.astype(out_ref.dtype)
 
 
-def first_token_gradient(x, dqkv, dx, gains, w_qk, w_v, half, dtype):
+def first_token_gradient(x, dqkv, dx, gains, w_qk, w_v, first, half, dtype):
     tokens, features = x.shape
     steps = tokens // BT
 
@@ -864,7 +864,7 @@
     return pl.pallas_call(
         tokens_kernel,
         grid=(steps,),
-        in_specs=[own, tall(3 * features), tall(features), whole(gains), whole(w_qk), whole(w_v)],
+        in_specs=[own, tall(3 * features), tall(features), whole(gains), whole(w_qk), whole(w_v), pl.BlockSpec(memory_space=pl.ANY)],
         out_specs=[own, pl.BlockSpec((8, features), lambda t: (0, 0))],
         out_shape=[jax.ShapeDtypeStruct((tokens, features), dtype), jax.ShapeDtypeStruct((8, features), F32)],
         compiler_params=pltpu.CompilerParams(vmem_limit_bytes=48 * MIB),
@@ -872,7 +872,7 @@
             flops=12 * tokens * features * features, bytes_accessed=16 * tokens * features, transcendentals=0
         ),
         name="first_token_gradient",
-    )(x, dqkv, dx, gains, w_qk, w_v)
+    )(x, dqkv, dx, gains, w_qk, w_v, first)
 
 
 def swap(value):
@@ -971,11 +971,7 @@
     paths = ((1, 2, *far, 0), (1, *far, 2, 0))
     orders = [weight_order(bits, path) for path in paths]
     summed = list(first_weight_gradient(x, x_other, dqkv, gains, orders))
-    d_other, sum_other = first_token_gradient(x_other, after(dqkv, *summed), dx, gains, w_qk, w_v, 1, BF)
-    d_own, sum_own = first_token_gradient(x, after(dqkv, d_other), dx, gains, w_qk, w_v, 0, F32)
-    sums = jnp.sum(sum_other + sum_own, axis=0)
-    g_gain = jnp.transpose(sums.reshape(*[2] * bits, -1), [bits - 1 - dim for dim in paths[0]] + [bits])
-    g_gain = g_gain.reshape(devices, 1, -1)
+    d_other, sum_other = first_token_gradient(x_other, dqkv, dx, gains, w_qk, w_v, summed[0], 1, BF)
     parts = cut(d_other, [0] * (bits - 5) + [1, 1, 1, 1])
     d_parts = []
     for stage in range(bits):
@@ -992,7 +988,14 @@
         if stage and parts:
             d_parts = d_parts + [swap(parts[0])]
             parts = parts[1:]
-        g_gain = halved(g_gain, paths[0][stage])
+        if stage:
+            g_gain = halved(g_gain, paths[0][stage - 1])
+        else:
+            d_own, sum_own = first_token_gradient(x, dqkv, dx, gains, w_qk, w_v, summed[0], 0, F32)
+            sums = jnp.sum(sum_other + sum_own, axis=0)
+            g_gain = jnp.transpose(sums.reshape(*[2] * bits, -1), [bits - 1 - dim for dim in paths[0]] + [bits])
+            g_gain = g_gain.reshape(devices, 1, -1)
+    g_gain = halved(g_gain, paths[0][-1])
     output = in_order(output[:half], output_other, position)
     d_tokens = in_order(d_own, jnp.concatenate(d_parts).astype(F32), position)
     g_out, g_up, g_down = unpack(r_later)

time: 449 us -> 450 us (level)
  no operation moved by 1% of the time
where the time goes in v5:
time: 450 us; the launch traced here: 449 us
  Pallas kernels  282 us (63%)
  waiting for transfers between devices  70.3 us (16%)
  starting transfers between devices  37.3 us (8%)
  other arithmetic  22.2 us (5%)
  local copies, waits for them, and re-layouts  21.7 us (5%)
  between operations  15.4 us (3%)
    pallas_call x1, Pallas kernels, feed_forward(): pl.pallas_call(mlp_kernel, grid=(chunks, steps), in_specs=[pl.BlockSpec(b...  92.4 us
    pallas_call x1, Pallas kernels, attention_backward(): pl.pallas_call(backward_kernel, grid_spec=pltpu.PrefetchScalarGridSpec(nu...  78.5 us
    pallas_call x1, Pallas kernels, attention_forward(): pl.pallas_call(forward_kernel, grid_spec=pltpu.PrefetchScalarGridSpec(num...  57.7 us
    ppermute x25, waiting for transfers between devices, exchange(): lax.ppermute(value, axis, [(i, i ^ step) for i in range(lax.axis_size(axi...  55.8 us
    ppermute x25, starting transfers between devices, exchange(): lax.ppermute(value, axis, [(i, i ^ step) for i in range(lax.axis_size(axi...  28.5 us
    pallas_call x2, Pallas kernels, first_token_gradient(): pl.pallas_call(tokens_kernel, grid=(steps,), in_specs=[own, tall(3 * feat...  17.1 us
    pallas_call x1, Pallas kernels, project_qkv(): pl.pallas_call(qkv_kernel, grid=(steps,), in_specs=[*halves(features, ste...  16.5 us
    ppermute x10, waiting for transfers between devices, swap(): return lax.ppermute(value, 'seq', [(0, 1), (1, 0)])  14.5 us
  transfers between devices with their start and end apart: 37, of which 18 were waited for; matrix products, arithmetic and copies ran while one was open for 8% of the time, Pallas kernels for 42%

profile of v5, /device:TPU:0, one launch (start us, length us, event | category | flops | bytes accessed | tf_op | source)
XLA Modules:
  0.0 448.6 jit_solution(4484672065594861519)
XLA Ops:
  11.2 3.0 collective-permute-start
  25.2 5.9 %collective-permute-done.2 = bf16[2,24,1536]{2,1,0:T(8,128)(2,1)S(1)} collective-permute-done((bf16[2,24,1536]{2,1,0:T(8,128)(2,1)S(1)}, bf16[2,24,1536]{2,1,0:T(8,128)(2,1)S(1)}, u32[]{:S(2)}, u32[]{:S(2)}) %collective-permute-start.2) | collective-permute-done | bytes 147488 | tf_op jit(solution)/shard_map/ppermute | solution.py:896
  36.8 4.5 %collective-permute-done.6 = bf16[4,24,896]{2,1,0:T(8,128)(2,1)S(1)} collective-permute-done((bf16[4,24,896]{2,1,0:T(8,128)(2,1)S(1)}, bf16[4,24,896]{2,1,0:T(8,128)(2,1)S(1)}, u32[]{:S(2)}, u32[]{:S(2)}) %collective-permute-start.6) | collective-permute-done | bytes 172064 | tf_op jit(solution)/shard_map/ppermute | solution.py:896
  47.6 5.6 %collective-permute-done.9 = bf16[8,24,896]{2,1,0:T(8,128)(2,1)S(1)} collective-permute-done((bf16[8,24,896]{2,1,0:T(8,128)(2,1)S(1)}, bf16[8,24,896]{2,1,0:T(8,128)(2,1)S(1)}, u32[]{:S(2)}, u32[]{:S(2)}) %collective-permute-start.9) | collective-permute-done | bytes 344096 | tf_op jit(solution)/shard_map/ppermute | solution.py:896
  54.1 6.6 %collective-permute-done.8 = bf16[8,24,1536]{2,1,0:T(8,128)(2,1)S(1)} collective-permute-done((bf16[8,24,1536]{2,1,0:T(8,128)(2,1)}, bf16[8,24,1536]{2,1,0:T(8,128)(2,1)S(1)}, u32[]{:S(2)}, u32[]{:S(2)}) %collective-permute-start.8) | collective-permute-done | bytes 589856 | tf_op jit(solution)/shard_map/ppermute | solution.py:896
  66.3 6.1 %collective-permute-done.11 = bf16[128,768]{1,0:T(8,128)(2,1)S(1)} collective-permute-done((bf16[128,768]{1,0:T(8,128)(2,1)S(1)}, bf16[128,768]{1,0:T(8,128)(2,1)S(1)}, u32[]{:S(2)}, u32[]{:S(2)}) %collective-permute-start.11) | collective-permute-done | bytes 196640 | tf_op jit(solution)/shard_map/ppermute | solution.py:879
  72.5 4.7 %maximum_select_fusion.2 = bf16[8,2,2,24,1536]{4,3,2,1,0:T(8,128)(2,1)} fusion(bf16[8,1,2,24,1536]{4,3,2,1,0:T(8,128)(2,1)} %bitcast.40, bf16[8,1,2,24,1536]{4,3,2,1,0:T(8,128)(2,1)} %bitcast.38, pred[]{:T(512)S(6)} %eq.34), kind=kLoop, calls=%fused_computation.2 | loop fusion | flops 3538944 | bytes 4718593 | tf_op jit(solution)/shard_map/jit(_where)/select_n | solution.py:908
  81.9 16.5 %project_qkv.1 = (bf16[2048,1536]{1,0:T(8,128)(2,1)}, bf16[2048,1536]{1,0:T(8,128)(2,1)}, bf16[2048,1536]{1,0:T(8,128)(2,1)}, f32[8,768]{1,0:T(8,128)S(1)}, f32[8,128]{1,0:T(8,128)S(1)}) custom-call(bf16[1024,768]{1,0:T(8,128)(2,1)S(1)} %dynamic-slice_bitcast_fusion.2.x_ref, bf16[1024,768]{1,0:T(8,128)(2,1)S(1)} %constant_dynamic-update-slice_fusion.other_ref.x2_ref.x_ref, ...), custom_call_target="tpu_custom_call" | custom-call | tf_op jit(solution)/shard_map/project_qkv/pallas_call | solution.py:176
  100.3 57.7 %attention_forward.1 = (bf16[2048,768]{1,0:T(8,128)(2,1)S(1)}, f32[2048,768]{1,0:T(8,128)}, bf16[36,13,256,256]{3,2,1,0:T(8,128)(2,1)}) custom-call(s32[5,37]{1,0:T(8,128)S(1)} %stack.179.tab, s32[1]{0:T(128)} %bitcast.47.slow, bf16[2048,1536]{1,0:T(8,128)(2,1)} %get-tuple-element.120.q_ref.q0_ref, bf16[2048,1536]{1,0:T(8,128)(2,1)} %get-tuple-element.120.q_ref.q0_ref, ...), custom_call_target="tpu_custom_call" | custom-call | tf_op jit(solution)/shard_map/attention_forward/pallas_call | solution.py:372
  159.6 92.4 %feed_forward.1 = (bf16[2048,768]{1,0:T(8,128)(2,1)}, bf16[2048,768]{1,0:T(8,128)(2,1)}, bf16[2048,1536]{1,0:T(8,128)(2,1)}, bf16[768,7040]{1,0:T(8,128)(2,1)}) custom-call(bf16[1024,768]{1,0:T(8,128)(2,1)} %copy-done.2, bf16[1024,768]{1,0:T(8,128)(2,1)} %copy-done.4, bf16[2048,768]{1,0:T(8,128)(2,1)} %copy-done.8, ...), custom_call_target="tpu_custom_call" | custom-call | tf_op jit(solution)/shard_map/feed_forward/pallas_call | solution.py:734
  257.4 78.5 %attention_backward.1.dqkv_ref = bf16[2048,2304]{1,0:T(8,128)(2,1)} custom-call(s32[5,37]{1,0:T(8,128)} %stack.190.tab, bf16[36,13,256,256]{3,2,1,0:T(8,128)(2,1)} %get-tuple-element.130.e_ref, bf16[2048,1536]{1,0:T(8,128)(2,1)} %get-tuple-element.120.q_ref.q0_ref, bf16[2048,1536]{1,0:T(8,128)(2,1)} %get-tuple-element.131.d_ref, ...), custom_call_target="tpu_custom_call" | custom-call | flops 28991029248 | bytes 2359296 | tf_op jit(solution)/shard_map/attention_backward/pallas_call | solution.py:523
  336.0 14.0 %first_weight_gradient.1 = (bf16[32,24,1536]{2,1,0:T(8,128)(2,1)}, bf16[32,24,768]{2,1,0:T(8,128)(2,1)S(1)}) custom-call(bf16[1024,768]{1,0:T(8,128)(2,1)S(1)} %copy-done.3, bf16[1024,768]{1,0:T(8,128)(2,1)S(1)} %copy-done.5, bf16[2048,2304]{1,0:T(8,128)(2,1)} %attention_backward.1.dqkv_ref, f32[8,768]{1,0:T(8,128)S(1)} %copy-done.10), custom_call_target="tpu_custom_call" | custom-call | flops 14495514624 | bytes 25165824 | tf_op jit(solution)/shard_map/first_weight_gradient/pallas_call | solution.py:815
  352.2 8.0 %first_token_gradient.3 = (bf16[1024,768]{1,0:T(8,128)(2,1)S(1)}, f32[8,768]{1,0:T(8,128)S(1)}) custom-call(bf16[1024,768]{1,0:T(8,128)(2,1)S(1)} %copy-done.5, bf16[2048,2304]{1,0:T(8,128)(2,1)} %attention_backward.1.dqkv_ref, bf16[2048,768]{1,0:T(8,128)(2,1)} %get-tuple-element.134.dx_ref, f32[8,768]{1,0:T(8,128)S(1)} %copy-done.10, ...), custom_call_target="tpu_custom_call" | custom-call | flops 7247757312 | bytes 12582912 | tf_op jit(solution)/shard_map/first_token_gradient/pallas_call | solution.py:864
  362.5 9.1 %first_token_gradient.2 = (f32[1024,768]{1,0:T(8,128)}, f32[8,768]{1,0:T(8,128)S(1)}) custom-call(bf16[1024,768]{1,0:T(8,128)(2,1)S(1)} %copy-done.3, bf16[2048,2304]{1,0:T(8,128)(2,1)} %attention_backward.1.dqkv_ref, bf16[2048,768]{1,0:T(8,128)(2,1)} %get-tuple-element.134.dx_ref, f32[8,768]{1,0:T(8,128)S(1)} %copy-done.10, bf16[768,1536]{1,0:T(8,128)(2,1)} %bitcast.86, ...), custom_call_target="tpu_custom_call" | custom-call | flops 7247757312 | bytes 12582912 | tf_op jit(solution)/shard_map/first_token_gradient/pallas_call | solution.py:864
  374.4 3.7 maximum_select_fusion.1
  378.1 3.3 collective-permute-done.19
  381.5 9.8 %collective-permute-done.18 = bf16[8,24,1536]{2,1,0:T(8,128)(2,1)S(1)} collective-permute-done((bf16[8,24,1536]{2,1,0:T(8,128)(2,1)S(1)}, bf16[8,24,1536]{2,1,0:T(8,128)(2,1)S(1)}, u32[]{:S(2)}, u32[]{:S(2)}) %collective-permute-start.18) | collective-permute-done | bytes 589856 | tf_op jit(solution)/shard_map/ppermute | solution.py:896
  396.8 6.6 %collective-permute-done.23 = bf16[4,24,768]{2,1,0:T(8,128)(2,1)S(1)} collective-permute-done((bf16[4,24,768]{2,1,0:T(8,128)(2,1)S(1)}, bf16[4,24,768]{2,1,0:T(8,128)(2,1)S(1)}, u32[]{:S(2)}, u32[]{:S(2)}) %collective-permute-start.23) | collective-permute-done | bytes 147488 | tf_op jit(solution)/shard_map/ppermute | solution.py:896
  403.4 3.1 collective-permute-done.22
  406.6 3.0 unpack_gradients.1
  415.8 4.8 %collective-permute-done.26 = bf16[2,24,1536]{2,1,0:T(8,128)(2,1)S(1)} collective-permute-done((bf16[2,24,1536]{2,1,0:T(8,128)(2,1)S(1)}, bf16[2,24,1536]{2,1,0:T(8,128)(2,1)S(1)}, u32[]{:S(2)}, u32[]{:S(2)}) %collective-permute-start.26) | collective-permute-done | bytes 147488 | tf_op jit(solution)/shard_map/ppermute | solution.py:896
  420.6 3.0 collective-permute-done.28
  433.0 4.0 collective-permute-done.29
  438.9 2.9 maximum_select_fusion
  (202 shorter events, 76.5 us)
Async XLA Ops:
  7.2 152.5 %all-gather.2.cloned.1.call-start = ((), (), s32[]{:S(2)}) async-start(), calls=%async_computation.1 | async-start | bytes 10948608 | tf_op jit(solution)/shard_map/all_gather | solution.py:955
  21.1 10.1 %collective-permute-start.4 = (bf16[256,768]{1,0:T(8,128)(2,1)S(1)}, bf16[256,768]{1,0:T(8,128)(2,1)S(1)}, u32[]{:S(2)}, u32[]{:S(2)}) collective-permute-start(bf16[256,768]{1,0:T(8,128)(2,1)S(1)} %get-tuple-element.97), channel_id=1, source_target_pairs={{0,1},{1,0},{2,3},{3,2},{4,5},{5,4},{6,7},{7,6},{8,9},{9,8},{10,11... | collective-permute-start | bytes 1179656 | tf_op jit(solution)/shard_map/ppermute | solution.py:879
  22.6 8.5 %collective-permute-start.2 = (bf16[2,24,1536]{2,1,0:T(8,128)(2,1)S(1)}, bf16[2,24,1536]{2,1,0:T(8,128)(2,1)S(1)}, u32[]{:S(2)}, u32[]{:S(2)}) collective-permute-start(bf16[2,24,1536]{2,1,0:T(8,128)(2,1)S(1)} %maximum_select_fusion.10), channel_id=1, source_target_pairs={{0,16},{2,18},{4,20},{6,22},{8,24},{10,26},{12,28},{14,30},{16,0},... | collective-permute-start | bytes 442376 | tf_op jit(solution)/shard_map/ppermute | solution.py:896
  31.2 11.6 %collective-permute-start.5 = (bf16[4,24,1536]{2,1,0:T(8,128)(2,1)S(1)}, bf16[4,24,1536]{2,1,0:T(8,128)(2,1)S(1)}, u32[]{:S(2)}, u32[]{:S(2)}) collective-permute-start(bf16[4,24,1536]{2,1,0:T(8,128)(2,1)S(1)} %bitcast.92), channel_id=1, source_target_pairs={{0,8},{2,10},{4,12},{6,14},{8,0},{10,2},{12,4},{14,6},{16,24},{18,... | collective-permute-start | bytes 884744 | tf_op jit(solution)/shard_map/ppermute | solution.py:896
  32.7 8.6 %collective-permute-start.6 = (bf16[4,24,896]{2,1,0:T(8,128)(2,1)S(1)}, bf16[4,24,896]{2,1,0:T(8,128)(2,1)S(1)}, u32[]{:S(2)}, u32[]{:S(2)}) collective-permute-start(bf16[4,24,896]{2,1,0:T(8,128)(2,1)S(1)} %bitcast.94), channel_id=1, source_target_pairs={{0,16},{2,18},{4,20},{6,22},{8,24},{10,26},{12,28},{14,30},{16,0},... | collective-permute-start | bytes 516104 | tf_op jit(solution)/shard_map/ppermute | solution.py:896
  35.3 9.7 %collective-permute-start.7 = (bf16[256,768]{1,0:T(8,128)(2,1)S(1)}, bf16[256,768]{1,0:T(8,128)(2,1)S(1)}, u32[]{:S(2)}, u32[]{:S(2)}) collective-permute-start(bf16[256,768]{1,0:T(8,128)(2,1)S(1)} %get-tuple-element.104), channel_id=1, source_target_pairs={{0,1},{1,0},{2,3},{3,2},{4,5},{5,4},{6,7},{7,6},{8,9},{9,8},{10,11... | collective-permute-start | bytes 1179656 | tf_op jit(solution)/shard_map/ppermute | solution.py:879
  45.0 361.5 %reduce-scatter.4.cloned.1.call-start = ((), (), s32[]{:S(2)}) async-start(), calls=%async_computation.2 | async-start | bytes 11151360
  45.1 15.7 %collective-permute-start.8 = (bf16[8,24,1536]{2,1,0:T(8,128)(2,1)}, bf16[8,24,1536]{2,1,0:T(8,128)(2,1)S(1)}, u32[]{:S(2)}, u32[]{:S(2)}) collective-permute-start(bf16[8,24,1536]{2,1,0:T(8,128)(2,1)} %bitcast.17), channel_id=1, source_target_pairs={{0,4},{2,6},{4,0},{6,2},{8,12},{10,14},{12,8},{14,10},{16,20},{18,... | collective-permute-start | bytes 1769480 | tf_op jit(solution)/shard_map/ppermute | solution.py:896
  47.1 16.1 %collective-permute-start.10 = (bf16[384,768]{1,0:T(8,128)(2,1)}, bf16[384,768]{1,0:T(8,128)(2,1)}, u32[]{:S(2)}, u32[]{:S(2)}) collective-permute-start(bf16[384,768]{1,0:T(8,128)(2,1)} %dynamic-slice_bitcast_fusion.3), channel_id=1, source_target_pairs={{0,1},{1,0},{2,3},{3,2},{4,5},{5,4},{6,7},{7,6},{8,9},{9,8},{10,11... | collective-permute-start | bytes 1769480 | tf_op jit(solution)/shard_map/ppermute | solution.py:879
  63.2 9.2 %collective-permute-start.12 = (bf16[16,24,1536]{2,1,0:T(8,128)(2,1)}, bf16[16,24,1536]{2,1,0:T(8,128)(2,1)}, u32[]{:S(2)}, u32[]{:S(2)}) collective-permute-start(bf16[16,24,1536]{2,1,0:T(8,128)(2,1)} %bitcast.27), channel_id=1, source_target_pairs={{0,2},{2,0},{4,6},{6,4},{8,10},{10,8},{12,14},{14,12},{16,18},{18,... | collective-permute-start | bytes 3538952 | tf_op jit(solution)/shard_map/ppermute | solution.py:896
  77.2 82.4 %collective-permute-start.14 = (bf16[1024,768]{1,0:T(8,128)(2,1)}, bf16[1024,768]{1,0:T(8,128)(2,1)}, u32[]{:S(2)}, u32[]{:S(2)}) collective-permute-start(bf16[1024,768]{1,0:T(8,128)(2,1)} %get-tuple-element.124), channel_id=1, source_target_pairs={{0,1},{1,0},{2,3},{3,2},{4,5},{5,4},{6,7},{7,6},{8,9},{9,8},{10,11... | collective-permute-start | bytes 4718600 | tf_op jit(solution)/shard_map/ppermute | solution.py:879
  255.5 80.4 %collective-permute-start.15 = (bf16[1024,768]{1,0:T(8,128)(2,1)S(1)}, bf16[1024,768]{1,0:T(8,128)(2,1)}, u32[]{:S(2)}, u32[]{:S(2)}) collective-permute-start(bf16[1024,768]{1,0:T(8,128)(2,1)S(1)} %get-tuple-element.179), channel_id=1, source_target_pairs={{0,1},{1,0},{2,3},{3,2},{4,5},{5,4},{6,7},{7,6},{8,9},{9,8},{10,11... | collective-permute-start | bytes 4718600 | tf_op jit(solution)/shard_map/ppermute | solution.py:879
  351.5 10.0 %collective-permute-start.16 = (bf16[16,24,1536]{2,1,0:T(8,128)(2,1)S(1)}, bf16[16,24,1536]{2,1,0:T(8,128)(2,1)S(1)}, u32[]{:S(2)}, u32[]{:S(2)}) collective-permute-start(bf16[16,24,1536]{2,1,0:T(8,128)(2,1)S(1)} %constant_dynamic-slice_fusion.19), channel_id=1, source_target_pairs={{0,2},{2,0},{4,6},{6,4},{8,10},{10,8},{12,14},{14,12},{16,18},{18,... | collective-permute-start | bytes 3538952 | tf_op jit(solution)/shard_map/ppermute | solution.py:896
  351.6 9.8 %collective-permute-start.17 = (bf16[16,24,768]{2,1,0:T(8,128)(2,1)S(1)}, bf16[16,24,768]{2,1,0:T(8,128)(2,1)S(1)}, u32[]{:S(2)}, u32[]{:S(2)}) collective-permute-start(bf16[16,24,768]{2,1,0:T(8,128)(2,1)S(1)} %constant_dynamic-slice_fusion.18), channel_id=1, source_target_pairs={{0,2},{2,0},{4,6},{6,4},{8,10},{10,8},{12,14},{14,12},{16,18},{18,... | collective-permute-start | bytes 1769480 | tf_op jit(solution)/shard_map/ppermute | solution.py:896
  371.9 9.5 %collective-permute-start.19 = (bf16[8,24,768]{2,1,0:T(8,128)(2,1)S(1)}, bf16[8,24,768]{2,1,0:T(8,128)(2,1)S(1)}, u32[]{:S(2)}, u32[]{:S(2)}) collective-permute-start(bf16[8,24,768]{2,1,0:T(8,128)(2,1)S(1)} %constant_dynamic-slice_fusion.16), channel_id=1, source_target_pairs={{0,8},{2,10},{4,12},{6,14},{8,0},{10,2},{12,4},{14,6},{16,24},{18,... | collective-permute-start | bytes 884744 | tf_op jit(solution)/shard_map/ppermute | solution.py:896
  373.4 17.9 %collective-permute-start.18 = (bf16[8,24,1536]{2,1,0:T(8,128)(2,1)S(1)}, bf16[8,24,1536]{2,1,0:T(8,128)(2,1)S(1)}, u32[]{:S(2)}, u32[]{:S(2)}) collective-permute-start(bf16[8,24,1536]{2,1,0:T(8,128)(2,1)S(1)} %constant_dynamic-slice_fusion.17), channel_id=1, source_target_pairs={{0,4},{2,6},{4,0},{6,2},{8,12},{10,14},{12,8},{14,10},{16,20},{18,... | collective-permute-start | bytes 1769480 | tf_op jit(solution)/shard_map/ppermute | solution.py:896
  378.1 13.3 %collective-permute-start.20 = (bf16[256,768]{1,0:T(8,128)(2,1)S(1)}, bf16[256,768]{1,0:T(8,128)(2,1)S(1)}, u32[]{:S(2)}, u32[]{:S(2)}) collective-permute-start(bf16[256,768]{1,0:T(8,128)(2,1)S(1)} %copy-done.17), channel_id=1, source_target_pairs={{0,1},{1,0},{2,3},{3,2},{4,5},{5,4},{6,7},{7,6},{8,9},{9,8},{10,11... | collective-permute-start | bytes 1179656 | tf_op jit(solution)/shard_map/ppermute | solution.py:879
  392.5 10.9 %collective-permute-start.23 = (bf16[4,24,768]{2,1,0:T(8,128)(2,1)S(1)}, bf16[4,24,768]{2,1,0:T(8,128)(2,1)S(1)}, u32[]{:S(2)}, u32[]{:S(2)}) collective-permute-start(bf16[4,24,768]{2,1,0:T(8,128)(2,1)S(1)} %constant_dynamic-slice_fusion.12), channel_id=1, source_target_pairs={{0,16},{2,18},{4,20},{6,22},{8,24},{10,26},{12,28},{14,30},{16,0},... | collective-permute-start | bytes 442376 | tf_op jit(solution)/shard_map/ppermute | solution.py:896
  395.2 11.3 %collective-permute-start.22 = (bf16[4,24,1536]{2,1,0:T(8,128)(2,1)S(1)}, bf16[4,24,1536]{2,1,0:T(8,128)(2,1)S(1)}, u32[]{:S(2)}, u32[]{:S(2)}) collective-permute-start(bf16[4,24,1536]{2,1,0:T(8,128)(2,1)S(1)} %constant_dynamic-slice_fusion.13), channel_id=1, source_target_pairs={{0,8},{2,10},{4,12},{6,14},{8,0},{10,2},{12,4},{14,6},{16,24},{18,... | collective-permute-start | bytes 884744 | tf_op jit(solution)/shard_map/ppermute | solution.py:896
  395.9 15.0 %collective-permute-start.24 = (bf16[256,768]{1,0:T(8,128)(2,1)}, bf16[256,768]{1,0:T(8,128)(2,1)S(1)}, u32[]{:S(2)}, u32[]{:S(2)}) collective-permute-start(bf16[256,768]{1,0:T(8,128)(2,1)} %get-tuple-element.154), channel_id=1, source_target_pairs={{0,1},{1,0},{2,3},{3,2},{4,5},{5,4},{6,7},{7,6},{8,9},{9,8},{10,11... | collective-permute-start | bytes 1179656 | tf_op jit(solution)/shard_map/ppermute | solution.py:879
  412.6 7.9 %collective-permute-start.26 = (bf16[2,24,1536]{2,1,0:T(8,128)(2,1)S(1)}, bf16[2,24,1536]{2,1,0:T(8,128)(2,1)S(1)}, u32[]{:S(2)}, u32[]{:S(2)}) collective-permute-start(bf16[2,24,1536]{2,1,0:T(8,128)(2,1)S(1)} %constant_dynamic-slice_fusion.9), channel_id=1, source_target_pairs={{0,16},{2,18},{4,20},{6,22},{8,24},{10,26},{12,28},{14,30},{16,0},... | collective-permute-start | bytes 442376 | tf_op jit(solution)/shard_map/ppermute | solution.py:896
  414.4 9.2 %collective-permute-start.28 = (bf16[256,768]{1,0:T(8,128)(2,1)S(1)}, bf16[256,768]{1,0:T(8,128)(2,1)S(1)}, u32[]{:S(2)}, u32[]{:S(2)}) collective-permute-start(bf16[256,768]{1,0:T(8,128)(2,1)S(1)} %copy-done.16), channel_id=1, source_target_pairs={{0,1},{1,0},{2,3},{3,2},{4,5},{5,4},{6,7},{7,6},{8,9},{9,8},{10,11... | collective-permute-start | bytes 1179656 | tf_op jit(solution)/shard_map/ppermute | solution.py:879
  424.4 7.9 %collective-permute-start.31 = (bf16[1,24,1536]{2,1,0:T(8,128)(2,1)S(1)}, bf16[1,24,1536]{2,1,0:T(8,128)(2,1)S(1)}, u32[]{:S(2)}, u32[]{:S(2)}) collective-permute-start(bf16[1,24,1536]{2,1,0:T(8,128)(2,1)S(1)} %constant_dynamic-slice_fusion.5), channel_id=1, source_target_pairs={{0,1},{1,0},{2,3},{3,2},{4,5},{5,4},{6,7},{7,6},{8,9},{9,8},{10,11... | collective-permute-start | bytes 221192 | tf_op jit(solution)/shard_map/ppermute | solution.py:896
  428.9 8.1 %collective-permute-start.29 = (bf16[256,768]{1,0:T(8,128)(2,1)S(1)}, bf16[256,768]{1,0:T(8,128)(2,1)S(1)}, u32[]{:S(2)}, u32[]{:S(2)}) collective-permute-start(bf16[256,768]{1,0:T(8,128)(2,1)S(1)} %copy-done.15), channel_id=1, source_target_pairs={{0,1},{1,0},{2,3},{3,2},{4,5},{5,4},{6,7},{7,6},{8,9},{9,8},{10,11... | collective-permute-start | bytes 1179656 | tf_op jit(solution)/shard_map/ppermute | solution.py:879
  (48 other events, 586.6 us)
Sparse Core Ops, SparseCore 0:
  45.2 101.9 all-gather.1
  252.3 150.1 reduce-scatter.3
